TPU v7x, 256 devices: a whole 4x4x8 slice. The times are simulated.
256 devices in a mesh: rep: 2 (over core), dp: 16 (over y_lo, z), tensor: 8 (over x, y_hi).
Axes of the slice: x: 4, y: 4 (y_hi: 2, y_lo: 2; y = y_hi * 2 + y_lo), z: 8, core: 2. Of those that a mesh axis runs over, the one named last changes fastest.
Arguments:
- hidden_in: bfloat16 [16384, 8192], P(('rep', 'dp', 'tensor')), may hold values from -24 to 24
- queries: bfloat16 [16384, 8192], P(('rep', 'dp'), 'tensor'), may hold values from -6 to 6
- keys: bfloat16 [16384, 1024], P(('rep', 'dp'), 'tensor'), may hold values from -6 to 6
- values: bfloat16 [16384, 1024], P(('rep', 'dp'), 'tensor'), may hold values from -6 to 6
- out_grad: bfloat16 [16384, 8192], P(('rep', 'dp'), 'tensor'), may hold values from -6 to 6
- w_key: bfloat16 [8192, 1024], P('dp', 'tensor'), may hold values from -0.0625 to 0.0625
- w_value: bfloat16 [8192, 1024], P('dp', 'tensor'), may hold values from -0.0625 to 0.0625
- adam_state: float32 [2, 2, 8192, 1024], P(None, None, ('rep', 'dp'), 'tensor'), may hold values from -6 to 6
Outputs:
- query_grad: bfloat16 [16384, 8192], P(('rep', 'dp'), 'tensor')
- input_grad: bfloat16 [16384, 8192], P(('rep', 'dp', 'tensor'))
- key_weight_grad: float32 [8192, 1024], P(('rep', 'dp'), 'tensor')
- value_weight_grad: float32 [8192, 1024], P(('rep', 'dp'), 'tensor')
- state_backup: float32 [2, 2, 8192, 1024], P(None, None, ('rep', 'dp'), 'tensor')
All inputs are finite; a program needn't handle non-finite values.
Results may differ from a plain program's by a relative error of at most 0.015.
Values may be sent and summed in bfloat16 or wider, within the bound.
No kernel may reach another device: no remote copies, remote signals or barrier semaphores. Data moves between devices by JAX's collectives and lax.ppermute only.
A program may use at most 128 MiB of HBM per device.

v0:
```python
import math

import jax
import jax.numpy as jnp
import numpy as np
from jax import lax
from jax.experimental import pallas as pl
from jax.experimental.pallas import tpu as pltpu
from jax.sharding import Mesh
from jax.sharding import PartitionSpec as P

HEADS = 64
KVH = 8
HD = 128
GROUP = HEADS // KVH
LEN = 512
REP, YLO, Z, TEN = 2, 2, 8, 8
PLANE = ("ylo", "tensor")
SCALE = 1.0 / math.sqrt(HD)
QB = 256
STEP_HEADS = 2
BF, F32 = jnp.bfloat16, jnp.float32

VMEM = pl.BlockSpec(memory_space=pltpu.VMEM)
SMEM = pl.BlockSpec(memory_space=pltpu.SMEM)
ANY = pl.BlockSpec(memory_space=pl.ANY)


def dot(a, b, ca, cb):
    return lax.dot_general(a, b, (((ca,), (cb,)), ((), ())), preferred_element_type=F32)


def struct(*shape, dtype=BF):
    return jax.ShapeDtypeStruct(shape, dtype)


def params(mib):
    return pltpu.CompilerParams(vmem_limit_bytes=mib * 2**20)


def cost(flops, nbytes):
    return pl.CostEstimate(flops=flops, bytes_accessed=nbytes, transcendentals=0)


def shift(block, axis, count, by):
    return lax.ppermute(block, axis, [(i, (i + by) % count) for i in range(count)])


def rope_wide():
    half = HD // 2
    angle = np.arange(LEN)[:, None] * 1000000.0 ** (-2.0 * np.arange(half) / HD)[None, :]
    cosine, sine = np.cos(angle), np.sin(angle)
    wide = np.concatenate([cosine, cosine], 1), np.concatenate([sine, -sine], 1)
    return [jnp.asarray(t.astype(np.float32)) for t in wide]


def attention_kernel(at_ref, q_ref, k_ref, v_ref, g_ref, c_ref, s_ref, _, qg_ref, own_ref, other_ref, kt, dk, dv):
    step = pl.program_id(0)

    @pl.when(step == 0)
    def _():
        kt[...] = k_ref[...].T
        dk[...] = jnp.zeros_like(dk)
        dv[...] = jnp.zeros_like(dv)

    key_at = lax.broadcasted_iota(jnp.int32, (QB, QB), 0)
    query_at = lax.broadcasted_iota(jnp.int32, (QB, QB), 1)
    allowed = key_at <= query_at
    for h in range(STEP_HEADS):
        lanes = slice(h * HD, (h + 1) * HD)
        for block in range(LEN // QB):
            rows = slice(block * QB, (block + 1) * QB)
            span = (block + 1) * QB
            q, g = q_ref[rows, lanes], g_ref[rows, lanes]
            scores = dot(k_ref[:span, :], q, 1, 1)
            scores = [scores[i * QB : (i + 1) * QB] for i in range(block + 1)]
            scores[-1] = jnp.where(allowed, scores[-1], -jnp.inf)
            scores = jnp.concatenate(scores, axis=0)
            top = jnp.max(scores, axis=0, keepdims=True)
            weights = jnp.exp2((scores - top) * (SCALE * math.log2(math.e)))
            inverse = 1.0 / jnp.sum(weights, axis=0, keepdims=True)
            probs = weights * inverse
            dprobs = dot(v_ref[:span, :], g, 1, 1)
            delta = jnp.sum(probs * dprobs, axis=0, keepdims=True)
            dscores = (probs * ((dprobs - delta) * SCALE)).astype(BF)
            dk[:span, :] += dot(dscores, q, 1, 0)
            dv[:span, :] += dot(probs.astype(BF), g, 1, 0)
            qg_ref[rows, lanes] = dot(kt[:, :span], dscores, 1, 0).T.astype(BF)

    @pl.when(step == GROUP // STEP_HEADS - 1)
    def _():
        rotated = dk[...]
        turned = pltpu.roll(rotated, HD // 2, 1)
        key_grad = (rotated * c_ref[...] + turned * s_ref[...]).astype(BF)
        value_grad = dv[...].astype(BF)

        @pl.when(at_ref[0] == 0)
        def _():
            own_ref[...] = key_grad
            other_ref[...] = value_grad

        @pl.when(at_ref[0] != 0)
        def _():
            own_ref[...] = value_grad
            other_ref[...] = key_grad


def attention_grads(where_at, queries, keys, values, out_grad, before):
    whole = pl.BlockSpec((LEN, HD), lambda h: (0, 0))
    head = pl.BlockSpec((LEN, STEP_HEADS * HD), lambda h: (0, h))
    return pl.pallas_call(
        attention_kernel,
        grid=(GROUP // STEP_HEADS,),
        in_specs=[SMEM, head, whole, whole, head, whole, whole, ANY],
        out_specs=[head, whole, whole],
        out_shape=[struct(LEN, GROUP * HD), struct(LEN, HD), struct(LEN, HD)],
        scratch_shapes=[
            pltpu.VMEM((HD, LEN), BF),
            pltpu.VMEM((LEN, HD), F32),
            pltpu.VMEM((LEN, HD), F32),
        ],
        compiler_params=params(60),
        cost_estimate=cost(12 * 10**9, 4 * 2**20),
        name="attention_grads",
    )(where_at, queries, keys, values, out_grad, *rope_wide(), before)


def deal_kernel(x_ref, out_ref):
    part = out_ref.shape[2] // (REP * YLO)
    for zz in range(Z):
        for i in range(REP * YLO):
            at = (i * Z + zz) * part
            out_ref[zz, :, i * part : (i + 1) * part] = x_ref[:, at : at + part]


def split_kernel(at_ref, own_ref, other_ref, *out_refs):
    ten = at_ref[2]
    rows = out_refs[0].shape[0] // REP
    for k, out_ref in enumerate(out_refs):
        at = pl.multiple_of(lax.bitwise_xor(ten, k) * rows, rows)
        out_ref[:rows, :] = own_ref[pl.ds(at, rows), :]
        out_ref[rows:, :] = other_ref[pl.ds(at, rows), :]


def place_kernel(at_ref, *refs):
    pieces, out_ref = refs[:TEN], refs[-1]
    ten = at_ref[2]
    for k, piece in enumerate(pieces):
        at = pl.multiple_of(lax.bitwise_xor(ten, k) * HD, HD)
        out_ref[:, pl.ds(at, HD)] = piece[...]


def select_kernel(at_ref, key_ref, value_ref, _, __, out_ref):
    @pl.when(at_ref[0] == 0)
    def _():
        out_ref[...] = key_ref[...]

    @pl.when(at_ref[0] != 0)
    def _():
        out_ref[...] = value_ref[...]


def turn_kernel(at_ref, x_ref, _, __, out_ref):
    z = at_ref[1]
    for j in range(Z // 2):
        one, two = x_ref[lax.rem(z + 2 * j, Z)], x_ref[lax.rem(z + 2 * j + 1, Z)]
        pair = jnp.concatenate([one, two])
        out_ref[:, j * pair.shape[0] : (j + 1) * pair.shape[0]] = pair.T


def side_weight(weight_ref, y, n):
    at = slice(n * 256, (n + 1) * 256)
    return jnp.concatenate([weight_ref[y * TEN + t, at, :] for t in range(TEN)], axis=1)


def term_kernel(grads_ref, weight_ref, out_ref):
    per = weight_ref.shape[1] // 256
    for y in range(YLO):
        for n in range(per):
            at = (y * per + n) * 256
            term = dot(grads_ref[...], side_weight(weight_ref, y, n), 1, 1)
            out_ref[:, at : at + 256] = term.astype(BF)


def add_kernel(grads_ref, weight_ref, given_ref, *outs):
    rows = outs[0].shape[0]
    per = weight_ref.shape[1] // 256
    for y in range(YLO):
        for n in range(per):
            at = (y * per + n) * 256
            term = dot(grads_ref[...], side_weight(weight_ref, y, n), 1, 1)
            term = (term + given_ref[:, at : at + 256].astype(F32)).astype(BF)
            for j, out_ref in enumerate(outs):
                out_ref[:, at : at + 256] = term[j * rows : (j + 1) * rows, :]


def weight_grad_kernel(h_own, h_other, *refs):
    near, (far_up, far_down, out_ref, own_ref, other_ref) = refs[: Z - 1], refs[Z - 1 :]
    rows = far_up.shape[0]
    for j in range(Z):
        at = slice(j * rows, (j + 1) * rows)
        if j == Z // 2:
            own_ref[at, :] = far_up[...]
            other_ref[at, :] = far_down[...]
        else:
            piece = near[j - (j > Z // 2)]
            own_ref[at, :] = piece[:rows, :]
            other_ref[at, :] = piece[rows:, :]
    out_rows = out_ref.shape[3]
    for pair in range(TEN // 2):
        cols = slice(pair * 2 * HD, (pair + 1) * 2 * HD)
        for r in range(REP):
            for y in range(YLO):
                at = slice((r * YLO + y) * out_rows, (r * YLO + y + 1) * out_rows)
                part = dot(h_own[at, :], own_ref[:, cols], 1, 0)
                part = (part + dot(h_other[at, :], other_ref[:, cols], 1, 0)).astype(BF)
                out_ref[y, 2 * pair, r] = part[:, :HD]
                out_ref[y, 2 * pair + 1, r] = part[:, HD:]


def sum_kernel(at_ref, x_ref, *refs):
    kept_ref, given_ref = refs[-2:]
    rep = at_ref[0]
    for core, out_ref in ((rep, kept_ref), (1 - rep, given_ref)):
        total = x_ref[0, core].astype(F32)
        for i in range(1, x_ref.shape[0]):
            total = total + x_ref[i, core].astype(F32)
        out_ref[...] = total


def join_kernel(at_ref, *refs):
    *pieces, out_ref = refs
    z = at_ref[1]
    part = pieces[0].shape[1] // YLO
    for s, piece in enumerate(pieces):
        source = lax.rem(z - s + Z, Z)
        for y in range(YLO):
            at = pl.multiple_of((y * Z + source) * part, part)
            out_ref[:, pl.ds(at, part)] = piece[:, y * part : (y + 1) * part]


def ring(both):
    rows = both.shape[0] // 2
    up, down = [both], [both]
    for _ in range(Z // 2 - 1):
        up.append(shift(up[-1], "z", Z, 1))
        down.append(shift(down[-1], "z", Z, -1))
    far_up = shift(up[-1][:rows], "z", Z, 1)
    far_down = shift(down[-1][rows:], "z", Z, -1)
    return down + up[:0:-1], far_up, far_down


def on_device(hidden_in, queries, keys, values, out_grad, w_key, w_value, adam_state):
    rep, z, ten = (lax.axis_index(name) for name in ("rep", "z", "tensor"))
    where_at = jnp.stack([rep, z, ten]).astype(jnp.int32)
    first = rep == 0
    state_backup = shift(adam_state, "rep", REP, 1)
    rows, width = hidden_in.shape
    out_rows = width // (REP * YLO * Z)
    w_rows = width // (YLO * Z)

    hidden = pl.pallas_call(
        deal_kernel,
        grid=(4,),
        in_specs=[pl.BlockSpec((rows // 4, width), lambda i: (i, 0))],
        out_specs=pl.BlockSpec((Z, rows // 4, REP * YLO * out_rows), lambda i: (0, i, 0)),
        out_shape=struct(Z, rows, REP * YLO * out_rows),
        compiler_params=params(16),
        cost_estimate=cost(0, 2 * 2**20),
        name="deal",
    )(hidden_in)
    hidden = lax.all_to_all(hidden, "z", split_axis=0, concat_axis=0, tiled=True)

    query_grad, own, other = attention_grads(where_at, queries, keys, values, out_grad, state_backup)
    other = shift(other, "rep", REP, 1)
    pieces = pl.pallas_call(
        split_kernel,
        in_specs=[SMEM, VMEM, VMEM],
        out_specs=[VMEM] * TEN,
        out_shape=[struct(REP * rows, HD)] * TEN,
        compiler_params=params(8),
        cost_estimate=cost(0, 2**19),
        name="split",
    )(where_at, own, other)
    moved = {0: pieces[0]}
    for k in (5, 4, 7, 6, 1, 3, 2):
        moved[k] = lax.ppermute(pieces[k], "tensor", [(i, i ^ k) for i in range(TEN)])
    grads = pl.pallas_call(
        place_kernel,
        in_specs=[SMEM] + [VMEM] * TEN + [ANY],
        out_specs=VMEM,
        out_shape=struct(REP * rows, TEN * HD),
        compiler_params=params(8),
        cost_estimate=cost(0, 2**19),
        name="place",
    )(where_at, *[moved[k] for k in range(TEN)], hidden)

    near, far_up, far_down = ring(grads)

    weight = pl.pallas_call(
        select_kernel,
        in_specs=[SMEM, VMEM, VMEM, ANY, ANY],
        out_specs=VMEM,
        out_shape=struct(w_rows, HD),
        compiler_params=params(8),
        cost_estimate=cost(0, 2**18),
        name="select",
    )(where_at, w_key, w_value, near[1], near[-1])
    weight = jnp.broadcast_to(weight[None], (YLO * TEN,) + weight.shape)
    weight = lax.all_to_all(weight, PLANE, split_axis=0, concat_axis=0, tiled=True)

    hidden = pl.pallas_call(
        turn_kernel,
        in_specs=[SMEM, VMEM, ANY, ANY],
        out_specs=VMEM,
        out_shape=struct(REP * YLO * out_rows, Z * rows),
        compiler_params=params(16),
        cost_estimate=cost(0, 2 * 2**20),
        name="turn",
    )(where_at, hidden, near[2], near[-2])
    hidden_other = shift(hidden, "rep", REP, 1)

    half = struct(Z * rows, TEN * HD)
    partial, grads_own, grads_other = pl.pallas_call(
        weight_grad_kernel,
        in_specs=[VMEM] * (Z + 3),
        out_specs=[VMEM] * 3,
        out_shape=[struct(YLO, TEN, REP, out_rows, HD), half, half],
        compiler_params=params(48),
        cost_estimate=cost(2 * 2**30, 8 * 2**20),
        name="weight_grad",
    )(hidden, hidden_other, *near, far_up, far_down)
    given = pl.pallas_call(
        term_kernel,
        in_specs=[VMEM] * 2,
        out_specs=VMEM,
        out_shape=struct(Z * rows, YLO * w_rows),
        compiler_params=params(24),
        cost_estimate=cost(2**30, 4 * 2**20),
        name="term",
    )(grads_other, weight)
    given = shift(given, "rep", REP, 1)
    partial = partial.reshape(YLO * TEN, REP, out_rows, HD)
    partial = lax.all_to_all(partial, PLANE, split_axis=0, concat_axis=0, tiled=True)

    pieces = pl.pallas_call(
        add_kernel,
        in_specs=[VMEM] * 3,
        out_specs=[VMEM] * Z,
        out_shape=[struct(rows, YLO * w_rows)] * Z,
        compiler_params=params(24),
        cost_estimate=cost(2**30, 5 * 2**20),
        name="add",
    )(grads_own, weight, given)
    moved = {0: pieces[0]}
    for k in (4, 3, 5, 2, 6, 1, 7):
        moved[k] = shift(pieces[k], "z", Z, k)
    moved = [moved[k] for k in range(Z)]
    input_grad = pl.pallas_call(
        join_kernel,
        in_specs=[SMEM] + [VMEM] * Z,
        out_specs=VMEM,
        out_shape=struct(rows, width),
        compiler_params=params(16),
        cost_estimate=cost(0, 2 * 2**20),
        name="join",
    )(where_at, *moved)

    kept, passed = pl.pallas_call(
        sum_kernel,
        in_specs=[SMEM, VMEM] + [ANY] * (Z - 1),
        out_specs=[VMEM] * 2,
        out_shape=[struct(out_rows, HD, dtype=F32)] * 2,
        compiler_params=params(16),
        cost_estimate=cost(0, 2 * 2**20),
        name="sum",
    )(where_at, partial, *moved[1:])
    passed = shift(passed, "rep", REP, 1)
    key_weight_grad = jnp.where(first, kept, passed)
    value_weight_grad = jnp.where(first, passed, kept)
    return (query_grad, input_grad, key_weight_grad, value_weight_grad, state_backup)


def solution(mesh):
    fine = Mesh(mesh.devices.reshape(REP, YLO, Z, TEN), ("rep", "ylo", "z", "tensor"))
    seqs = ("rep", "ylo", "z")
    return jax.shard_map(
        on_device,
        mesh=fine,
        in_specs=(
            P(seqs + ("tensor",), None),
            P(seqs, "tensor"),
            P(seqs, "tensor"),
            P(seqs, "tensor"),
            P(seqs, "tensor"),
            P(("ylo", "z"), "tensor"),
            P(("ylo", "z"), "tensor"),
            P(None, None, seqs, "tensor"),
        ),
        out_specs=(
            P(seqs, "tensor"),
            P(seqs + ("tensor",), None),
            P(seqs, "tensor"),
            P(seqs, "tensor"),
            P(None, None, seqs, "tensor"),
        ),
        check_vma=False,
    )
```

profile of v0, /device:TPU:1, one launch (start us, length us, event | category | flops | bytes accessed | tf_op | source)
XLA Modules:
  0.0 152.1 jit_solution(11651691757936630055)
XLA Ops:
  0.6 3.3 %collective-permute-start = (f32[2,2,256,128]{3,2,1,0:T(8,128)}, f32[2,2,256,128]{3,2,1,0:T(8,128)S(1)}, u32[]{:S(2)}, u32[]{:S(2)}) collective-permute-start(f32[2,2,256,128]{3,2,1,0:T(8,128)} %param.17), channel_id=1, source_target_pairs={{0,128},{128,0},{1,129},{129,1},{2,130},{130,2},{3,131},{131,3},{4... | collective-permute-start | bytes 1572872 | tf_op jit(solution)/shard_map/ppermute | solution.py:46
  4.0 1.2 copy-done
  5.2 1.5 %deal.1 = bf16[8,64,1024]{2,1,0:T(8,128)(2,1)} custom-call(bf16[64,8192]{1,0:T(8,128)(2,1)S(1)} %copy-done), custom_call_target="tpu_custom_call" | custom-call | bytes 2097152 | tf_op jit(solution)/shard_map/deal/pallas_call | solution.py:262
  6.7 6.5 %all-to-all-start = ((bf16[8,64,1024]{2,1,0:T(8,128)(2,1)}), bf16[8,64,1024]{2,1,0:T(8,128)(2,1)S(1)}, u32[]{:S(2)}, u32[]{:S(2)}) async-start(bf16[8,64,1024]{2,1,0:T(8,128)(2,1)} %deal.1), calls=%async_computation | async-start | bytes 2097152 | tf_op jit(solution)/shard_map/all_to_all | solution.py:272
  13.8 0.8 copy-done.11
  14.6 11.1 %attention_grads.1 = (bf16[512,1024]{1,0:T(8,128)(2,1)}, bf16[512,128]{1,0:T(8,128)(2,1)}, bf16[512,128]{1,0:T(8,128)(2,1)}) custom-call(s32[3]{0:T(128)} %pad_add_fusion.at_ref, bf16[512,1024]{1,0:T(8,128)(2,1)} %q_ref.1, bf16[512,128]{1,0:T(8,128)(2,1)} %k_ref.1, bf16[512,128]{1,0:T(8,128)(2,1)} %v_ref.1, bf16[512,1024]{1,0:T(8,128)(2,1)} %g_ref.1, ...), custom_call_target="tpu_custom_call" | custom-call | flops 12000000000 | bytes 4194304 | tf_op jit(solution)/shard_map/attention_grads/pallas_call | solution.py:111
  26.1 1.3 collective-permute-done.1.other_ref
  27.4 0.9 copy-done.9
  28.8 3.0 %collective-permute-start.2 = (bf16[128,128]{1,0:T(8,128)(2,1)S(1)}, bf16[128,128]{1,0:T(8,128)(2,1)S(1)}, u32[]{:S(2)}, u32[]{:S(2)}) collective-permute-start(bf16[128,128]{1,0:T(8,128)(2,1)S(1)} %get-tuple-element.33), channel_id=1, source_target_pairs={{0,1},{1,0},{2,3},{3,2},{4,5},{5,4},{6,7},{7,6},{8,9},{9,8},{10,11... | collective-permute-start | bytes 98312 | tf_op jit(solution)/shard_map/ppermute | solution.py:287
  31.8 1.2 collective-permute-start.3
  33.1 2.7 %collective-permute-start.5 = (bf16[128,128]{1,0:T(8,128)(2,1)S(1)}, bf16[128,128]{1,0:T(8,128)(2,1)S(1)}, u32[]{:S(2)}, u32[]{:S(2)}) collective-permute-start(bf16[128,128]{1,0:T(8,128)(2,1)S(1)} %get-tuple-element.36), channel_id=1, source_target_pairs={{0,4},{1,5},{2,6},{3,7},{4,0},{5,1},{6,2},{7,3},{8,12},{9,13},{10,... | collective-permute-start | bytes 98312 | tf_op jit(solution)/shard_map/ppermute | solution.py:287
  35.9 2.8 %collective-permute-start.6 = (bf16[128,128]{1,0:T(8,128)(2,1)S(1)}, bf16[128,128]{1,0:T(8,128)(2,1)S(1)}, u32[]{:S(2)}, u32[]{:S(2)}) collective-permute-start(bf16[128,128]{1,0:T(8,128)(2,1)S(1)} %get-tuple-element.37), channel_id=1, source_target_pairs={{0,5},{1,4},{2,7},{3,6},{4,1},{5,0},{6,3},{7,2},{8,13},{9,12},{10,... | collective-permute-start | bytes 98312 | tf_op jit(solution)/shard_map/ppermute | solution.py:287
  38.7 2.5 %collective-permute-start.7 = (bf16[128,128]{1,0:T(8,128)(2,1)S(1)}, bf16[128,128]{1,0:T(8,128)(2,1)S(1)}, u32[]{:S(2)}, u32[]{:S(2)}) collective-permute-start(bf16[128,128]{1,0:T(8,128)(2,1)S(1)} %get-tuple-element.38), channel_id=1, source_target_pairs={{0,6},{1,7},{2,4},{3,5},{4,2},{5,3},{6,0},{7,1},{8,14},{9,15},{10,... | collective-permute-start | bytes 98312 | tf_op jit(solution)/shard_map/ppermute | solution.py:287
  41.2 1.5 collective-permute-done.6.refs_5_
  43.3 4.2 %collective-permute-done.8.refs_7_ = bf16[128,128]{1,0:T(8,128)(2,1)S(1)} collective-permute-done((bf16[128,128]{1,0:T(8,128)(2,1)S(1)}, bf16[128,128]{1,0:T(8,128)(2,1)S(1)}, u32[]{:S(2)}, u32[]{:S(2)}) %collective-permute-start.8) | collective-permute-done | bytes 32800 | tf_op jit(solution)/shard_map/ppermute | solution.py:287
  48.2 3.0 %collective-permute-start.9 = (bf16[128,1024]{1,0:T(8,128)(2,1)S(1)}, bf16[128,1024]{1,0:T(8,128)(2,1)S(1)}, u32[]{:S(2)}, u32[]{:S(2)}) collective-permute-start(bf16[128,1024]{1,0:T(8,128)(2,1)S(1)} %place.1.refs_0_), channel_id=1, source_target_pairs={{0,56},{8,0},{16,8},{24,16},{32,24},{40,32},{48,40},{56,48},{1,57}... | collective-permute-start | bytes 786440 | tf_op jit(solution)/shard_map/ppermute | solution.py:46
  51.8 2.6 %collective-permute-done.9.refs_1_._ = bf16[128,1024]{1,0:T(8,128)(2,1)S(1)} collective-permute-done((bf16[128,1024]{1,0:T(8,128)(2,1)S(1)}, bf16[128,1024]{1,0:T(8,128)(2,1)S(1)}, u32[]{:S(2)}, u32[]{:S(2)}) %collective-permute-start.9) | collective-permute-done | bytes 262176 | tf_op jit(solution)/shard_map/ppermute | solution.py:46
  54.4 3.1 %collective-permute-done.11.refs_6_.__ = bf16[128,1024]{1,0:T(8,128)(2,1)S(1)} collective-permute-done((bf16[128,1024]{1,0:T(8,128)(2,1)S(1)}, bf16[128,1024]{1,0:T(8,128)(2,1)S(1)}, u32[]{:S(2)}, u32[]{:S(2)}) %collective-permute-start.11) | collective-permute-done | bytes 262176 | tf_op jit(solution)/shard_map/ppermute | solution.py:46
  58.1 1.7 %broadcast_in_dim.2 = bf16[16,512,128]{2,1,0:T(8,128)(2,1)} broadcast(bf16[512,128]{1,0:T(8,128)(2,1)S(1)} %select.1), dimensions={1,2} | broadcast | bytes 2228224 | tf_op jit(solution)/shard_map/broadcast_in_dim | solution.py:309
  59.9 3.7 %all-to-all-start.1 = ((bf16[16,512,128]{2,1,0:T(8,128)(2,1)}), bf16[16,512,128]{2,1,0:T(8,128)(2,1)S(1)}, u32[]{:S(2)}, u32[]{:S(2)}) async-start(bf16[16,512,128]{2,1,0:T(8,128)(2,1)} %broadcast_in_dim.2), calls=%async_computation.1 | async-start | bytes 4194304 | tf_op jit(solution)/shard_map/all_to_all | solution.py:310
  63.7 1.5 collective-permute-start.12
  65.2 3.8 %collective-permute-done.10._.refs_2_ = bf16[128,1024]{1,0:T(8,128)(2,1)S(1)} collective-permute-done((bf16[128,1024]{1,0:T(8,128)(2,1)S(1)}, bf16[128,1024]{1,0:T(8,128)(2,1)S(1)}, u32[]{:S(2)}, u32[]{:S(2)}) %collective-permute-start.10) | collective-permute-done | bytes 262176 | tf_op jit(solution)/shard_map/ppermute | solution.py:46
  68.9 1.5 collective-permute-done.12.__.refs_5_
  70.4 0.9 turn.1.h_own
  71.3 6.0 %collective-permute-start.13 = (bf16[1024,512]{1,0:T(8,128)(2,1)S(1)}, bf16[1024,512]{1,0:T(8,128)(2,1)S(1)}, u32[]{:S(2)}, u32[]{:S(2)}) collective-permute-start(bf16[1024,512]{1,0:T(8,128)(2,1)S(1)} %turn.1.h_own), channel_id=1, source_target_pairs={{0,128},{128,0},{1,129},{129,1},{2,130},{130,2},{3,131},{131,3},{4... | collective-permute-start | bytes 3145736 | tf_op jit(solution)/shard_map/ppermute | solution.py:46
  77.6 2.4 %collective-permute-start.14 = (bf16[128,1024]{1,0:T(8,128)(2,1)S(1)}, bf16[128,1024]{1,0:T(8,128)(2,1)S(1)}, u32[]{:S(2)}, u32[]{:S(2)}) collective-permute-start(bf16[128,1024]{1,0:T(8,128)(2,1)S(1)} %collective-permute-done.10._.refs_2_), channel_id=1, source_target_pairs={{0,56},{8,0},{16,8},{24,16},{32,24},{40,32},{48,40},{56,48},{1,57}... | collective-permute-start | bytes 786440 | tf_op jit(solution)/shard_map/ppermute | solution.py:46
  80.0 6.2 %collective-permute-done.15.refs_4_ = bf16[128,1024]{1,0:T(8,128)(2,1)S(1)} collective-permute-done((bf16[128,1024]{1,0:T(8,128)(2,1)S(1)}, bf16[128,1024]{1,0:T(8,128)(2,1)S(1)}, u32[]{:S(2)}, u32[]{:S(2)}) %collective-permute-start.15) | collective-permute-done | bytes 262176 | tf_op jit(solution)/shard_map/ppermute | solution.py:46
  86.3 2.7 %collective-permute-start.17 = (bf16[64,1024]{1,0:T(8,128)(2,1)S(1)}, bf16[64,1024]{1,0:T(8,128)(2,1)S(1)}, u32[]{:S(2)}, u32[]{:S(2)}) collective-permute-start(bf16[64,1024]{1,0:T(8,128)(2,1)S(1)} %slice.9), channel_id=1, source_target_pairs={{0,56},{8,0},{16,8},{24,16},{32,24},{40,32},{48,40},{56,48},{1,57}... | collective-permute-start | bytes 393224 | tf_op jit(solution)/shard_map/ppermute | solution.py:46
  89.0 2.6 %collective-permute-done.16.refs_7_ = bf16[64,1024]{1,0:T(8,128)(2,1)S(1)} collective-permute-done((bf16[64,1024]{1,0:T(8,128)(2,1)S(1)}, bf16[64,1024]{1,0:T(8,128)(2,1)S(1)}, u32[]{:S(2)}, u32[]{:S(2)}) %collective-permute-start.16) | collective-permute-done | bytes 131104 | tf_op jit(solution)/shard_map/ppermute | solution.py:46
  91.6 1.0 copy-done.13
  92.6 4.9 %weight_grad.1 = (bf16[2,8,2,256,128]{4,3,2,1,0:T(8,128)(2,1)}, bf16[512,1024]{1,0:T(8,128)(2,1)S(1)}, bf16[512,1024]{1,0:T(8,128)(2,1)S(1)}) custom-call(bf16[1024,512]{1,0:T(8,128)(2,1)S(1)} %turn.1.h_own, bf16[1024,512]{1,0:T(8,128)(2,1)} %copy-done.13, bf16[128,1024]{1,0:T(8,128)(2,1)S(1)} %copy-done.6, ...), custom_call_target="tpu_custom_call" | custom-call | flops 2147483648 | bytes 8388608 | tf_op jit(solution)/shard_map/weight_grad/pallas_call | solution.py:324
  97.5 1.0 copy-done.1
  98.4 6.7 %all-to-all-start.2 = ((bf16[16,2,256,128]{3,2,1,0:T(8,128)(2,1)}), bf16[16,2,256,128]{3,2,1,0:T(8,128)(2,1)}, u32[]{:S(2)}, u32[]{:S(2)}) async-start(bf16[16,2,256,128]{3,2,1,0:T(8,128)(2,1)} %bitcast.4), calls=%async_computation.2 | async-start | bytes 4194304 | tf_op jit(solution)/shard_map/all_to_all | solution.py:344
  105.1 1.2 copy-done.2
  106.3 1.3 term.1
  107.6 2.6 %collective-permute-start.18 = (bf16[512,1024]{1,0:T(8,128)(2,1)S(1)}, bf16[512,1024]{1,0:T(8,128)(2,1)S(1)}, u32[]{:S(2)}, u32[]{:S(2)}) collective-permute-start(bf16[512,1024]{1,0:T(8,128)(2,1)S(1)} %term.1), channel_id=1, source_target_pairs={{0,128},{128,0},{1,129},{129,1},{2,130},{130,2},{3,131},{131,3},{4... | collective-permute-start | bytes 3145736 | tf_op jit(solution)/shard_map/ppermute | solution.py:46
  110.2 2.3 %collective-permute-done.18.given_ref = bf16[512,1024]{1,0:T(8,128)(2,1)S(1)} collective-permute-done((bf16[512,1024]{1,0:T(8,128)(2,1)S(1)}, bf16[512,1024]{1,0:T(8,128)(2,1)S(1)}, u32[]{:S(2)}, u32[]{:S(2)}) %collective-permute-start.18) | collective-permute-done | bytes 1048608 | tf_op jit(solution)/shard_map/ppermute | solution.py:46
  112.5 1.3 add.5
  113.8 3.7 %collective-permute-start.20 = (bf16[64,1024]{1,0:T(8,128)(2,1)S(1)}, bf16[64,1024]{1,0:T(8,128)(2,1)S(1)}, u32[]{:S(2)}, u32[]{:S(2)}) collective-permute-start(bf16[64,1024]{1,0:T(8,128)(2,1)S(1)} %get-tuple-element.44), channel_id=1, source_target_pairs={{0,16},{8,24},{16,32},{24,40},{32,48},{40,56},{48,0},{56,8},{1,17}... | collective-permute-start | bytes 393224 | tf_op jit(solution)/shard_map/ppermute | solution.py:46
  117.6 2.7 %collective-permute-start.22 = (bf16[64,1024]{1,0:T(8,128)(2,1)S(1)}, bf16[64,1024]{1,0:T(8,128)(2,1)S(1)}, u32[]{:S(2)}, u32[]{:S(2)}) collective-permute-start(bf16[64,1024]{1,0:T(8,128)(2,1)S(1)} %get-tuple-element.46), channel_id=1, source_target_pairs={{0,32},{8,40},{16,48},{24,56},{32,0},{40,8},{48,16},{56,24},{1,33}... | collective-permute-start | bytes 393224 | tf_op jit(solution)/shard_map/ppermute | solution.py:46
  120.3 4.3 %collective-permute-start.23 = (bf16[64,1024]{1,0:T(8,128)(2,1)S(1)}, bf16[64,1024]{1,0:T(8,128)(2,1)S(1)}, u32[]{:S(2)}, u32[]{:S(2)}) collective-permute-start(bf16[64,1024]{1,0:T(8,128)(2,1)S(1)} %get-tuple-element.47), channel_id=1, source_target_pairs={{0,40},{8,48},{16,56},{24,0},{32,8},{40,16},{48,24},{56,32},{1,41}... | collective-permute-start | bytes 393224 | tf_op jit(solution)/shard_map/ppermute | solution.py:46
  125.4 3.5 %collective-permute-done.20.refs_2_.refs_1_ = bf16[64,1024]{1,0:T(8,128)(2,1)S(1)} collective-permute-done((bf16[64,1024]{1,0:T(8,128)(2,1)S(1)}, bf16[64,1024]{1,0:T(8,128)(2,1)S(1)}, u32[]{:S(2)}, u32[]{:S(2)}) %collective-permute-start.20) | collective-permute-done | bytes 131104 | tf_op jit(solution)/shard_map/ppermute | solution.py:46
  128.9 6.3 %collective-permute-done.21.refs_3_.refs_2_ = bf16[64,1024]{1,0:T(8,128)(2,1)S(1)} collective-permute-done((bf16[64,1024]{1,0:T(8,128)(2,1)S(1)}, bf16[64,1024]{1,0:T(8,128)(2,1)S(1)}, u32[]{:S(2)}, u32[]{:S(2)}) %collective-permute-start.21) | collective-permute-done | bytes 131104 | tf_op jit(solution)/shard_map/ppermute | solution.py:46
  135.5 8.4 %collective-permute-done.24.refs_6_.refs_5_ = bf16[64,1024]{1,0:T(8,128)(2,1)S(1)} collective-permute-done((bf16[64,1024]{1,0:T(8,128)(2,1)S(1)}, bf16[64,1024]{1,0:T(8,128)(2,1)S(1)}, u32[]{:S(2)}, u32[]{:S(2)}) %collective-permute-start.24) | collective-permute-done | bytes 131104 | tf_op jit(solution)/shard_map/ppermute | solution.py:46
  143.9 2.7 %collective-permute-done.25.refs_7_.refs_6_ = bf16[64,1024]{1,0:T(8,128)(2,1)S(1)} collective-permute-done((bf16[64,1024]{1,0:T(8,128)(2,1)S(1)}, bf16[64,1024]{1,0:T(8,128)(2,1)S(1)}, u32[]{:S(2)}, u32[]{:S(2)}) %collective-permute-start.25) | collective-permute-done | bytes 131104 | tf_op jit(solution)/shard_map/ppermute | solution.py:46
  146.6 1.9 %sum.1 = (f32[256,128]{1,0:T(8,128)S(1)}, f32[256,128]{1,0:T(8,128)S(1)}) custom-call(s32[3]{0:T(128)S(1)} %copy-done.10, bf16[16,2,256,128]{3,2,1,0:T(8,128)(2,1)} %all-to-all-done.2.x_ref, bf16[64,1024]{1,0:T(8,128)(2,1)S(1)} %collective-permute-done.19.refs_1_.refs_0_, bf16[64,1024]{1,0:T(8,128)(2,1)S(1)} %collective-permute-done.20.refs_2_.refs_1_, ...), custom_call_target="tpu_custom_call" | custom-call | bytes 2097152 | tf_op jit(solution)/shard_map/sum/pallas_call | solution.py:369
  149.0 1.6 %join.1 = bf16[64,8192]{1,0:T(8,128)(2,1)} custom-call(s32[3]{0:T(128)S(1)} %copy-done.10, bf16[64,1024]{1,0:T(8,128)(2,1)S(1)} %get-tuple-element.42.refs_0_, bf16[64,1024]{1,0:T(8,128)(2,1)S(1)} %collective-permute-done.19.refs_1_.refs_0_, bf16[64,1024]{1,0:T(8,128)(2,1)S(1)} %collective-permute-done.20.refs_2_.refs_1_, ...), custom_call_target="tpu_custom_call" | custom-call | bytes 2097152 | tf_op jit(solution)/shard_map/join/pallas_call | solution.py:359
  151.3 0.8 copy.16
  (57 shorter events, 7.2 us)
Async XLA Ops:
  0.6 13.2 %collective-permute-start = (f32[2,2,256,128]{3,2,1,0:T(8,128)}, f32[2,2,256,128]{3,2,1,0:T(8,128)S(1)}, u32[]{:S(2)}, u32[]{:S(2)}) collective-permute-start(f32[2,2,256,128]{3,2,1,0:T(8,128)} %param.17), channel_id=1, source_target_pairs={{0,128},{128,0},{1,129},{129,1},{2,130},{130,2},{3,131},{131,3},{4... | collective-permute-start | bytes 1572872 | tf_op jit(solution)/shard_map/ppermute | solution.py:46
  4.0 1.2 copy-start
  6.7 40.8 %all-to-all-start = ((bf16[8,64,1024]{2,1,0:T(8,128)(2,1)}), bf16[8,64,1024]{2,1,0:T(8,128)(2,1)S(1)}, u32[]{:S(2)}, u32[]{:S(2)}) async-start(bf16[8,64,1024]{2,1,0:T(8,128)(2,1)} %deal.1), calls=%async_computation | async-start | bytes 2097152 | tf_op jit(solution)/shard_map/all_to_all | solution.py:272
  13.8 13.6 %copy-start.10 = (s32[3]{0:T(128)S(1)}, s32[3]{0:T(128)}, u32[]{:S(2)}) copy-start(s32[3]{0:T(128)} %pad_add_fusion.at_ref) | copy-start | bytes 40
  13.8 43.8 %copy-start.7 = (bf16[512,128]{1,0:T(8,128)(2,1)S(1)}, bf16[512,128]{1,0:T(8,128)(2,1)}, u32[]{:S(2)}) copy-start(bf16[512,128]{1,0:T(8,128)(2,1)} %key_ref.1) | copy-start | bytes 393220
  13.8 43.8 %copy-start.8 = (bf16[512,128]{1,0:T(8,128)(2,1)S(1)}, bf16[512,128]{1,0:T(8,128)(2,1)}, u32[]{:S(2)}) copy-start(bf16[512,128]{1,0:T(8,128)(2,1)} %value_ref.1) | copy-start | bytes 393220
  13.8 0.8 copy-start.11
  25.7 1.6 %collective-permute-start.1 = (bf16[512,128]{1,0:T(8,128)(2,1)}, bf16[512,128]{1,0:T(8,128)(2,1)S(1)}, u32[]{:S(2)}, u32[]{:S(2)}) collective-permute-start(bf16[512,128]{1,0:T(8,128)(2,1)} %get-tuple-element.31), channel_id=1, source_target_pairs={{0,128},{128,0},{1,129},{129,1},{2,130},{130,2},{3,131},{131,3},{4... | collective-permute-start | bytes 393224 | tf_op jit(solution)/shard_map/ppermute | solution.py:46
  27.4 0.9 copy-start.9
  28.8 9.9 %collective-permute-start.2 = (bf16[128,128]{1,0:T(8,128)(2,1)S(1)}, bf16[128,128]{1,0:T(8,128)(2,1)S(1)}, u32[]{:S(2)}, u32[]{:S(2)}) collective-permute-start(bf16[128,128]{1,0:T(8,128)(2,1)S(1)} %get-tuple-element.33), channel_id=1, source_target_pairs={{0,1},{1,0},{2,3},{3,2},{4,5},{5,4},{6,7},{7,6},{8,9},{9,8},{10,11... | collective-permute-start | bytes 98312 | tf_op jit(solution)/shard_map/ppermute | solution.py:287
  31.8 9.3 %collective-permute-start.3 = (bf16[128,128]{1,0:T(8,128)(2,1)S(1)}, bf16[128,128]{1,0:T(8,128)(2,1)S(1)}, u32[]{:S(2)}, u32[]{:S(2)}) collective-permute-start(bf16[128,128]{1,0:T(8,128)(2,1)S(1)} %get-tuple-element.34), channel_id=1, source_target_pairs={{0,2},{1,3},{2,0},{3,1},{4,6},{5,7},{6,4},{7,5},{8,10},{9,11},{10,... | collective-permute-start | bytes 98312 | tf_op jit(solution)/shard_map/ppermute | solution.py:287
  33.1 8.1 %collective-permute-start.4 = (bf16[128,128]{1,0:T(8,128)(2,1)S(1)}, bf16[128,128]{1,0:T(8,128)(2,1)S(1)}, u32[]{:S(2)}, u32[]{:S(2)}) collective-permute-start(bf16[128,128]{1,0:T(8,128)(2,1)S(1)} %get-tuple-element.35), channel_id=1, source_target_pairs={{0,3},{1,2},{2,1},{3,0},{4,7},{5,6},{6,5},{7,4},{8,11},{9,10},{10,... | collective-permute-start | bytes 98312 | tf_op jit(solution)/shard_map/ppermute | solution.py:287
  33.1 8.1 %collective-permute-start.5 = (bf16[128,128]{1,0:T(8,128)(2,1)S(1)}, bf16[128,128]{1,0:T(8,128)(2,1)S(1)}, u32[]{:S(2)}, u32[]{:S(2)}) collective-permute-start(bf16[128,128]{1,0:T(8,128)(2,1)S(1)} %get-tuple-element.36), channel_id=1, source_target_pairs={{0,4},{1,5},{2,6},{3,7},{4,0},{5,1},{6,2},{7,3},{8,12},{9,13},{10,... | collective-permute-start | bytes 98312 | tf_op jit(solution)/shard_map/ppermute | solution.py:287
  35.9 6.8 %collective-permute-start.6 = (bf16[128,128]{1,0:T(8,128)(2,1)S(1)}, bf16[128,128]{1,0:T(8,128)(2,1)S(1)}, u32[]{:S(2)}, u32[]{:S(2)}) collective-permute-start(bf16[128,128]{1,0:T(8,128)(2,1)S(1)} %get-tuple-element.37), channel_id=1, source_target_pairs={{0,5},{1,4},{2,7},{3,6},{4,1},{5,0},{6,3},{7,2},{8,13},{9,12},{10,... | collective-permute-start | bytes 98312 | tf_op jit(solution)/shard_map/ppermute | solution.py:287
  38.7 4.6 %collective-permute-start.7 = (bf16[128,128]{1,0:T(8,128)(2,1)S(1)}, bf16[128,128]{1,0:T(8,128)(2,1)S(1)}, u32[]{:S(2)}, u32[]{:S(2)}) collective-permute-start(bf16[128,128]{1,0:T(8,128)(2,1)S(1)} %get-tuple-element.38), channel_id=1, source_target_pairs={{0,6},{1,7},{2,4},{3,5},{4,2},{5,3},{6,0},{7,1},{8,14},{9,15},{10,... | collective-permute-start | bytes 98312 | tf_op jit(solution)/shard_map/ppermute | solution.py:287
  41.2 6.4 %collective-permute-start.8 = (bf16[128,128]{1,0:T(8,128)(2,1)S(1)}, bf16[128,128]{1,0:T(8,128)(2,1)S(1)}, u32[]{:S(2)}, u32[]{:S(2)}) collective-permute-start(bf16[128,128]{1,0:T(8,128)(2,1)S(1)} %get-tuple-element.39), channel_id=1, source_target_pairs={{0,7},{1,6},{2,5},{3,4},{4,3},{5,2},{6,1},{7,0},{8,15},{9,14},{10,... | collective-permute-start | bytes 98312 | tf_op jit(solution)/shard_map/ppermute | solution.py:287
  48.2 6.3 %collective-permute-start.9 = (bf16[128,1024]{1,0:T(8,128)(2,1)S(1)}, bf16[128,1024]{1,0:T(8,128)(2,1)S(1)}, u32[]{:S(2)}, u32[]{:S(2)}) collective-permute-start(bf16[128,1024]{1,0:T(8,128)(2,1)S(1)} %place.1.refs_0_), channel_id=1, source_target_pairs={{0,56},{8,0},{16,8},{24,16},{32,24},{40,32},{48,40},{56,48},{1,57}... | collective-permute-start | bytes 786440 | tf_op jit(solution)/shard_map/ppermute | solution.py:46
  51.1 6.4 %collective-permute-start.11 = (bf16[128,1024]{1,0:T(8,128)(2,1)S(1)}, bf16[128,1024]{1,0:T(8,128)(2,1)S(1)}, u32[]{:S(2)}, u32[]{:S(2)}) collective-permute-start(bf16[128,1024]{1,0:T(8,128)(2,1)S(1)} %place.1.refs_0_), channel_id=1, source_target_pairs={{0,8},{8,16},{16,24},{24,32},{32,40},{40,48},{48,56},{56,0},{1,9},... | collective-permute-start | bytes 786440 | tf_op jit(solution)/shard_map/ppermute | solution.py:46
  51.1 0.7 copy-start.5
  57.6 2.3 %copy-start.3 = (bf16[128,1024]{1,0:T(8,128)(2,1)}, bf16[128,1024]{1,0:T(8,128)(2,1)S(1)}, u32[]{:S(2)}) copy-start(bf16[128,1024]{1,0:T(8,128)(2,1)S(1)} %collective-permute-done.11.refs_6_.__) | copy-start | bytes 786436
  59.9 38.6 %all-to-all-start.1 = ((bf16[16,512,128]{2,1,0:T(8,128)(2,1)}), bf16[16,512,128]{2,1,0:T(8,128)(2,1)S(1)}, u32[]{:S(2)}, u32[]{:S(2)}) async-start(bf16[16,512,128]{2,1,0:T(8,128)(2,1)} %broadcast_in_dim.2), calls=%async_computation.1 | async-start | bytes 4194304 | tf_op jit(solution)/shard_map/all_to_all | solution.py:310
  63.6 29.0 %copy-start.4 = (bf16[128,1024]{1,0:T(8,128)(2,1)S(1)}, bf16[128,1024]{1,0:T(8,128)(2,1)}, u32[]{:S(2)}) copy-start(bf16[128,1024]{1,0:T(8,128)(2,1)} %copy-done.3) | copy-start | bytes 786436
  63.6 29.0 %copy-start.6 = (bf16[128,1024]{1,0:T(8,128)(2,1)S(1)}, bf16[128,1024]{1,0:T(8,128)(2,1)}, u32[]{:S(2)}) copy-start(bf16[128,1024]{1,0:T(8,128)(2,1)} %copy-done.5) | copy-start | bytes 786436
  63.6 5.3 %collective-permute-start.10 = (bf16[128,1024]{1,0:T(8,128)(2,1)S(1)}, bf16[128,1024]{1,0:T(8,128)(2,1)S(1)}, u32[]{:S(2)}, u32[]{:S(2)}) collective-permute-start(bf16[128,1024]{1,0:T(8,128)(2,1)S(1)} %collective-permute-done.9.refs_1_._), channel_id=1, source_target_pairs={{0,56},{8,0},{16,8},{24,16},{32,24},{40,32},{48,40},{56,48},{1,57}... | collective-permute-start | bytes 786440 | tf_op jit(solution)/shard_map/ppermute | solution.py:46
  63.7 6.7 %collective-permute-start.12 = (bf16[128,1024]{1,0:T(8,128)(2,1)}, bf16[128,1024]{1,0:T(8,128)(2,1)S(1)}, u32[]{:S(2)}, u32[]{:S(2)}) collective-permute-start(bf16[128,1024]{1,0:T(8,128)(2,1)} %copy-done.3), channel_id=1, source_target_pairs={{0,8},{8,16},{16,24},{24,32},{32,40},{40,48},{48,56},{56,0},{1,9},... | collective-permute-start | bytes 786440 | tf_op jit(solution)/shard_map/ppermute | solution.py:46
  71.3 20.3 %collective-permute-start.13 = (bf16[1024,512]{1,0:T(8,128)(2,1)S(1)}, bf16[1024,512]{1,0:T(8,128)(2,1)S(1)}, u32[]{:S(2)}, u32[]{:S(2)}) collective-permute-start(bf16[1024,512]{1,0:T(8,128)(2,1)S(1)} %turn.1.h_own), channel_id=1, source_target_pairs={{0,128},{128,0},{1,129},{129,1},{2,130},{130,2},{3,131},{131,3},{4... | collective-permute-start | bytes 3145736 | tf_op jit(solution)/shard_map/ppermute | solution.py:46
  77.3 8.8 %collective-permute-start.15 = (bf16[128,1024]{1,0:T(8,128)(2,1)S(1)}, bf16[128,1024]{1,0:T(8,128)(2,1)S(1)}, u32[]{:S(2)}, u32[]{:S(2)}) collective-permute-start(bf16[128,1024]{1,0:T(8,128)(2,1)S(1)} %collective-permute-done.12.__.refs_5_), channel_id=1, source_target_pairs={{0,8},{8,16},{16,24},{24,32},{32,40},{40,48},{48,56},{56,0},{1,9},... | collective-permute-start | bytes 786440 | tf_op jit(solution)/shard_map/ppermute | solution.py:46
  77.6 8.7 %collective-permute-start.14 = (bf16[128,1024]{1,0:T(8,128)(2,1)S(1)}, bf16[128,1024]{1,0:T(8,128)(2,1)S(1)}, u32[]{:S(2)}, u32[]{:S(2)}) collective-permute-start(bf16[128,1024]{1,0:T(8,128)(2,1)S(1)} %collective-permute-done.10._.refs_2_), channel_id=1, source_target_pairs={{0,56},{8,0},{16,8},{24,16},{32,24},{40,32},{48,40},{56,48},{1,57}... | collective-permute-start | bytes 786440 | tf_op jit(solution)/shard_map/ppermute | solution.py:46
  86.2 5.4 %collective-permute-start.16 = (bf16[64,1024]{1,0:T(8,128)(2,1)S(1)}, bf16[64,1024]{1,0:T(8,128)(2,1)S(1)}, u32[]{:S(2)}, u32[]{:S(2)}) collective-permute-start(bf16[64,1024]{1,0:T(8,128)(2,1)S(1)} %slice.8), channel_id=1, source_target_pairs={{0,8},{8,16},{16,24},{24,32},{32,40},{40,48},{48,56},{56,0},{1,9},... | collective-permute-start | bytes 393224 | tf_op jit(solution)/shard_map/ppermute | solution.py:46
  86.3 5.3 %collective-permute-start.17 = (bf16[64,1024]{1,0:T(8,128)(2,1)S(1)}, bf16[64,1024]{1,0:T(8,128)(2,1)S(1)}, u32[]{:S(2)}, u32[]{:S(2)}) collective-permute-start(bf16[64,1024]{1,0:T(8,128)(2,1)S(1)} %slice.9), channel_id=1, source_target_pairs={{0,56},{8,0},{16,8},{24,16},{32,24},{40,32},{48,40},{56,48},{1,57}... | collective-permute-start | bytes 393224 | tf_op jit(solution)/shard_map/ppermute | solution.py:46
  91.6 1.0 copy-start.13
  97.5 1.0 copy-start.1
  98.4 48.1 %all-to-all-start.2 = ((bf16[16,2,256,128]{3,2,1,0:T(8,128)(2,1)}), bf16[16,2,256,128]{3,2,1,0:T(8,128)(2,1)}, u32[]{:S(2)}, u32[]{:S(2)}) async-start(bf16[16,2,256,128]{3,2,1,0:T(8,128)(2,1)} %bitcast.4), calls=%async_computation.2 | async-start | bytes 4194304 | tf_op jit(solution)/shard_map/all_to_all | solution.py:344
  105.1 1.2 copy-start.2
  107.6 4.8 %collective-permute-start.18 = (bf16[512,1024]{1,0:T(8,128)(2,1)S(1)}, bf16[512,1024]{1,0:T(8,128)(2,1)S(1)}, u32[]{:S(2)}, u32[]{:S(2)}) collective-permute-start(bf16[512,1024]{1,0:T(8,128)(2,1)S(1)} %term.1), channel_id=1, source_target_pairs={{0,128},{128,0},{1,129},{129,1},{2,130},{130,2},{3,131},{131,3},{4... | collective-permute-start | bytes 3145736 | tf_op jit(solution)/shard_map/ppermute | solution.py:46
  113.8 10.9 %collective-permute-start.19 = (bf16[64,1024]{1,0:T(8,128)(2,1)S(1)}, bf16[64,1024]{1,0:T(8,128)(2,1)S(1)}, u32[]{:S(2)}, u32[]{:S(2)}) collective-permute-start(bf16[64,1024]{1,0:T(8,128)(2,1)S(1)} %get-tuple-element.43), channel_id=1, source_target_pairs={{0,8},{8,16},{16,24},{24,32},{32,40},{40,48},{48,56},{56,0},{1,9},... | collective-permute-start | bytes 393224 | tf_op jit(solution)/shard_map/ppermute | solution.py:46
  113.8 15.0 %collective-permute-start.20 = (bf16[64,1024]{1,0:T(8,128)(2,1)S(1)}, bf16[64,1024]{1,0:T(8,128)(2,1)S(1)}, u32[]{:S(2)}, u32[]{:S(2)}) collective-permute-start(bf16[64,1024]{1,0:T(8,128)(2,1)S(1)} %get-tuple-element.44), channel_id=1, source_target_pairs={{0,16},{8,24},{16,32},{24,40},{32,48},{40,56},{48,0},{56,8},{1,17}... | collective-permute-start | bytes 393224 | tf_op jit(solution)/shard_map/ppermute | solution.py:46
  117.6 17.6 %collective-permute-start.21 = (bf16[64,1024]{1,0:T(8,128)(2,1)S(1)}, bf16[64,1024]{1,0:T(8,128)(2,1)S(1)}, u32[]{:S(2)}, u32[]{:S(2)}) collective-permute-start(bf16[64,1024]{1,0:T(8,128)(2,1)S(1)} %get-tuple-element.45), channel_id=1, source_target_pairs={{0,24},{8,32},{16,40},{24,48},{32,56},{40,0},{48,8},{56,16},{1,25}... | collective-permute-start | bytes 393224 | tf_op jit(solution)/shard_map/ppermute | solution.py:46
  117.6 17.9 %collective-permute-start.22 = (bf16[64,1024]{1,0:T(8,128)(2,1)S(1)}, bf16[64,1024]{1,0:T(8,128)(2,1)S(1)}, u32[]{:S(2)}, u32[]{:S(2)}) collective-permute-start(bf16[64,1024]{1,0:T(8,128)(2,1)S(1)} %get-tuple-element.46), channel_id=1, source_target_pairs={{0,32},{8,40},{16,48},{24,56},{32,0},{40,8},{48,16},{56,24},{1,33}... | collective-permute-start | bytes 393224 | tf_op jit(solution)/shard_map/ppermute | solution.py:46
  120.3 15.2 %collective-permute-start.23 = (bf16[64,1024]{1,0:T(8,128)(2,1)S(1)}, bf16[64,1024]{1,0:T(8,128)(2,1)S(1)}, u32[]{:S(2)}, u32[]{:S(2)}) collective-permute-start(bf16[64,1024]{1,0:T(8,128)(2,1)S(1)} %get-tuple-element.47), channel_id=1, source_target_pairs={{0,40},{8,48},{16,56},{24,0},{32,8},{40,16},{48,24},{56,32},{1,41}... | collective-permute-start | bytes 393224 | tf_op jit(solution)/shard_map/ppermute | solution.py:46
  124.6 19.2 %collective-permute-start.24 = (bf16[64,1024]{1,0:T(8,128)(2,1)S(1)}, bf16[64,1024]{1,0:T(8,128)(2,1)S(1)}, u32[]{:S(2)}, u32[]{:S(2)}) collective-permute-start(bf16[64,1024]{1,0:T(8,128)(2,1)S(1)} %get-tuple-element.48), channel_id=1, source_target_pairs={{0,48},{8,56},{16,0},{24,8},{32,16},{40,24},{48,32},{56,40},{1,49}... | collective-permute-start | bytes 393224 | tf_op jit(solution)/shard_map/ppermute | solution.py:46
  128.9 22.5 %copy-start.12 = (f32[2,2,256,128]{3,2,1,0:T(8,128)S(1)}, f32[2,2,256,128]{3,2,1,0:T(8,128)}, u32[]{:S(2)}) copy-start(f32[2,2,256,128]{3,2,1,0:T(8,128)} %copy-done.11) | copy-start | bytes 1572868
  128.9 17.7 %collective-permute-start.25 = (bf16[64,1024]{1,0:T(8,128)(2,1)S(1)}, bf16[64,1024]{1,0:T(8,128)(2,1)S(1)}, u32[]{:S(2)}, u32[]{:S(2)}) collective-permute-start(bf16[64,1024]{1,0:T(8,128)(2,1)S(1)} %get-tuple-element.49), channel_id=1, source_target_pairs={{0,56},{8,0},{16,8},{24,16},{32,24},{40,32},{48,40},{56,48},{1,57}... | collective-permute-start | bytes 393224 | tf_op jit(solution)/shard_map/ppermute | solution.py:46
  148.5 2.2 %collective-permute-start.26 = (f32[256,128]{1,0:T(8,128)S(1)}, f32[256,128]{1,0:T(8,128)S(1)}, u32[]{:S(2)}, u32[]{:S(2)}) collective-permute-start(f32[256,128]{1,0:T(8,128)S(1)} %get-tuple-element.52), channel_id=1, source_target_pairs={{0,128},{128,0},{1,129},{129,1},{2,130},{130,2},{3,131},{131,3},{4... | collective-permute-start | bytes 393224 | tf_op jit(solution)/shard_map/ppermute | solution.py:46
where the time goes:
time: 153 us; the launch traced here: 152 us
  starting transfers between devices  63.6 us (42%)
  waiting for transfers between devices  50.8 us (33%)
  Pallas kernels  26.1 us (17%)
  local copies, waits for them, and re-layouts  9.38 us (6%)
    ppermute x20, waiting for transfers between devices, shift(): lax.ppermute(block, axis, [(i, (i + by) % count) for i in range(count)])  44.5 us
    ppermute x20, starting transfers between devices, shift(): lax.ppermute(block, axis, [(i, (i + by) % count) for i in range(count)])  34.5 us
    ppermute x7, starting transfers between devices, on_device(): lax.ppermute(pieces[k], 'tensor', [(i, i ^ k) for i in range(TEN)])  12.3 us
    pallas_call x1, Pallas kernels, attention_grads(): pl.pallas_call(attention_kernel, grid=(GROUP // STEP_HEADS,), in_specs=[S...  11.1 us
    unnamed x29, local copies, waits for them, and re-layouts  7.62 us
    all_to_all x1, starting transfers between devices, on_device(): lax.all_to_all(partial, PLANE, split_axis=0, concat_axis=0, tiled=True)  6.65 us
    all_to_all x1, starting transfers between devices, on_device(): lax.all_to_all(hidden, 'z', split_axis=0, concat_axis=0, tiled=True)  6.45 us
    ppermute x7, waiting for transfers between devices, on_device(): lax.ppermute(pieces[k], 'tensor', [(i, i ^ k) for i in range(TEN)])  6.37 us
  transfers between devices with their start and end apart: 30, of which 16 were waited for; matrix products, arithmetic and copies ran while one was open for 0% of the time, Pallas kernels for 15%

commit v1 on v0

--- a/solution.py
+++ b/solution.py
@@ -24,6 +24,7 @@
 VMEM = pl.BlockSpec(memory_space=pltpu.VMEM)
 SMEM = pl.BlockSpec(memory_space=pltpu.SMEM)
 ANY = pl.BlockSpec(memory_space=pl.ANY)
+HBM = pl.BlockSpec(memory_space=pltpu.HBM)
 
 
 def dot(a, b, ca, cb):
@@ -54,7 +55,7 @@
     return [jnp.asarray(t.astype(np.float32)) for t in wide]
 
 
-def attention_kernel(at_ref, q_ref, k_ref, v_ref, g_ref, c_ref, s_ref, _, qg_ref, own_ref, other_ref, kt, dk, dv):
+def attention_kernel(at_ref, q_ref, k_ref, v_ref, g_ref, c_ref, s_ref, qg_ref, own_ref, other_ref, kt, dk, dv):
     step = pl.program_id(0)
 
     @pl.when(step == 0)
@@ -105,13 +106,13 @@
             other_ref[...] = key_grad
 
 
-def attention_grads(where_at, queries, keys, values, out_grad, before):
+def attention_grads(where_at, queries, keys, values, out_grad):
     whole = pl.BlockSpec((LEN, HD), lambda h: (0, 0))
     head = pl.BlockSpec((LEN, STEP_HEADS * HD), lambda h: (0, h))
     return pl.pallas_call(
         attention_kernel,
         grid=(GROUP // STEP_HEADS,),
-        in_specs=[SMEM, head, whole, whole, head, whole, whole, ANY],
+        in_specs=[SMEM, head, whole, whole, head, whole, whole],
         out_specs=[head, whole, whole],
         out_shape=[struct(LEN, GROUP * HD), struct(LEN, HD), struct(LEN, HD)],
         scratch_shapes=[
@@ -122,7 +123,7 @@
         compiler_params=params(60),
         cost_estimate=cost(12 * 10**9, 4 * 2**20),
         name="attention_grads",
-    )(where_at, queries, keys, values, out_grad, *rope_wide(), before)
+    )(where_at, queries, keys, values, out_grad, *rope_wide())
 
 
 def deal_kernel(x_ref, out_ref):
@@ -150,7 +151,7 @@
         out_ref[:, pl.ds(at, HD)] = piece[...]
 
 
-def select_kernel(at_ref, key_ref, value_ref, _, __, out_ref):
+def select_kernel(at_ref, key_ref, value_ref, _, out_ref):
     @pl.when(at_ref[0] == 0)
     def _():
         out_ref[...] = key_ref[...]
@@ -195,8 +196,11 @@
 
 
 def weight_grad_kernel(h_own, h_other, *refs):
-    near, (far_up, far_down, out_ref, own_ref, other_ref) = refs[: Z - 1], refs[Z - 1 :]
+    near, (far_up, far_down, state_ref) = refs[: Z - 1], refs[Z - 1 : Z + 2]
+    out_ref, own_ref, other_ref, state_out, sem = refs[Z + 2 :]
     rows = far_up.shape[0]
+    passing = pltpu.make_async_copy(state_ref, state_out, sem)
+    passing.start()
     for j in range(Z):
         at = slice(j * rows, (j + 1) * rows)
         if j == Z // 2:
@@ -216,6 +220,7 @@
                 part = (part + dot(h_other[at, :], other_ref[:, cols], 1, 0)).astype(BF)
                 out_ref[y, 2 * pair, r] = part[:, :HD]
                 out_ref[y, 2 * pair + 1, r] = part[:, HD:]
+    passing.wait()
 
 
 def sum_kernel(at_ref, x_ref, *refs):
@@ -271,7 +276,7 @@
     )(hidden_in)
     hidden = lax.all_to_all(hidden, "z", split_axis=0, concat_axis=0, tiled=True)
 
-    query_grad, own, other = attention_grads(where_at, queries, keys, values, out_grad, state_backup)
+    query_grad, own, other = attention_grads(where_at, queries, keys, values, out_grad)
     other = shift(other, "rep", REP, 1)
     pieces = pl.pallas_call(
         split_kernel,
@@ -299,13 +304,13 @@
 
     weight = pl.pallas_call(
         select_kernel,
-        in_specs=[SMEM, VMEM, VMEM, ANY, ANY],
+        in_specs=[SMEM, VMEM, VMEM, ANY],
         out_specs=VMEM,
         out_shape=struct(w_rows, HD),
         compiler_params=params(8),
         cost_estimate=cost(0, 2**18),
         name="select",
-    )(where_at, w_key, w_value, near[1], near[-1])
+    )(where_at, w_key, w_value, grads)
     weight = jnp.broadcast_to(weight[None], (YLO * TEN,) + weight.shape)
     weight = lax.all_to_all(weight, PLANE, split_axis=0, concat_axis=0, tiled=True)
 
@@ -321,15 +326,17 @@
     hidden_other = shift(hidden, "rep", REP, 1)
 
     half = struct(Z * rows, TEN * HD)
-    partial, grads_own, grads_other = pl.pallas_call(
+    state = jax.ShapeDtypeStruct(adam_state.shape, adam_state.dtype)
+    partial, grads_own, grads_other, state_backup = pl.pallas_call(
         weight_grad_kernel,
-        in_specs=[VMEM] * (Z + 3),
-        out_specs=[VMEM] * 3,
-        out_shape=[struct(YLO, TEN, REP, out_rows, HD), half, half],
+        in_specs=[VMEM] * (Z + 3) + [ANY],
+        out_specs=[VMEM] * 3 + [HBM],
+        out_shape=[struct(YLO, TEN, REP, out_rows, HD), half, half, state],
+        scratch_shapes=[pltpu.SemaphoreType.DMA],
         compiler_params=params(48),
-        cost_estimate=cost(2 * 2**30, 8 * 2**20),
+        cost_estimate=cost(2 * 2**31, 8 * 2**20),
         name="weight_grad",
-    )(hidden, hidden_other, *near, far_up, far_down)
+    )(hidden, hidden_other, *near, far_up, far_down, state_backup)
     given = pl.pallas_call(
         term_kernel,
         in_specs=[VMEM] * 2,
@@ -368,13 +375,13 @@
 
     kept, passed = pl.pallas_call(
         sum_kernel,
-        in_specs=[SMEM, VMEM] + [ANY] * (Z - 1),
+        in_specs=[SMEM, VMEM] + [ANY] * 3,
         out_specs=[VMEM] * 2,
         out_shape=[struct(out_rows, HD, dtype=F32)] * 2,
         compiler_params=params(16),
         cost_estimate=cost(0, 2 * 2**20),
         name="sum",
-    )(where_at, partial, *moved[1:])
+    )(where_at, partial, moved[4], moved[3], moved[5])
     passed = shift(passed, "rep", REP, 1)
     key_weight_grad = jnp.where(first, kept, passed)
     value_weight_grad = jnp.where(first, passed, kept)

time: 153 us -> 141 us (0.922)
  waiting for transfers between devices: 50.8 us -> 33.1 us
  starting transfers between devices: 63.6 us -> 71.5 us
  local copies, waits for them, and re-layouts: 9.38 us -> 7.06 us
    ppermute x20, waiting for transfers between devices: 44.5 us -> 26.7 us  [shift(): lax.ppermute(block, axis, [(i, (i + by) % count) for i in range(count)])]
    ppermute x20, starting transfers between devices: 34.5 us -> 39.8 us  [shift(): lax.ppermute(block, axis, [(i, (i + by) % count) for i in range(count)])]
    all_to_all x1, starting transfers between devices: 6.45 us -> 9.01 us  [on_device(): lax.all_to_all(hidden, 'z', split_axis=0, concat_axis=0, tiled=True)]
    unnamed x29 -> x18, local copies, waits for them, and re-layouts: 7.62 us -> 5.29 us
  transfers between devices with their start and end apart: 30 -> 30, of which waited for: 16 -> 12; matrix products, arithmetic and copies ran while one was open for 0% -> 2% of each run, Pallas kernels for 15% -> 18%
where the time goes in v1:
time: 141 us
  starting transfers between devices  71.5 us (51%)
  waiting for transfers between devices  33.1 us (23%)
  Pallas kernels  26.9 us (19%)
  local copies, waits for them, and re-layouts  7.06 us (5%)
    ppermute x20, starting transfers between devices, shift(): lax.ppermute(block, axis, [(i, (i + by) % count) for i in range(count)])  39.8 us
    ppermute x20, waiting for transfers between devices, shift(): lax.ppermute(block, axis, [(i, (i + by) % count) for i in range(count)])  26.7 us
    ppermute x7, starting transfers between devices, on_device(): lax.ppermute(pieces[k], 'tensor', [(i, i ^ k) for i in range(TEN)])  12.3 us
    pallas_call x1, Pallas kernels, attention_grads(): pl.pallas_call(attention_kernel, grid=(GROUP // STEP_HEADS,), in_specs=[S...  11.2 us
    all_to_all x1, starting transfers between devices, on_device(): lax.all_to_all(hidden, 'z', split_axis=0, concat_axis=0, tiled=True)  9.01 us
    all_to_all x1, starting transfers between devices, on_device(): lax.all_to_all(partial, PLANE, split_axis=0, concat_axis=0, tiled=True)  6.59 us
    ppermute x7, waiting for transfers between devices, on_device(): lax.ppermute(pieces[k], 'tensor', [(i, i ^ k) for i in range(TEN)])  6.37 us
    unnamed x18, local copies, waits for them, and re-layouts  5.29 us
  transfers between devices with their start and end apart: 30, of which 12 were waited for; matrix products, arithmetic and copies ran while one was open for 2% of the time, Pallas kernels for 18%

profile of v1, /device:TPU:1, one launch (start us, length us, event | category | flops | bytes accessed | tf_op | source)
XLA Modules:
  0.0 140.7 jit_solution(4475970188855619532)
XLA Ops:
  0.6 1.2 copy-done
  1.9 1.5 %deal.1 = bf16[8,64,1024]{2,1,0:T(8,128)(2,1)} custom-call(bf16[64,8192]{1,0:T(8,128)(2,1)S(1)} %copy-done), custom_call_target="tpu_custom_call" | custom-call | bytes 2097152 | tf_op jit(solution)/shard_map/deal/pallas_call | solution.py:267
  3.4 9.0 %all-to-all-start = ((bf16[8,64,1024]{2,1,0:T(8,128)(2,1)}), bf16[8,64,1024]{2,1,0:T(8,128)(2,1)S(1)}, u32[]{:S(2)}, u32[]{:S(2)}) async-start(bf16[8,64,1024]{2,1,0:T(8,128)(2,1)} %deal.1), calls=%async_computation | async-start | bytes 2097152 | tf_op jit(solution)/shard_map/all_to_all | solution.py:277
  13.0 11.2 %attention_grads.1 = (bf16[512,1024]{1,0:T(8,128)(2,1)}, bf16[512,128]{1,0:T(8,128)(2,1)}, bf16[512,128]{1,0:T(8,128)(2,1)}) custom-call(s32[3]{0:T(128)} %pad_add_fusion.at_ref, bf16[512,1024]{1,0:T(8,128)(2,1)} %q_ref.1, bf16[512,128]{1,0:T(8,128)(2,1)} %k_ref.1, bf16[512,128]{1,0:T(8,128)(2,1)} %v_ref.1, bf16[512,1024]{1,0:T(8,128)(2,1)} %g_ref.1, ...), custom_call_target="tpu_custom_call" | custom-call | flops 12000000000 | bytes 4194304 | tf_op jit(solution)/shard_map/attention_grads/pallas_call | solution.py:112
  24.2 1.0 collective-permute-start
  25.2 1.2 collective-permute-done.other_ref
  26.4 0.9 copy-done.3
  27.9 3.0 %collective-permute-start.1 = (bf16[128,128]{1,0:T(8,128)(2,1)S(1)}, bf16[128,128]{1,0:T(8,128)(2,1)S(1)}, u32[]{:S(2)}, u32[]{:S(2)}) collective-permute-start(bf16[128,128]{1,0:T(8,128)(2,1)S(1)} %get-tuple-element.34), channel_id=1, source_target_pairs={{0,1},{1,0},{2,3},{3,2},{4,5},{5,4},{6,7},{7,6},{8,9},{9,8},{10,11... | collective-permute-start | bytes 98312 | tf_op jit(solution)/shard_map/ppermute | solution.py:292
  30.9 1.2 collective-permute-start.2
  32.2 2.7 %collective-permute-start.4 = (bf16[128,128]{1,0:T(8,128)(2,1)S(1)}, bf16[128,128]{1,0:T(8,128)(2,1)S(1)}, u32[]{:S(2)}, u32[]{:S(2)}) collective-permute-start(bf16[128,128]{1,0:T(8,128)(2,1)S(1)} %get-tuple-element.37), channel_id=1, source_target_pairs={{0,4},{1,5},{2,6},{3,7},{4,0},{5,1},{6,2},{7,3},{8,12},{9,13},{10,... | collective-permute-start | bytes 98312 | tf_op jit(solution)/shard_map/ppermute | solution.py:292
  34.9 2.8 %collective-permute-start.5 = (bf16[128,128]{1,0:T(8,128)(2,1)S(1)}, bf16[128,128]{1,0:T(8,128)(2,1)S(1)}, u32[]{:S(2)}, u32[]{:S(2)}) collective-permute-start(bf16[128,128]{1,0:T(8,128)(2,1)S(1)} %get-tuple-element.38), channel_id=1, source_target_pairs={{0,5},{1,4},{2,7},{3,6},{4,1},{5,0},{6,3},{7,2},{8,13},{9,12},{10,... | collective-permute-start | bytes 98312 | tf_op jit(solution)/shard_map/ppermute | solution.py:292
  37.7 2.5 %collective-permute-start.6 = (bf16[128,128]{1,0:T(8,128)(2,1)S(1)}, bf16[128,128]{1,0:T(8,128)(2,1)S(1)}, u32[]{:S(2)}, u32[]{:S(2)}) collective-permute-start(bf16[128,128]{1,0:T(8,128)(2,1)S(1)} %get-tuple-element.39), channel_id=1, source_target_pairs={{0,6},{1,7},{2,4},{3,5},{4,2},{5,3},{6,0},{7,1},{8,14},{9,15},{10,... | collective-permute-start | bytes 98312 | tf_op jit(solution)/shard_map/ppermute | solution.py:292
  40.2 1.5 %collective-permute-done.5.refs_5_ = bf16[128,128]{1,0:T(8,128)(2,1)S(1)} collective-permute-done((bf16[128,128]{1,0:T(8,128)(2,1)S(1)}, bf16[128,128]{1,0:T(8,128)(2,1)S(1)}, u32[]{:S(2)}, u32[]{:S(2)}) %collective-permute-start.5) | collective-permute-done | bytes 32800 | tf_op jit(solution)/shard_map/ppermute | solution.py:292
  41.7 0.7 collective-permute-done.6.refs_6_
  42.3 4.2 %collective-permute-done.7.refs_7_ = bf16[128,128]{1,0:T(8,128)(2,1)S(1)} collective-permute-done((bf16[128,128]{1,0:T(8,128)(2,1)S(1)}, bf16[128,128]{1,0:T(8,128)(2,1)S(1)}, u32[]{:S(2)}, u32[]{:S(2)}) %collective-permute-start.7) | collective-permute-done | bytes 32800 | tf_op jit(solution)/shard_map/ppermute | solution.py:292
  47.2 3.0 %collective-permute-start.8 = (bf16[128,1024]{1,0:T(8,128)(2,1)S(1)}, bf16[128,1024]{1,0:T(8,128)(2,1)}, u32[]{:S(2)}, u32[]{:S(2)}) collective-permute-start(bf16[128,1024]{1,0:T(8,128)(2,1)S(1)} %place.1.refs_0_._), channel_id=1, source_target_pairs={{0,56},{8,0},{16,8},{24,16},{32,24},{40,32},{48,40},{56,48},{1,57}... | collective-permute-start | bytes 786440 | tf_op jit(solution)/shard_map/ppermute | solution.py:47
  50.8 1.7 %broadcast_in_dim.2 = bf16[16,512,128]{2,1,0:T(8,128)(2,1)} broadcast(bf16[512,128]{1,0:T(8,128)(2,1)S(1)} %select.1), dimensions={1,2} | broadcast | bytes 2228224 | tf_op jit(solution)/shard_map/broadcast_in_dim | solution.py:314
  52.6 3.7 %all-to-all-start.1 = ((bf16[16,512,128]{2,1,0:T(8,128)(2,1)}), bf16[16,512,128]{2,1,0:T(8,128)(2,1)S(1)}, u32[]{:S(2)}, u32[]{:S(2)}) async-start(bf16[16,512,128]{2,1,0:T(8,128)(2,1)} %broadcast_in_dim.2), calls=%async_computation.1 | async-start | bytes 4194304 | tf_op jit(solution)/shard_map/all_to_all | solution.py:315
  56.3 2.7 %collective-permute-start.9 = (bf16[128,1024]{1,0:T(8,128)(2,1)}, bf16[128,1024]{1,0:T(8,128)(2,1)S(1)}, u32[]{:S(2)}, u32[]{:S(2)}) collective-permute-start(bf16[128,1024]{1,0:T(8,128)(2,1)} %collective-permute-done.8.refs_1_), channel_id=1, source_target_pairs={{0,56},{8,0},{16,8},{24,16},{32,24},{40,32},{48,40},{56,48},{1,57}... | collective-permute-start | bytes 786440 | tf_op jit(solution)/shard_map/ppermute | solution.py:47
  59.1 3.6 %collective-permute-done.9._.refs_2_ = bf16[128,1024]{1,0:T(8,128)(2,1)S(1)} collective-permute-done((bf16[128,1024]{1,0:T(8,128)(2,1)}, bf16[128,1024]{1,0:T(8,128)(2,1)S(1)}, u32[]{:S(2)}, u32[]{:S(2)}) %collective-permute-start.9) | collective-permute-done | bytes 262176 | tf_op jit(solution)/shard_map/ppermute | solution.py:47
  62.7 3.3 %collective-permute-done.11.__.refs_5_ = bf16[128,1024]{1,0:T(8,128)(2,1)S(1)} collective-permute-done((bf16[128,1024]{1,0:T(8,128)(2,1)}, bf16[128,1024]{1,0:T(8,128)(2,1)S(1)}, u32[]{:S(2)}, u32[]{:S(2)}) %collective-permute-start.11) | collective-permute-done | bytes 262176 | tf_op jit(solution)/shard_map/ppermute | solution.py:47
  66.0 0.9 turn.1.h_own
  66.9 5.0 %collective-permute-start.12 = (bf16[1024,512]{1,0:T(8,128)(2,1)S(1)}, bf16[1024,512]{1,0:T(8,128)(2,1)S(1)}, u32[]{:S(2)}, u32[]{:S(2)}) collective-permute-start(bf16[1024,512]{1,0:T(8,128)(2,1)S(1)} %turn.1.h_own), channel_id=1, source_target_pairs={{0,128},{128,0},{1,129},{129,1},{2,130},{130,2},{3,131},{131,3},{4... | collective-permute-start | bytes 3145736 | tf_op jit(solution)/shard_map/ppermute | solution.py:47
  72.0 2.7 %collective-permute-start.13 = (bf16[128,1024]{1,0:T(8,128)(2,1)S(1)}, bf16[128,1024]{1,0:T(8,128)(2,1)S(1)}, u32[]{:S(2)}, u32[]{:S(2)}) collective-permute-start(bf16[128,1024]{1,0:T(8,128)(2,1)S(1)} %collective-permute-done.9._.refs_2_), channel_id=1, source_target_pairs={{0,56},{8,0},{16,8},{24,16},{32,24},{40,32},{48,40},{56,48},{1,57}... | collective-permute-start | bytes 786440 | tf_op jit(solution)/shard_map/ppermute | solution.py:47
  74.6 6.0 %collective-permute-done.14.refs_4_ = bf16[128,1024]{1,0:T(8,128)(2,1)S(1)} collective-permute-done((bf16[128,1024]{1,0:T(8,128)(2,1)S(1)}, bf16[128,1024]{1,0:T(8,128)(2,1)S(1)}, u32[]{:S(2)}, u32[]{:S(2)}) %collective-permute-start.14) | collective-permute-done | bytes 262176 | tf_op jit(solution)/shard_map/ppermute | solution.py:47
  80.8 2.7 %collective-permute-start.16 = (bf16[64,1024]{1,0:T(8,128)(2,1)S(1)}, bf16[64,1024]{1,0:T(8,128)(2,1)S(1)}, u32[]{:S(2)}, u32[]{:S(2)}) collective-permute-start(bf16[64,1024]{1,0:T(8,128)(2,1)S(1)} %slice.9), channel_id=1, source_target_pairs={{0,56},{8,0},{16,8},{24,16},{32,24},{40,32},{48,40},{56,48},{1,57}... | collective-permute-start | bytes 393224 | tf_op jit(solution)/shard_map/ppermute | solution.py:47
  83.5 2.5 %collective-permute-done.15.refs_7_ = bf16[64,1024]{1,0:T(8,128)(2,1)S(1)} collective-permute-done((bf16[64,1024]{1,0:T(8,128)(2,1)S(1)}, bf16[64,1024]{1,0:T(8,128)(2,1)S(1)}, u32[]{:S(2)}, u32[]{:S(2)}) %collective-permute-start.15) | collective-permute-done | bytes 131104 | tf_op jit(solution)/shard_map/ppermute | solution.py:47
  86.1 1.0 copy-done.7
  87.0 5.0 %weight_grad.1 = (bf16[2,8,2,256,128]{4,3,2,1,0:T(8,128)(2,1)}, bf16[512,1024]{1,0:T(8,128)(2,1)S(1)}, bf16[512,1024]{1,0:T(8,128)(2,1)S(1)}, f32[2,2,256,128]{3,2,1,0:T(8,128)}) custom-call(bf16[1024,512]{1,0:T(8,128)(2,1)S(1)} %turn.1.h_own, bf16[1024,512]{1,0:T(8,128)(2,1)} %copy-done.7, bf16[128,1024]{1,0:T(8,128)(2,1)S(1)} %place.1.refs_0_._, ...), custom_call_target="tpu_custom_call" | custom-call | flops 4294967296 | bytes 8388608 | tf_op jit(solution)/shard_map/weight_grad/pallas_call | solution.py:330
  92.1 1.0 copy-done.1
  93.1 6.6 %all-to-all-start.2 = ((bf16[16,2,256,128]{3,2,1,0:T(8,128)(2,1)}), bf16[16,2,256,128]{3,2,1,0:T(8,128)(2,1)}, u32[]{:S(2)}, u32[]{:S(2)}) async-start(bf16[16,2,256,128]{3,2,1,0:T(8,128)(2,1)} %bitcast.4), calls=%async_computation.2 | async-start | bytes 4194304 | tf_op jit(solution)/shard_map/all_to_all | solution.py:351
  99.7 1.2 copy-done.2
  100.9 1.3 term.1
  102.2 2.8 %collective-permute-start.18 = (bf16[512,1024]{1,0:T(8,128)(2,1)S(1)}, bf16[512,1024]{1,0:T(8,128)(2,1)S(1)}, u32[]{:S(2)}, u32[]{:S(2)}) collective-permute-start(bf16[512,1024]{1,0:T(8,128)(2,1)S(1)} %term.1), channel_id=1, source_target_pairs={{0,128},{128,0},{1,129},{129,1},{2,130},{130,2},{3,131},{131,3},{4... | collective-permute-start | bytes 3145736 | tf_op jit(solution)/shard_map/ppermute | solution.py:47
  104.9 2.3 %collective-permute-done.18.given_ref = bf16[512,1024]{1,0:T(8,128)(2,1)S(1)} collective-permute-done((bf16[512,1024]{1,0:T(8,128)(2,1)S(1)}, bf16[512,1024]{1,0:T(8,128)(2,1)S(1)}, u32[]{:S(2)}, u32[]{:S(2)}) %collective-permute-start.18) | collective-permute-done | bytes 1048608 | tf_op jit(solution)/shard_map/ppermute | solution.py:47
  107.2 1.9 %add.5 = (bf16[64,1024]{1,0:T(8,128)(2,1)S(1)}, bf16[64,1024]{1,0:T(8,128)(2,1)}, bf16[64,1024]{1,0:T(8,128)(2,1)}, bf16[64,1024]{1,0:T(8,128)(2,1)S(1)}, bf16[6...) custom-call(bf16[512,1024]{1,0:T(8,128)(2,1)S(1)} %get-tuple-element, ...), custom_call_target="tpu_custom_call" | custom-call | flops 1073741824 | bytes 5242880 | tf_op jit(solution)/shard_map/add/pallas_call | solution.py:353
  109.1 3.6 %collective-permute-start.21 = (bf16[64,1024]{1,0:T(8,128)(2,1)S(1)}, bf16[64,1024]{1,0:T(8,128)(2,1)S(1)}, u32[]{:S(2)}, u32[]{:S(2)}) collective-permute-start(bf16[64,1024]{1,0:T(8,128)(2,1)S(1)} %get-tuple-element.46), channel_id=1, source_target_pairs={{0,24},{8,32},{16,40},{24,48},{32,56},{40,0},{48,8},{56,16},{1,25}... | collective-permute-start | bytes 393224 | tf_op jit(solution)/shard_map/ppermute | solution.py:47
  112.7 2.4 %collective-permute-start.22 = (bf16[64,1024]{1,0:T(8,128)(2,1)S(1)}, bf16[64,1024]{1,0:T(8,128)(2,1)S(1)}, u32[]{:S(2)}, u32[]{:S(2)}) collective-permute-start(bf16[64,1024]{1,0:T(8,128)(2,1)S(1)} %get-tuple-element.47), channel_id=1, source_target_pairs={{0,32},{8,40},{16,48},{24,56},{32,0},{40,8},{48,16},{56,24},{1,33}... | collective-permute-start | bytes 393224 | tf_op jit(solution)/shard_map/ppermute | solution.py:47
  115.1 1.4 %collective-permute-start.23 = (bf16[64,1024]{1,0:T(8,128)(2,1)S(1)}, bf16[64,1024]{1,0:T(8,128)(2,1)S(1)}, u32[]{:S(2)}, u32[]{:S(2)}) collective-permute-start(bf16[64,1024]{1,0:T(8,128)(2,1)S(1)} %get-tuple-element.48), channel_id=1, source_target_pairs={{0,40},{8,48},{16,56},{24,0},{32,8},{40,16},{48,24},{56,32},{1,41}... | collective-permute-start | bytes 393224 | tf_op jit(solution)/shard_map/ppermute | solution.py:47
  116.6 2.1 %collective-permute-start.20 = (bf16[64,1024]{1,0:T(8,128)(2,1)}, bf16[64,1024]{1,0:T(8,128)(2,1)S(1)}, u32[]{:S(2)}, u32[]{:S(2)}) collective-permute-start(bf16[64,1024]{1,0:T(8,128)(2,1)} %get-tuple-element.45), channel_id=1, source_target_pairs={{0,16},{8,24},{16,32},{24,40},{32,48},{40,56},{48,0},{56,8},{1,17}... | collective-permute-start | bytes 393224 | tf_op jit(solution)/shard_map/ppermute | solution.py:47
  118.7 6.8 %collective-permute-start.24 = (bf16[64,1024]{1,0:T(8,128)(2,1)S(1)}, bf16[64,1024]{1,0:T(8,128)(2,1)S(1)}, u32[]{:S(2)}, u32[]{:S(2)}) collective-permute-start(bf16[64,1024]{1,0:T(8,128)(2,1)S(1)} %get-tuple-element.49), channel_id=1, source_target_pairs={{0,48},{8,56},{16,0},{24,8},{32,16},{40,24},{48,32},{56,40},{1,49}... | collective-permute-start | bytes 393224 | tf_op jit(solution)/shard_map/ppermute | solution.py:47
  125.5 3.4 %collective-permute-done.22.refs_4_.refs_0_ = bf16[64,1024]{1,0:T(8,128)(2,1)S(1)} collective-permute-done((bf16[64,1024]{1,0:T(8,128)(2,1)S(1)}, bf16[64,1024]{1,0:T(8,128)(2,1)S(1)}, u32[]{:S(2)}, u32[]{:S(2)}) %collective-permute-start.22) | collective-permute-done | bytes 131104 | tf_op jit(solution)/shard_map/ppermute | solution.py:47
  128.9 1.9 %sum.1 = (f32[256,128]{1,0:T(8,128)S(1)}, f32[256,128]{1,0:T(8,128)S(1)}) custom-call(s32[3]{0:T(128)S(1)} %copy-done.6, bf16[16,2,256,128]{3,2,1,0:T(8,128)(2,1)} %all-to-all-done.2.x_ref, bf16[64,1024]{1,0:T(8,128)(2,1)S(1)} %collective-permute-done.22.refs_4_.refs_0_, bf16[64,1024]{1,0:T(8,128)(2,1)S(1)} %collective-permute-done.21.refs_3_.refs_1_, ...), custom_call_target="tpu_custom_call" | custom-call | bytes 2097152 | tf_op jit(solution)/shard_map/sum/pallas_call | solution.py:376
  130.8 3.3 %collective-permute-start.26 = (f32[256,128]{1,0:T(8,128)S(1)}, f32[256,128]{1,0:T(8,128)S(1)}, u32[]{:S(2)}, u32[]{:S(2)}) collective-permute-start(f32[256,128]{1,0:T(8,128)S(1)} %get-tuple-element.53), channel_id=1, source_target_pairs={{0,128},{128,0},{1,129},{129,1},{2,130},{130,2},{3,131},{131,3},{4... | collective-permute-start | bytes 393224 | tf_op jit(solution)/shard_map/ppermute | solution.py:47
  134.1 1.3 collective-permute-done.24.refs_6_
  135.4 2.9 %collective-permute-done.25.refs_7_ = bf16[64,1024]{1,0:T(8,128)(2,1)S(1)} collective-permute-done((bf16[64,1024]{1,0:T(8,128)(2,1)S(1)}, bf16[64,1024]{1,0:T(8,128)(2,1)S(1)}, u32[]{:S(2)}, u32[]{:S(2)}) %collective-permute-start.25) | collective-permute-done | bytes 131104 | tf_op jit(solution)/shard_map/ppermute | solution.py:47
  138.4 1.6 %join.1 = bf16[64,8192]{1,0:T(8,128)(2,1)} custom-call(s32[3]{0:T(128)S(1)} %copy-done.6, bf16[64,1024]{1,0:T(8,128)(2,1)S(1)} %get-tuple-element.43.refs_0_, bf16[64,1024]{1,0:T(8,128)(2,1)S(1)} %collective-permute-done.19.refs_1_, bf16[64,1024]{1,0:T(8,128)(2,1)S(1)} %collective-permute-done.20.refs_2_, ...), custom_call_target="tpu_custom_call" | custom-call | bytes 2097152 | tf_op jit(solution)/shard_map/join/pallas_call | solution.py:366
  139.9 0.7 broadcast_select_fusion
  (46 shorter events, 2.7 us)
Async XLA Ops:
  0.6 1.2 copy-start
  3.4 43.2 %all-to-all-start = ((bf16[8,64,1024]{2,1,0:T(8,128)(2,1)}), bf16[8,64,1024]{2,1,0:T(8,128)(2,1)S(1)}, u32[]{:S(2)}, u32[]{:S(2)}) async-start(bf16[8,64,1024]{2,1,0:T(8,128)(2,1)} %deal.1), calls=%async_computation | async-start | bytes 2097152 | tf_op jit(solution)/shard_map/all_to_all | solution.py:277
  13.0 13.4 %copy-start.6 = (s32[3]{0:T(128)S(1)}, s32[3]{0:T(128)}, u32[]{:S(2)}) copy-start(s32[3]{0:T(128)} %pad_add_fusion.at_ref) | copy-start | bytes 40
  13.0 37.2 %copy-start.4 = (bf16[512,128]{1,0:T(8,128)(2,1)S(1)}, bf16[512,128]{1,0:T(8,128)(2,1)}, u32[]{:S(2)}) copy-start(bf16[512,128]{1,0:T(8,128)(2,1)} %key_ref.1) | copy-start | bytes 393220
  13.0 37.2 %copy-start.5 = (bf16[512,128]{1,0:T(8,128)(2,1)S(1)}, bf16[512,128]{1,0:T(8,128)(2,1)}, u32[]{:S(2)}) copy-start(bf16[512,128]{1,0:T(8,128)(2,1)} %value_ref.1) | copy-start | bytes 393220
  24.2 2.2 %collective-permute-start = (bf16[512,128]{1,0:T(8,128)(2,1)}, bf16[512,128]{1,0:T(8,128)(2,1)S(1)}, u32[]{:S(2)}, u32[]{:S(2)}) collective-permute-start(bf16[512,128]{1,0:T(8,128)(2,1)} %get-tuple-element.32), channel_id=1, source_target_pairs={{0,128},{128,0},{1,129},{129,1},{2,130},{130,2},{3,131},{131,3},{4... | collective-permute-start | bytes 393224 | tf_op jit(solution)/shard_map/ppermute | solution.py:47
  26.4 0.9 copy-start.3
  27.9 9.8 %collective-permute-start.1 = (bf16[128,128]{1,0:T(8,128)(2,1)S(1)}, bf16[128,128]{1,0:T(8,128)(2,1)S(1)}, u32[]{:S(2)}, u32[]{:S(2)}) collective-permute-start(bf16[128,128]{1,0:T(8,128)(2,1)S(1)} %get-tuple-element.34), channel_id=1, source_target_pairs={{0,1},{1,0},{2,3},{3,2},{4,5},{5,4},{6,7},{7,6},{8,9},{9,8},{10,11... | collective-permute-start | bytes 98312 | tf_op jit(solution)/shard_map/ppermute | solution.py:292
  30.9 9.3 %collective-permute-start.2 = (bf16[128,128]{1,0:T(8,128)(2,1)S(1)}, bf16[128,128]{1,0:T(8,128)(2,1)S(1)}, u32[]{:S(2)}, u32[]{:S(2)}) collective-permute-start(bf16[128,128]{1,0:T(8,128)(2,1)S(1)} %get-tuple-element.35), channel_id=1, source_target_pairs={{0,2},{1,3},{2,0},{3,1},{4,6},{5,7},{6,4},{7,5},{8,10},{9,11},{10,... | collective-permute-start | bytes 98312 | tf_op jit(solution)/shard_map/ppermute | solution.py:292
  32.1 8.1 %collective-permute-start.3 = (bf16[128,128]{1,0:T(8,128)(2,1)S(1)}, bf16[128,128]{1,0:T(8,128)(2,1)S(1)}, u32[]{:S(2)}, u32[]{:S(2)}) collective-permute-start(bf16[128,128]{1,0:T(8,128)(2,1)S(1)} %get-tuple-element.36), channel_id=1, source_target_pairs={{0,3},{1,2},{2,1},{3,0},{4,7},{5,6},{6,5},{7,4},{8,11},{9,10},{10,... | collective-permute-start | bytes 98312 | tf_op jit(solution)/shard_map/ppermute | solution.py:292
  32.2 8.1 %collective-permute-start.4 = (bf16[128,128]{1,0:T(8,128)(2,1)S(1)}, bf16[128,128]{1,0:T(8,128)(2,1)S(1)}, u32[]{:S(2)}, u32[]{:S(2)}) collective-permute-start(bf16[128,128]{1,0:T(8,128)(2,1)S(1)} %get-tuple-element.37), channel_id=1, source_target_pairs={{0,4},{1,5},{2,6},{3,7},{4,0},{5,1},{6,2},{7,3},{8,12},{9,13},{10,... | collective-permute-start | bytes 98312 | tf_op jit(solution)/shard_map/ppermute | solution.py:292
  34.9 6.8 %collective-permute-start.5 = (bf16[128,128]{1,0:T(8,128)(2,1)S(1)}, bf16[128,128]{1,0:T(8,128)(2,1)S(1)}, u32[]{:S(2)}, u32[]{:S(2)}) collective-permute-start(bf16[128,128]{1,0:T(8,128)(2,1)S(1)} %get-tuple-element.38), channel_id=1, source_target_pairs={{0,5},{1,4},{2,7},{3,6},{4,1},{5,0},{6,3},{7,2},{8,13},{9,12},{10,... | collective-permute-start | bytes 98312 | tf_op jit(solution)/shard_map/ppermute | solution.py:292
  37.7 4.6 %collective-permute-start.6 = (bf16[128,128]{1,0:T(8,128)(2,1)S(1)}, bf16[128,128]{1,0:T(8,128)(2,1)S(1)}, u32[]{:S(2)}, u32[]{:S(2)}) collective-permute-start(bf16[128,128]{1,0:T(8,128)(2,1)S(1)} %get-tuple-element.39), channel_id=1, source_target_pairs={{0,6},{1,7},{2,4},{3,5},{4,2},{5,3},{6,0},{7,1},{8,14},{9,15},{10,... | collective-permute-start | bytes 98312 | tf_op jit(solution)/shard_map/ppermute | solution.py:292
  40.2 6.4 %collective-permute-start.7 = (bf16[128,128]{1,0:T(8,128)(2,1)S(1)}, bf16[128,128]{1,0:T(8,128)(2,1)S(1)}, u32[]{:S(2)}, u32[]{:S(2)}) collective-permute-start(bf16[128,128]{1,0:T(8,128)(2,1)S(1)} %get-tuple-element.40), channel_id=1, source_target_pairs={{0,7},{1,6},{2,5},{3,4},{4,3},{5,2},{6,1},{7,0},{8,15},{9,14},{10,... | collective-permute-start | bytes 98312 | tf_op jit(solution)/shard_map/ppermute | solution.py:292
  47.2 9.1 %collective-permute-start.8 = (bf16[128,1024]{1,0:T(8,128)(2,1)S(1)}, bf16[128,1024]{1,0:T(8,128)(2,1)}, u32[]{:S(2)}, u32[]{:S(2)}) collective-permute-start(bf16[128,1024]{1,0:T(8,128)(2,1)S(1)} %place.1.refs_0_._), channel_id=1, source_target_pairs={{0,56},{8,0},{16,8},{24,16},{32,24},{40,32},{48,40},{56,48},{1,57}... | collective-permute-start | bytes 786440 | tf_op jit(solution)/shard_map/ppermute | solution.py:47
  50.2 8.8 %collective-permute-start.10 = (bf16[128,1024]{1,0:T(8,128)(2,1)S(1)}, bf16[128,1024]{1,0:T(8,128)(2,1)}, u32[]{:S(2)}, u32[]{:S(2)}) collective-permute-start(bf16[128,1024]{1,0:T(8,128)(2,1)S(1)} %place.1.refs_0_._), channel_id=1, source_target_pairs={{0,8},{8,16},{16,24},{24,32},{32,40},{40,48},{48,56},{56,0},{1,9},... | collective-permute-start | bytes 786440 | tf_op jit(solution)/shard_map/ppermute | solution.py:47
  52.6 40.5 %all-to-all-start.1 = ((bf16[16,512,128]{2,1,0:T(8,128)(2,1)}), bf16[16,512,128]{2,1,0:T(8,128)(2,1)S(1)}, u32[]{:S(2)}, u32[]{:S(2)}) async-start(bf16[16,512,128]{2,1,0:T(8,128)(2,1)} %broadcast_in_dim.2), calls=%async_computation.1 | async-start | bytes 4194304 | tf_op jit(solution)/shard_map/all_to_all | solution.py:315
  56.3 15.6 %copy-start.8 = (f32[2,2,256,128]{3,2,1,0:T(8,128)S(1)}, f32[2,2,256,128]{3,2,1,0:T(8,128)}, u32[]{:S(2)}) copy-start(f32[2,2,256,128]{3,2,1,0:T(8,128)} %param.17) | copy-start | bytes 1572868
  56.3 6.4 %collective-permute-start.9 = (bf16[128,1024]{1,0:T(8,128)(2,1)}, bf16[128,1024]{1,0:T(8,128)(2,1)S(1)}, u32[]{:S(2)}, u32[]{:S(2)}) collective-permute-start(bf16[128,1024]{1,0:T(8,128)(2,1)} %collective-permute-done.8.refs_1_), channel_id=1, source_target_pairs={{0,56},{8,0},{16,8},{24,16},{32,24},{40,32},{48,40},{56,48},{1,57}... | collective-permute-start | bytes 786440 | tf_op jit(solution)/shard_map/ppermute | solution.py:47
  59.1 6.9 %collective-permute-start.11 = (bf16[128,1024]{1,0:T(8,128)(2,1)}, bf16[128,1024]{1,0:T(8,128)(2,1)S(1)}, u32[]{:S(2)}, u32[]{:S(2)}) collective-permute-start(bf16[128,1024]{1,0:T(8,128)(2,1)} %collective-permute-done.10.refs_6_), channel_id=1, source_target_pairs={{0,8},{8,16},{16,24},{24,32},{32,40},{40,48},{48,56},{56,0},{1,9},... | collective-permute-start | bytes 786440 | tf_op jit(solution)/shard_map/ppermute | solution.py:47
  66.9 19.2 %collective-permute-start.12 = (bf16[1024,512]{1,0:T(8,128)(2,1)S(1)}, bf16[1024,512]{1,0:T(8,128)(2,1)S(1)}, u32[]{:S(2)}, u32[]{:S(2)}) collective-permute-start(bf16[1024,512]{1,0:T(8,128)(2,1)S(1)} %turn.1.h_own), channel_id=1, source_target_pairs={{0,128},{128,0},{1,129},{129,1},{2,130},{130,2},{3,131},{131,3},{4... | collective-permute-start | bytes 3145736 | tf_op jit(solution)/shard_map/ppermute | solution.py:47
  71.8 11.7 %collective-permute-start.17 = (f32[2,2,256,128]{3,2,1,0:T(8,128)S(1)}, f32[2,2,256,128]{3,2,1,0:T(8,128)S(1)}, u32[]{:S(2)}, u32[]{:S(2)}) collective-permute-start(f32[2,2,256,128]{3,2,1,0:T(8,128)S(1)} %copy-done.8), channel_id=1, source_target_pairs={{0,128},{128,0},{1,129},{129,1},{2,130},{130,2},{3,131},{131,3},{4... | collective-permute-start | bytes 1572872 | tf_op jit(solution)/shard_map/ppermute | solution.py:47
  71.9 8.7 %collective-permute-start.14 = (bf16[128,1024]{1,0:T(8,128)(2,1)S(1)}, bf16[128,1024]{1,0:T(8,128)(2,1)S(1)}, u32[]{:S(2)}, u32[]{:S(2)}) collective-permute-start(bf16[128,1024]{1,0:T(8,128)(2,1)S(1)} %collective-permute-done.11.__.refs_5_), channel_id=1, source_target_pairs={{0,8},{8,16},{16,24},{24,32},{32,40},{40,48},{48,56},{56,0},{1,9},... | collective-permute-start | bytes 786440 | tf_op jit(solution)/shard_map/ppermute | solution.py:47
  72.0 8.8 %collective-permute-start.13 = (bf16[128,1024]{1,0:T(8,128)(2,1)S(1)}, bf16[128,1024]{1,0:T(8,128)(2,1)S(1)}, u32[]{:S(2)}, u32[]{:S(2)}) collective-permute-start(bf16[128,1024]{1,0:T(8,128)(2,1)S(1)} %collective-permute-done.9._.refs_2_), channel_id=1, source_target_pairs={{0,56},{8,0},{16,8},{24,16},{32,24},{40,32},{48,40},{56,48},{1,57}... | collective-permute-start | bytes 786440 | tf_op jit(solution)/shard_map/ppermute | solution.py:47
  80.7 5.4 %collective-permute-start.15 = (bf16[64,1024]{1,0:T(8,128)(2,1)S(1)}, bf16[64,1024]{1,0:T(8,128)(2,1)S(1)}, u32[]{:S(2)}, u32[]{:S(2)}) collective-permute-start(bf16[64,1024]{1,0:T(8,128)(2,1)S(1)} %slice.8), channel_id=1, source_target_pairs={{0,8},{8,16},{16,24},{24,32},{32,40},{40,48},{48,56},{56,0},{1,9},... | collective-permute-start | bytes 393224 | tf_op jit(solution)/shard_map/ppermute | solution.py:47
  80.8 5.3 %collective-permute-start.16 = (bf16[64,1024]{1,0:T(8,128)(2,1)S(1)}, bf16[64,1024]{1,0:T(8,128)(2,1)S(1)}, u32[]{:S(2)}, u32[]{:S(2)}) collective-permute-start(bf16[64,1024]{1,0:T(8,128)(2,1)S(1)} %slice.9), channel_id=1, source_target_pairs={{0,56},{8,0},{16,8},{24,16},{32,24},{40,32},{48,40},{56,48},{1,57}... | collective-permute-start | bytes 393224 | tf_op jit(solution)/shard_map/ppermute | solution.py:47
  86.1 1.0 copy-start.7
  92.1 1.0 copy-start.1
  93.1 35.9 %all-to-all-start.2 = ((bf16[16,2,256,128]{3,2,1,0:T(8,128)(2,1)}), bf16[16,2,256,128]{3,2,1,0:T(8,128)(2,1)}, u32[]{:S(2)}, u32[]{:S(2)}) async-start(bf16[16,2,256,128]{3,2,1,0:T(8,128)(2,1)} %bitcast.4), calls=%async_computation.2 | async-start | bytes 4194304 | tf_op jit(solution)/shard_map/all_to_all | solution.py:351
  99.7 1.2 copy-start.2
  102.2 5.0 %collective-permute-start.18 = (bf16[512,1024]{1,0:T(8,128)(2,1)S(1)}, bf16[512,1024]{1,0:T(8,128)(2,1)S(1)}, u32[]{:S(2)}, u32[]{:S(2)}) collective-permute-start(bf16[512,1024]{1,0:T(8,128)(2,1)S(1)} %term.1), channel_id=1, source_target_pairs={{0,128},{128,0},{1,129},{129,1},{2,130},{130,2},{3,131},{131,3},{4... | collective-permute-start | bytes 3145736 | tf_op jit(solution)/shard_map/ppermute | solution.py:47
  109.1 9.6 %collective-permute-start.21 = (bf16[64,1024]{1,0:T(8,128)(2,1)S(1)}, bf16[64,1024]{1,0:T(8,128)(2,1)S(1)}, u32[]{:S(2)}, u32[]{:S(2)}) collective-permute-start(bf16[64,1024]{1,0:T(8,128)(2,1)S(1)} %get-tuple-element.46), channel_id=1, source_target_pairs={{0,24},{8,32},{16,40},{24,48},{32,56},{40,0},{48,8},{56,16},{1,25}... | collective-permute-start | bytes 393224 | tf_op jit(solution)/shard_map/ppermute | solution.py:47
  112.7 16.2 %collective-permute-start.22 = (bf16[64,1024]{1,0:T(8,128)(2,1)S(1)}, bf16[64,1024]{1,0:T(8,128)(2,1)S(1)}, u32[]{:S(2)}, u32[]{:S(2)}) collective-permute-start(bf16[64,1024]{1,0:T(8,128)(2,1)S(1)} %get-tuple-element.47), channel_id=1, source_target_pairs={{0,32},{8,40},{16,48},{24,56},{32,0},{40,8},{48,16},{56,24},{1,33}... | collective-permute-start | bytes 393224 | tf_op jit(solution)/shard_map/ppermute | solution.py:47
  115.1 13.8 %collective-permute-start.23 = (bf16[64,1024]{1,0:T(8,128)(2,1)S(1)}, bf16[64,1024]{1,0:T(8,128)(2,1)S(1)}, u32[]{:S(2)}, u32[]{:S(2)}) collective-permute-start(bf16[64,1024]{1,0:T(8,128)(2,1)S(1)} %get-tuple-element.48), channel_id=1, source_target_pairs={{0,40},{8,48},{16,56},{24,0},{32,8},{40,16},{48,24},{56,32},{1,41}... | collective-permute-start | bytes 393224 | tf_op jit(solution)/shard_map/ppermute | solution.py:47
  116.6 17.5 %collective-permute-start.19 = (bf16[64,1024]{1,0:T(8,128)(2,1)}, bf16[64,1024]{1,0:T(8,128)(2,1)S(1)}, u32[]{:S(2)}, u32[]{:S(2)}) collective-permute-start(bf16[64,1024]{1,0:T(8,128)(2,1)} %get-tuple-element.44), channel_id=1, source_target_pairs={{0,8},{8,16},{16,24},{24,32},{32,40},{40,48},{48,56},{56,0},{1,9},... | collective-permute-start | bytes 393224 | tf_op jit(solution)/shard_map/ppermute | solution.py:47
  116.6 17.5 %collective-permute-start.20 = (bf16[64,1024]{1,0:T(8,128)(2,1)}, bf16[64,1024]{1,0:T(8,128)(2,1)S(1)}, u32[]{:S(2)}, u32[]{:S(2)}) collective-permute-start(bf16[64,1024]{1,0:T(8,128)(2,1)} %get-tuple-element.45), channel_id=1, source_target_pairs={{0,16},{8,24},{16,32},{24,40},{32,48},{40,56},{48,0},{56,8},{1,17}... | collective-permute-start | bytes 393224 | tf_op jit(solution)/shard_map/ppermute | solution.py:47
  118.7 16.7 %collective-permute-start.24 = (bf16[64,1024]{1,0:T(8,128)(2,1)S(1)}, bf16[64,1024]{1,0:T(8,128)(2,1)S(1)}, u32[]{:S(2)}, u32[]{:S(2)}) collective-permute-start(bf16[64,1024]{1,0:T(8,128)(2,1)S(1)} %get-tuple-element.49), channel_id=1, source_target_pairs={{0,48},{8,56},{16,0},{24,8},{32,16},{40,24},{48,32},{56,40},{1,49}... | collective-permute-start | bytes 393224 | tf_op jit(solution)/shard_map/ppermute | solution.py:47
  128.9 9.4 %collective-permute-start.25 = (bf16[64,1024]{1,0:T(8,128)(2,1)S(1)}, bf16[64,1024]{1,0:T(8,128)(2,1)S(1)}, u32[]{:S(2)}, u32[]{:S(2)}) collective-permute-start(bf16[64,1024]{1,0:T(8,128)(2,1)S(1)} %get-tuple-element.50), channel_id=1, source_target_pairs={{0,56},{8,0},{16,8},{24,16},{32,24},{40,32},{48,40},{56,48},{1,57}... | collective-permute-start | bytes 393224 | tf_op jit(solution)/shard_map/ppermute | solution.py:47
  130.8 9.1 %collective-permute-start.26 = (f32[256,128]{1,0:T(8,128)S(1)}, f32[256,128]{1,0:T(8,128)S(1)}, u32[]{:S(2)}, u32[]{:S(2)}) collective-permute-start(f32[256,128]{1,0:T(8,128)S(1)} %get-tuple-element.53), channel_id=1, source_target_pairs={{0,128},{128,0},{1,129},{129,1},{2,130},{130,2},{3,131},{131,3},{4... | collective-permute-start | bytes 393224 | tf_op jit(solution)/shard_map/ppermute | solution.py:47

commit v2 on v1

--- a/solution.py
+++ b/solution.py
@@ -18,7 +18,7 @@
 PLANE = ("ylo", "tensor")
 SCALE = 1.0 / math.sqrt(HD)
 QB = 256
-STEP_HEADS = 2
+STEP_HEADS = 4
 BF, F32 = jnp.bfloat16, jnp.float32
 
 VMEM = pl.BlockSpec(memory_space=pltpu.VMEM)
@@ -136,19 +136,31 @@
 
 def split_kernel(at_ref, own_ref, other_ref, *out_refs):
     ten = at_ref[2]
-    rows = out_refs[0].shape[0] // REP
+    rows = out_refs[0].shape[0] // 4
     for k, out_ref in enumerate(out_refs):
-        at = pl.multiple_of(lax.bitwise_xor(ten, k) * rows, rows)
-        out_ref[:rows, :] = own_ref[pl.ds(at, rows), :]
-        out_ref[rows:, :] = other_ref[pl.ds(at, rows), :]
+        for side in range(2):
+            at = pl.multiple_of(lax.bitwise_xor(ten, 2 * k + side) * rows, rows)
+            row = 2 * side * rows
+            out_ref[row : row + rows, :] = own_ref[pl.ds(at, rows), :]
+            out_ref[row + rows : row + 2 * rows, :] = other_ref[pl.ds(at, rows), :]
+
+
+def middle_kernel(*refs):
+    pieces, out_ref = refs[:-1], refs[-1]
+    rows = out_ref.shape[1]
+    for k, piece in enumerate(pieces):
+        out_ref[k] = piece[rows:, :]
 
 
 def place_kernel(at_ref, *refs):
-    pieces, out_ref = refs[:TEN], refs[-1]
+    pieces, passed_ref, out_ref = refs[: TEN // 2], refs[TEN // 2], refs[-1]
     ten = at_ref[2]
+    rows = out_ref.shape[0]
     for k, piece in enumerate(pieces):
-        at = pl.multiple_of(lax.bitwise_xor(ten, k) * HD, HD)
-        out_ref[:, pl.ds(at, HD)] = piece[...]
+        at = pl.multiple_of(lax.bitwise_xor(ten, 2 * k) * HD, HD)
+        out_ref[:, pl.ds(at, HD)] = piece[:rows, :]
+        at = pl.multiple_of(lax.bitwise_xor(ten, 2 * k + 1) * HD, HD)
+        out_ref[:, pl.ds(at, HD)] = passed_ref[k]
 
 
 def select_kernel(at_ref, key_ref, value_ref, _, out_ref):
@@ -281,24 +293,39 @@
     pieces = pl.pallas_call(
         split_kernel,
         in_specs=[SMEM, VMEM, VMEM],
-        out_specs=[VMEM] * TEN,
-        out_shape=[struct(REP * rows, HD)] * TEN,
+        out_specs=[VMEM] * (TEN // 2),
+        out_shape=[struct(2 * REP * rows, HD)] * (TEN // 2),
         compiler_params=params(8),
         cost_estimate=cost(0, 2**19),
         name="split",
     )(where_at, own, other)
+
+    def across(block, mask):
+        return lax.ppermute(block, "tensor", [(i, i ^ mask) for i in range(TEN)])
+
     moved = {0: pieces[0]}
-    for k in (5, 4, 7, 6, 1, 3, 2):
-        moved[k] = lax.ppermute(pieces[k], "tensor", [(i, i ^ k) for i in range(TEN)])
+    for k in (2, 1, 3):
+        moved[k] = across(pieces[k], 2 * k)
+    moved = [moved[k] for k in range(TEN // 2)]
+    passed = pl.pallas_call(
+        middle_kernel,
+        in_specs=[VMEM] * (TEN // 2),
+        out_specs=VMEM,
+        out_shape=struct(TEN // 2, REP * rows, HD),
+        compiler_params=params(8),
+        cost_estimate=cost(0, 2**18),
+        name="middle",
+    )(*moved)
+    passed = across(passed, 1)
     grads = pl.pallas_call(
         place_kernel,
-        in_specs=[SMEM] + [VMEM] * TEN + [ANY],
+        in_specs=[SMEM] + [VMEM] * (TEN // 2 + 1) + [ANY],
         out_specs=VMEM,
         out_shape=struct(REP * rows, TEN * HD),
         compiler_params=params(8),
         cost_estimate=cost(0, 2**19),
         name="place",
-    )(where_at, *[moved[k] for k in range(TEN)], hidden)
+    )(where_at, *moved, passed, hidden)
 
     near, far_up, far_down = ring(grads)
 
@@ -333,7 +360,7 @@
         out_specs=[VMEM] * 3 + [HBM],
         out_shape=[struct(YLO, TEN, REP, out_rows, HD), half, half, state],
         scratch_shapes=[pltpu.SemaphoreType.DMA],
-        compiler_params=params(48),
+        compiler_params=params(32),
         cost_estimate=cost(2 * 2**31, 8 * 2**20),
         name="weight_grad",
     )(hidden, hidden_other, *near, far_up, far_down, state_backup)

time: 141 us -> 136 us (0.965)
  starting transfers between devices: 71.5 us -> 67.4 us
  Pallas kernels: 26.9 us -> 25.3 us
    ppermute x7 -> x4, starting transfers between devices: 12.3 us -> 6.94 us  [across(): return lax.ppermute(block, 'tensor', [(i, i ^ mask) for i in range(TEN)])]
    pallas_call x1, Pallas kernels: 5.03 us -> 3.46 us  [on_device(): pl.pallas_call(weight_grad_kernel, in_specs=[VMEM] * (Z + 3) + [ANY], out...]
    all_to_all x1, starting transfers between devices: 3.72 us -> 5.18 us  [on_device(): lax.all_to_all(weight, PLANE, split_axis=0, concat_axis=0, tiled=True)]
    ppermute x7 -> x4, waiting for transfers between devices: 6.37 us -> 6.99 us  [across(): return lax.ppermute(block, 'tensor', [(i, i ^ mask) for i in range(TEN)])]
  transfers between devices with their start and end apart: 30 -> 27, of which waited for: 12 -> 12; matrix products, arithmetic and copies ran while one was open for 2% -> 2% of each run, Pallas kernels for 18% -> 17%
where the time goes in v2:
time: 136 us; the launch traced here: 135 us
  starting transfers between devices  67.4 us (50%)
  waiting for transfers between devices  33 us (24%)
  Pallas kernels  25.3 us (19%)
  local copies, waits for them, and re-layouts  7.42 us (5%)
    ppermute x20, starting transfers between devices, shift(): lax.ppermute(block, axis, [(i, (i + by) % count) for i in range(count)])  39.4 us
    ppermute x20, waiting for transfers between devices, shift(): lax.ppermute(block, axis, [(i, (i + by) % count) for i in range(count)])  26 us
    pallas_call x1, Pallas kernels, attention_grads(): pl.pallas_call(attention_kernel, grid=(GROUP // STEP_HEADS,), in_specs=[S...  11 us
    all_to_all x1, starting transfers between devices, on_device(): lax.all_to_all(hidden, 'z', split_axis=0, concat_axis=0, tiled=True)  9.01 us
    ppermute x4, waiting for transfers between devices, across(): return lax.ppermute(block, 'tensor', [(i, i ^ mask) for i in range(TEN)])  6.99 us
    ppermute x4, starting transfers between devices, across(): return lax.ppermute(block, 'tensor', [(i, i ^ mask) for i in range(TEN)])  6.94 us
    all_to_all x1, starting transfers between devices, on_device(): lax.all_to_all(partial, PLANE, split_axis=0, concat_axis=0, tiled=True)  6.83 us
    unnamed x18, local copies, waits for them, and re-layouts  5.64 us
  transfers between devices with their start and end apart: 27, of which 12 were waited for; matrix products, arithmetic and copies ran while one was open for 2% of the time, Pallas kernels for 17%

profile of v2, /device:TPU:1, one launch (start us, length us, event | category | flops | bytes accessed | tf_op | source)
XLA Modules:
  0.0 135.2 jit_solution(3871076839174409990)
XLA Ops:
  0.6 1.2 copy-done.1
  1.9 1.5 %deal.1 = bf16[8,64,1024]{2,1,0:T(8,128)(2,1)} custom-call(bf16[64,8192]{1,0:T(8,128)(2,1)S(1)} %copy-done.1), custom_call_target="tpu_custom_call" | custom-call | bytes 2097152 | tf_op jit(solution)/shard_map/deal/pallas_call | solution.py:279
  3.4 9.0 %all-to-all-start = ((bf16[8,64,1024]{2,1,0:T(8,128)(2,1)}), bf16[8,64,1024]{2,1,0:T(8,128)(2,1)S(1)}, u32[]{:S(2)}, u32[]{:S(2)}) async-start(bf16[8,64,1024]{2,1,0:T(8,128)(2,1)} %deal.1), calls=%async_computation | async-start | bytes 2097152 | tf_op jit(solution)/shard_map/all_to_all | solution.py:289
  12.4 0.6 pad_add_fusion.at_ref
  13.0 11.0 %attention_grads.1 = (bf16[512,1024]{1,0:T(8,128)(2,1)}, bf16[512,128]{1,0:T(8,128)(2,1)}, bf16[512,128]{1,0:T(8,128)(2,1)}) custom-call(s32[3]{0:T(128)} %pad_add_fusion.at_ref, bf16[512,1024]{1,0:T(8,128)(2,1)} %q_ref.1, bf16[512,128]{1,0:T(8,128)(2,1)} %k_ref.1, bf16[512,128]{1,0:T(8,128)(2,1)} %v_ref.1, bf16[512,1024]{1,0:T(8,128)(2,1)} %g_ref.1, ...), custom_call_target="tpu_custom_call" | custom-call | flops 12000000000 | bytes 4194304 | tf_op jit(solution)/shard_map/attention_grads/pallas_call | solution.py:112
  24.0 1.0 collective-permute-start
  25.1 1.2 collective-permute-done.other_ref
  26.3 0.9 copy-done.4
  27.7 1.3 collective-permute-start.1
  29.0 2.5 %collective-permute-start.2 = (bf16[256,128]{1,0:T(8,128)(2,1)S(1)}, bf16[256,128]{1,0:T(8,128)(2,1)S(1)}, u32[]{:S(2)}, u32[]{:S(2)}) collective-permute-start(bf16[256,128]{1,0:T(8,128)(2,1)S(1)} %get-tuple-element.31), channel_id=1, source_target_pairs={{0,4},{1,5},{2,6},{3,7},{4,0},{5,1},{6,2},{7,3},{8,12},{9,13},{10,... | collective-permute-start | bytes 196616 | tf_op jit(solution)/shard_map/ppermute | solution.py:304
  31.7 2.9 %collective-permute-done.2.refs_2_ = bf16[256,128]{1,0:T(8,128)(2,1)S(1)} collective-permute-done((bf16[256,128]{1,0:T(8,128)(2,1)S(1)}, bf16[256,128]{1,0:T(8,128)(2,1)S(1)}, u32[]{:S(2)}, u32[]{:S(2)}) %collective-permute-start.2) | collective-permute-done | bytes 65568 | tf_op jit(solution)/shard_map/ppermute | solution.py:304
  34.6 1.7 %collective-permute-done.3.refs_3_ = bf16[256,128]{1,0:T(8,128)(2,1)S(1)} collective-permute-done((bf16[256,128]{1,0:T(8,128)(2,1)S(1)}, bf16[256,128]{1,0:T(8,128)(2,1)S(1)}, u32[]{:S(2)}, u32[]{:S(2)}) %collective-permute-start.3) | collective-permute-done | bytes 65568 | tf_op jit(solution)/shard_map/ppermute | solution.py:304
  36.3 3.0 %collective-permute-start.4 = (bf16[4,128,128]{2,1,0:T(8,128)(2,1)S(1)}, bf16[4,128,128]{2,1,0:T(8,128)(2,1)S(1)}, u32[]{:S(2)}, u32[]{:S(2)}) collective-permute-start(bf16[4,128,128]{2,1,0:T(8,128)(2,1)S(1)} %middle.1), channel_id=1, source_target_pairs={{0,1},{1,0},{2,3},{3,2},{4,5},{5,4},{6,7},{7,6},{8,9},{9,8},{10,11... | collective-permute-start | bytes 393224 | tf_op jit(solution)/shard_map/ppermute | solution.py:304
  39.2 2.4 %collective-permute-done.4.refs_4_ = bf16[4,128,128]{2,1,0:T(8,128)(2,1)S(1)} collective-permute-done((bf16[4,128,128]{2,1,0:T(8,128)(2,1)S(1)}, bf16[4,128,128]{2,1,0:T(8,128)(2,1)S(1)}, u32[]{:S(2)}, u32[]{:S(2)}) %collective-permute-start.4) | collective-permute-done | bytes 131104 | tf_op jit(solution)/shard_map/ppermute | solution.py:304
  41.7 0.6 place.1.refs_0_._
  42.3 3.0 %collective-permute-start.5 = (bf16[128,1024]{1,0:T(8,128)(2,1)S(1)}, bf16[128,1024]{1,0:T(8,128)(2,1)}, u32[]{:S(2)}, u32[]{:S(2)}) collective-permute-start(bf16[128,1024]{1,0:T(8,128)(2,1)S(1)} %place.1.refs_0_._), channel_id=1, source_target_pairs={{0,56},{8,0},{16,8},{24,16},{32,24},{40,32},{48,40},{56,48},{1,57}... | collective-permute-start | bytes 786440 | tf_op jit(solution)/shard_map/ppermute | solution.py:47
  45.9 1.8 %broadcast_in_dim.2 = bf16[16,512,128]{2,1,0:T(8,128)(2,1)} broadcast(bf16[512,128]{1,0:T(8,128)(2,1)S(1)} %select.1), dimensions={1,2} | broadcast | bytes 2228224 | tf_op jit(solution)/shard_map/broadcast_in_dim | solution.py:341
  47.6 5.2 %all-to-all-start.1 = ((bf16[16,512,128]{2,1,0:T(8,128)(2,1)}), bf16[16,512,128]{2,1,0:T(8,128)(2,1)S(1)}, u32[]{:S(2)}, u32[]{:S(2)}) async-start(bf16[16,512,128]{2,1,0:T(8,128)(2,1)} %broadcast_in_dim.2), calls=%async_computation.1 | async-start | bytes 4194304 | tf_op jit(solution)/shard_map/all_to_all | solution.py:342
  52.9 2.6 %collective-permute-start.6 = (bf16[128,1024]{1,0:T(8,128)(2,1)}, bf16[128,1024]{1,0:T(8,128)(2,1)S(1)}, u32[]{:S(2)}, u32[]{:S(2)}) collective-permute-start(bf16[128,1024]{1,0:T(8,128)(2,1)} %collective-permute-done.5.refs_1_), channel_id=1, source_target_pairs={{0,56},{8,0},{16,8},{24,16},{32,24},{40,32},{48,40},{56,48},{1,57}... | collective-permute-start | bytes 786440 | tf_op jit(solution)/shard_map/ppermute | solution.py:47
  55.5 3.6 %collective-permute-done.6._.refs_2_ = bf16[128,1024]{1,0:T(8,128)(2,1)S(1)} collective-permute-done((bf16[128,1024]{1,0:T(8,128)(2,1)}, bf16[128,1024]{1,0:T(8,128)(2,1)S(1)}, u32[]{:S(2)}, u32[]{:S(2)}) %collective-permute-start.6) | collective-permute-done | bytes 262176 | tf_op jit(solution)/shard_map/ppermute | solution.py:47
  59.1 3.3 %collective-permute-done.8.__.refs_5_ = bf16[128,1024]{1,0:T(8,128)(2,1)S(1)} collective-permute-done((bf16[128,1024]{1,0:T(8,128)(2,1)}, bf16[128,1024]{1,0:T(8,128)(2,1)S(1)}, u32[]{:S(2)}, u32[]{:S(2)}) %collective-permute-start.8) | collective-permute-done | bytes 262176 | tf_op jit(solution)/shard_map/ppermute | solution.py:47
  62.4 0.9 turn.1.h_own
  63.3 4.2 %collective-permute-start.9 = (bf16[1024,512]{1,0:T(8,128)(2,1)S(1)}, bf16[1024,512]{1,0:T(8,128)(2,1)S(1)}, u32[]{:S(2)}, u32[]{:S(2)}) collective-permute-start(bf16[1024,512]{1,0:T(8,128)(2,1)S(1)} %turn.1.h_own), channel_id=1, source_target_pairs={{0,128},{128,0},{1,129},{129,1},{2,130},{130,2},{3,131},{131,3},{4... | collective-permute-start | bytes 3145736 | tf_op jit(solution)/shard_map/ppermute | solution.py:47
  67.8 2.7 %collective-permute-start.10 = (bf16[128,1024]{1,0:T(8,128)(2,1)S(1)}, bf16[128,1024]{1,0:T(8,128)(2,1)S(1)}, u32[]{:S(2)}, u32[]{:S(2)}) collective-permute-start(bf16[128,1024]{1,0:T(8,128)(2,1)S(1)} %collective-permute-done.6._.refs_2_), channel_id=1, source_target_pairs={{0,56},{8,0},{16,8},{24,16},{32,24},{40,32},{48,40},{56,48},{1,57}... | collective-permute-start | bytes 786440 | tf_op jit(solution)/shard_map/ppermute | solution.py:47
  70.5 6.2 %collective-permute-done.11.refs_4_ = bf16[128,1024]{1,0:T(8,128)(2,1)S(1)} collective-permute-done((bf16[128,1024]{1,0:T(8,128)(2,1)S(1)}, bf16[128,1024]{1,0:T(8,128)(2,1)S(1)}, u32[]{:S(2)}, u32[]{:S(2)}) %collective-permute-start.11) | collective-permute-done | bytes 262176 | tf_op jit(solution)/shard_map/ppermute | solution.py:47
  76.8 2.7 %collective-permute-start.13 = (bf16[64,1024]{1,0:T(8,128)(2,1)S(1)}, bf16[64,1024]{1,0:T(8,128)(2,1)S(1)}, u32[]{:S(2)}, u32[]{:S(2)}) collective-permute-start(bf16[64,1024]{1,0:T(8,128)(2,1)S(1)} %slice.9), channel_id=1, source_target_pairs={{0,56},{8,0},{16,8},{24,16},{32,24},{40,32},{48,40},{56,48},{1,57}... | collective-permute-start | bytes 393224 | tf_op jit(solution)/shard_map/ppermute | solution.py:47
  79.5 2.5 %collective-permute-done.12.refs_7_ = bf16[64,1024]{1,0:T(8,128)(2,1)S(1)} collective-permute-done((bf16[64,1024]{1,0:T(8,128)(2,1)S(1)}, bf16[64,1024]{1,0:T(8,128)(2,1)S(1)}, u32[]{:S(2)}, u32[]{:S(2)}) %collective-permute-start.12) | collective-permute-done | bytes 131104 | tf_op jit(solution)/shard_map/ppermute | solution.py:47
  82.1 3.5 %weight_grad.1 = (bf16[2,8,2,256,128]{4,3,2,1,0:T(8,128)(2,1)S(1)}, bf16[512,1024]{1,0:T(8,128)(2,1)S(1)}, bf16[512,1024]{1,0:T(8,128)(2,1)S(1)}, f32[2,2,256,128]{3,2,1,0:T(8,128)}) custom-call(bf16[1024,512]{1,0:T(8,128)(2,1)S(1)} %turn.1.h_own, bf16[1024,512]{1,0:T(8,128)(2,1)S(1)} %collective-permute-done.9.h_other, ...), custom_call_target="tpu_custom_call" | custom-call | flops 4294967296 | bytes 8388608 | tf_op jit(solution)/shard_map/weight_grad/pallas_call | solution.py:357
  85.6 1.3 copy-done
  86.9 1.0 copy-done.2
  87.9 6.8 %all-to-all-start.2 = ((bf16[16,2,256,128]{3,2,1,0:T(8,128)(2,1)}), bf16[16,2,256,128]{3,2,1,0:T(8,128)(2,1)}, u32[]{:S(2)}, u32[]{:S(2)}) async-start(bf16[16,2,256,128]{3,2,1,0:T(8,128)(2,1)} %bitcast.4), calls=%async_computation.2 | async-start | bytes 4194304 | tf_op jit(solution)/shard_map/all_to_all | solution.py:378
  94.7 1.2 copy-done.3
  95.9 1.3 term.1
  97.2 2.4 %collective-permute-start.15 = (bf16[512,1024]{1,0:T(8,128)(2,1)S(1)}, bf16[512,1024]{1,0:T(8,128)(2,1)S(1)}, u32[]{:S(2)}, u32[]{:S(2)}) collective-permute-start(bf16[512,1024]{1,0:T(8,128)(2,1)S(1)} %term.1), channel_id=1, source_target_pairs={{0,128},{128,0},{1,129},{129,1},{2,130},{130,2},{3,131},{131,3},{4... | collective-permute-start | bytes 3145736 | tf_op jit(solution)/shard_map/ppermute | solution.py:47
  99.6 2.3 %collective-permute-done.15.given_ref = bf16[512,1024]{1,0:T(8,128)(2,1)S(1)} collective-permute-done((bf16[512,1024]{1,0:T(8,128)(2,1)S(1)}, bf16[512,1024]{1,0:T(8,128)(2,1)S(1)}, u32[]{:S(2)}, u32[]{:S(2)}) %collective-permute-start.15) | collective-permute-done | bytes 1048608 | tf_op jit(solution)/shard_map/ppermute | solution.py:47
  101.9 1.9 %add.5 = (bf16[64,1024]{1,0:T(8,128)(2,1)S(1)}, bf16[64,1024]{1,0:T(8,128)(2,1)}, bf16[64,1024]{1,0:T(8,128)(2,1)}, bf16[64,1024]{1,0:T(8,128)(2,1)S(1)}, bf16[6...) custom-call(bf16[512,1024]{1,0:T(8,128)(2,1)S(1)} %get-tuple-element, ...), custom_call_target="tpu_custom_call" | custom-call | flops 1073741824 | bytes 5242880 | tf_op jit(solution)/shard_map/add/pallas_call | solution.py:380
  103.8 3.6 %collective-permute-start.18 = (bf16[64,1024]{1,0:T(8,128)(2,1)S(1)}, bf16[64,1024]{1,0:T(8,128)(2,1)S(1)}, u32[]{:S(2)}, u32[]{:S(2)}) collective-permute-start(bf16[64,1024]{1,0:T(8,128)(2,1)S(1)} %get-tuple-element.38), channel_id=1, source_target_pairs={{0,24},{8,32},{16,40},{24,48},{32,56},{40,0},{48,8},{56,16},{1,25}... | collective-permute-start | bytes 393224 | tf_op jit(solution)/shard_map/ppermute | solution.py:47
  107.4 2.4 %collective-permute-start.19 = (bf16[64,1024]{1,0:T(8,128)(2,1)S(1)}, bf16[64,1024]{1,0:T(8,128)(2,1)S(1)}, u32[]{:S(2)}, u32[]{:S(2)}) collective-permute-start(bf16[64,1024]{1,0:T(8,128)(2,1)S(1)} %get-tuple-element.39), channel_id=1, source_target_pairs={{0,32},{8,40},{16,48},{24,56},{32,0},{40,8},{48,16},{56,24},{1,33}... | collective-permute-start | bytes 393224 | tf_op jit(solution)/shard_map/ppermute | solution.py:47
  109.8 1.4 %collective-permute-start.20 = (bf16[64,1024]{1,0:T(8,128)(2,1)S(1)}, bf16[64,1024]{1,0:T(8,128)(2,1)S(1)}, u32[]{:S(2)}, u32[]{:S(2)}) collective-permute-start(bf16[64,1024]{1,0:T(8,128)(2,1)S(1)} %get-tuple-element.40), channel_id=1, source_target_pairs={{0,40},{8,48},{16,56},{24,0},{32,8},{40,16},{48,24},{56,32},{1,41}... | collective-permute-start | bytes 393224 | tf_op jit(solution)/shard_map/ppermute | solution.py:47
  111.3 2.1 %collective-permute-start.17 = (bf16[64,1024]{1,0:T(8,128)(2,1)}, bf16[64,1024]{1,0:T(8,128)(2,1)S(1)}, u32[]{:S(2)}, u32[]{:S(2)}) collective-permute-start(bf16[64,1024]{1,0:T(8,128)(2,1)} %get-tuple-element.37), channel_id=1, source_target_pairs={{0,16},{8,24},{16,32},{24,40},{32,48},{40,56},{48,0},{56,8},{1,17}... | collective-permute-start | bytes 393224 | tf_op jit(solution)/shard_map/ppermute | solution.py:47
  113.4 7.1 %collective-permute-start.21 = (bf16[64,1024]{1,0:T(8,128)(2,1)S(1)}, bf16[64,1024]{1,0:T(8,128)(2,1)S(1)}, u32[]{:S(2)}, u32[]{:S(2)}) collective-permute-start(bf16[64,1024]{1,0:T(8,128)(2,1)S(1)} %get-tuple-element.41), channel_id=1, source_target_pairs={{0,48},{8,56},{16,0},{24,8},{32,16},{40,24},{48,32},{56,40},{1,49}... | collective-permute-start | bytes 393224 | tf_op jit(solution)/shard_map/ppermute | solution.py:47
  120.5 3.3 %collective-permute-done.19.refs_4_.refs_0_ = bf16[64,1024]{1,0:T(8,128)(2,1)S(1)} collective-permute-done((bf16[64,1024]{1,0:T(8,128)(2,1)S(1)}, bf16[64,1024]{1,0:T(8,128)(2,1)S(1)}, u32[]{:S(2)}, u32[]{:S(2)}) %collective-permute-start.19) | collective-permute-done | bytes 131104 | tf_op jit(solution)/shard_map/ppermute | solution.py:47
  123.8 1.9 %sum.1 = (f32[256,128]{1,0:T(8,128)S(1)}, f32[256,128]{1,0:T(8,128)S(1)}) custom-call(s32[3]{0:T(128)S(1)} %copy-done.7, bf16[16,2,256,128]{3,2,1,0:T(8,128)(2,1)} %all-to-all-done.2.x_ref, bf16[64,1024]{1,0:T(8,128)(2,1)S(1)} %collective-permute-done.19.refs_4_.refs_0_, bf16[64,1024]{1,0:T(8,128)(2,1)S(1)} %collective-permute-done.18.refs_3_.refs_1_, ...), custom_call_target="tpu_custom_call" | custom-call | bytes 2097152 | tf_op jit(solution)/shard_map/sum/pallas_call | solution.py:403
  125.7 3.7 %collective-permute-start.23 = (f32[256,128]{1,0:T(8,128)S(1)}, f32[256,128]{1,0:T(8,128)S(1)}, u32[]{:S(2)}, u32[]{:S(2)}) collective-permute-start(f32[256,128]{1,0:T(8,128)S(1)} %get-tuple-element.45), channel_id=1, source_target_pairs={{0,128},{128,0},{1,129},{129,1},{2,130},{130,2},{3,131},{131,3},{4... | collective-permute-start | bytes 393224 | tf_op jit(solution)/shard_map/ppermute | solution.py:47
  129.4 1.6 %collective-permute-done.21.refs_6_ = bf16[64,1024]{1,0:T(8,128)(2,1)S(1)} collective-permute-done((bf16[64,1024]{1,0:T(8,128)(2,1)S(1)}, bf16[64,1024]{1,0:T(8,128)(2,1)S(1)}, u32[]{:S(2)}, u32[]{:S(2)}) %collective-permute-start.21) | collective-permute-done | bytes 131104 | tf_op jit(solution)/shard_map/ppermute | solution.py:47
  131.0 1.8 %collective-permute-done.22.refs_7_ = bf16[64,1024]{1,0:T(8,128)(2,1)S(1)} collective-permute-done((bf16[64,1024]{1,0:T(8,128)(2,1)S(1)}, bf16[64,1024]{1,0:T(8,128)(2,1)S(1)}, u32[]{:S(2)}, u32[]{:S(2)}) %collective-permute-start.22) | collective-permute-done | bytes 131104 | tf_op jit(solution)/shard_map/ppermute | solution.py:47
  132.9 1.6 %join.1 = bf16[64,8192]{1,0:T(8,128)(2,1)} custom-call(s32[3]{0:T(128)S(1)} %copy-done.7, bf16[64,1024]{1,0:T(8,128)(2,1)S(1)} %get-tuple-element.35.refs_0_, bf16[64,1024]{1,0:T(8,128)(2,1)S(1)} %collective-permute-done.16.refs_1_, bf16[64,1024]{1,0:T(8,128)(2,1)S(1)} %collective-permute-done.17.refs_2_, ...), custom_call_target="tpu_custom_call" | custom-call | bytes 2097152 | tf_op jit(solution)/shard_map/join/pallas_call | solution.py:393
  134.5 0.7 broadcast_select_fusion
  (41 shorter events, 1.8 us)
Async XLA Ops:
  0.6 1.2 copy-start.1
  3.4 38.3 %all-to-all-start = ((bf16[8,64,1024]{2,1,0:T(8,128)(2,1)}), bf16[8,64,1024]{2,1,0:T(8,128)(2,1)S(1)}, u32[]{:S(2)}, u32[]{:S(2)}) async-start(bf16[8,64,1024]{2,1,0:T(8,128)(2,1)} %deal.1), calls=%async_computation | async-start | bytes 2097152 | tf_op jit(solution)/shard_map/all_to_all | solution.py:289
  13.0 13.3 %copy-start.7 = (s32[3]{0:T(128)S(1)}, s32[3]{0:T(128)}, u32[]{:S(2)}) copy-start(s32[3]{0:T(128)} %pad_add_fusion.at_ref) | copy-start | bytes 40
  13.0 32.3 %copy-start.5 = (bf16[512,128]{1,0:T(8,128)(2,1)S(1)}, bf16[512,128]{1,0:T(8,128)(2,1)}, u32[]{:S(2)}) copy-start(bf16[512,128]{1,0:T(8,128)(2,1)} %key_ref.1) | copy-start | bytes 393220
  13.0 32.3 %copy-start.6 = (bf16[512,128]{1,0:T(8,128)(2,1)S(1)}, bf16[512,128]{1,0:T(8,128)(2,1)}, u32[]{:S(2)}) copy-start(bf16[512,128]{1,0:T(8,128)(2,1)} %value_ref.1) | copy-start | bytes 393220
  24.0 2.2 %collective-permute-start = (bf16[512,128]{1,0:T(8,128)(2,1)}, bf16[512,128]{1,0:T(8,128)(2,1)S(1)}, u32[]{:S(2)}, u32[]{:S(2)}) collective-permute-start(bf16[512,128]{1,0:T(8,128)(2,1)} %get-tuple-element.28), channel_id=1, source_target_pairs={{0,128},{128,0},{1,129},{129,1},{2,130},{130,2},{3,131},{131,3},{4... | collective-permute-start | bytes 393224 | tf_op jit(solution)/shard_map/ppermute | solution.py:47
  26.3 0.9 copy-start.4
  27.7 3.9 %collective-permute-start.1 = (bf16[256,128]{1,0:T(8,128)(2,1)S(1)}, bf16[256,128]{1,0:T(8,128)(2,1)S(1)}, u32[]{:S(2)}, u32[]{:S(2)}) collective-permute-start(bf16[256,128]{1,0:T(8,128)(2,1)S(1)} %get-tuple-element.30), channel_id=1, source_target_pairs={{0,2},{1,3},{2,0},{3,1},{4,6},{5,7},{6,4},{7,5},{8,10},{9,11},{10,... | collective-permute-start | bytes 196616 | tf_op jit(solution)/shard_map/ppermute | solution.py:304
  29.0 5.6 %collective-permute-start.2 = (bf16[256,128]{1,0:T(8,128)(2,1)S(1)}, bf16[256,128]{1,0:T(8,128)(2,1)S(1)}, u32[]{:S(2)}, u32[]{:S(2)}) collective-permute-start(bf16[256,128]{1,0:T(8,128)(2,1)S(1)} %get-tuple-element.31), channel_id=1, source_target_pairs={{0,4},{1,5},{2,6},{3,7},{4,0},{5,1},{6,2},{7,3},{8,12},{9,13},{10,... | collective-permute-start | bytes 196616 | tf_op jit(solution)/shard_map/ppermute | solution.py:304
  31.5 4.8 %collective-permute-start.3 = (bf16[256,128]{1,0:T(8,128)(2,1)S(1)}, bf16[256,128]{1,0:T(8,128)(2,1)S(1)}, u32[]{:S(2)}, u32[]{:S(2)}) collective-permute-start(bf16[256,128]{1,0:T(8,128)(2,1)S(1)} %get-tuple-element.32), channel_id=1, source_target_pairs={{0,6},{1,7},{2,4},{3,5},{4,2},{5,3},{6,0},{7,1},{8,14},{9,15},{10,... | collective-permute-start | bytes 196616 | tf_op jit(solution)/shard_map/ppermute | solution.py:304
  36.3 5.4 %collective-permute-start.4 = (bf16[4,128,128]{2,1,0:T(8,128)(2,1)S(1)}, bf16[4,128,128]{2,1,0:T(8,128)(2,1)S(1)}, u32[]{:S(2)}, u32[]{:S(2)}) collective-permute-start(bf16[4,128,128]{2,1,0:T(8,128)(2,1)S(1)} %middle.1), channel_id=1, source_target_pairs={{0,1},{1,0},{2,3},{3,2},{4,5},{5,4},{6,7},{7,6},{8,9},{9,8},{10,11... | collective-permute-start | bytes 393224 | tf_op jit(solution)/shard_map/ppermute | solution.py:304
  42.3 10.6 %collective-permute-start.5 = (bf16[128,1024]{1,0:T(8,128)(2,1)S(1)}, bf16[128,1024]{1,0:T(8,128)(2,1)}, u32[]{:S(2)}, u32[]{:S(2)}) collective-permute-start(bf16[128,1024]{1,0:T(8,128)(2,1)S(1)} %place.1.refs_0_._), channel_id=1, source_target_pairs={{0,56},{8,0},{16,8},{24,16},{32,24},{40,32},{48,40},{56,48},{1,57}... | collective-permute-start | bytes 786440 | tf_op jit(solution)/shard_map/ppermute | solution.py:47
  45.3 10.2 %collective-permute-start.7 = (bf16[128,1024]{1,0:T(8,128)(2,1)S(1)}, bf16[128,1024]{1,0:T(8,128)(2,1)}, u32[]{:S(2)}, u32[]{:S(2)}) collective-permute-start(bf16[128,1024]{1,0:T(8,128)(2,1)S(1)} %place.1.refs_0_._), channel_id=1, source_target_pairs={{0,8},{8,16},{16,24},{24,32},{32,40},{40,48},{48,56},{56,0},{1,9},... | collective-permute-start | bytes 786440 | tf_op jit(solution)/shard_map/ppermute | solution.py:47
  47.6 40.2 %all-to-all-start.1 = ((bf16[16,512,128]{2,1,0:T(8,128)(2,1)}), bf16[16,512,128]{2,1,0:T(8,128)(2,1)S(1)}, u32[]{:S(2)}, u32[]{:S(2)}) async-start(bf16[16,512,128]{2,1,0:T(8,128)(2,1)} %broadcast_in_dim.2), calls=%async_computation.1 | async-start | bytes 4194304 | tf_op jit(solution)/shard_map/all_to_all | solution.py:342
  52.8 14.7 %copy-start.8 = (f32[2,2,256,128]{3,2,1,0:T(8,128)S(1)}, f32[2,2,256,128]{3,2,1,0:T(8,128)}, u32[]{:S(2)}) copy-start(f32[2,2,256,128]{3,2,1,0:T(8,128)} %param.17) | copy-start | bytes 1572868
  52.9 6.3 %collective-permute-start.6 = (bf16[128,1024]{1,0:T(8,128)(2,1)}, bf16[128,1024]{1,0:T(8,128)(2,1)S(1)}, u32[]{:S(2)}, u32[]{:S(2)}) collective-permute-start(bf16[128,1024]{1,0:T(8,128)(2,1)} %collective-permute-done.5.refs_1_), channel_id=1, source_target_pairs={{0,56},{8,0},{16,8},{24,16},{32,24},{40,32},{48,40},{56,48},{1,57}... | collective-permute-start | bytes 786440 | tf_op jit(solution)/shard_map/ppermute | solution.py:47
  55.5 6.9 %collective-permute-start.8 = (bf16[128,1024]{1,0:T(8,128)(2,1)}, bf16[128,1024]{1,0:T(8,128)(2,1)S(1)}, u32[]{:S(2)}, u32[]{:S(2)}) collective-permute-start(bf16[128,1024]{1,0:T(8,128)(2,1)} %collective-permute-done.7.refs_6_), channel_id=1, source_target_pairs={{0,8},{8,16},{16,24},{24,32},{32,40},{40,48},{48,56},{56,0},{1,9},... | collective-permute-start | bytes 786440 | tf_op jit(solution)/shard_map/ppermute | solution.py:47
  63.3 18.8 %collective-permute-start.9 = (bf16[1024,512]{1,0:T(8,128)(2,1)S(1)}, bf16[1024,512]{1,0:T(8,128)(2,1)S(1)}, u32[]{:S(2)}, u32[]{:S(2)}) collective-permute-start(bf16[1024,512]{1,0:T(8,128)(2,1)S(1)} %turn.1.h_own), channel_id=1, source_target_pairs={{0,128},{128,0},{1,129},{129,1},{2,130},{130,2},{3,131},{131,3},{4... | collective-permute-start | bytes 3145736 | tf_op jit(solution)/shard_map/ppermute | solution.py:47
  67.5 12.1 %collective-permute-start.14 = (f32[2,2,256,128]{3,2,1,0:T(8,128)S(1)}, f32[2,2,256,128]{3,2,1,0:T(8,128)S(1)}, u32[]{:S(2)}, u32[]{:S(2)}) collective-permute-start(f32[2,2,256,128]{3,2,1,0:T(8,128)S(1)} %copy-done.8), channel_id=1, source_target_pairs={{0,128},{128,0},{1,129},{129,1},{2,130},{130,2},{3,131},{131,3},{4... | collective-permute-start | bytes 1572872 | tf_op jit(solution)/shard_map/ppermute | solution.py:47
  67.8 8.9 %collective-permute-start.11 = (bf16[128,1024]{1,0:T(8,128)(2,1)S(1)}, bf16[128,1024]{1,0:T(8,128)(2,1)S(1)}, u32[]{:S(2)}, u32[]{:S(2)}) collective-permute-start(bf16[128,1024]{1,0:T(8,128)(2,1)S(1)} %collective-permute-done.8.__.refs_5_), channel_id=1, source_target_pairs={{0,8},{8,16},{16,24},{24,32},{32,40},{40,48},{48,56},{56,0},{1,9},... | collective-permute-start | bytes 786440 | tf_op jit(solution)/shard_map/ppermute | solution.py:47
  67.8 9.0 %collective-permute-start.10 = (bf16[128,1024]{1,0:T(8,128)(2,1)S(1)}, bf16[128,1024]{1,0:T(8,128)(2,1)S(1)}, u32[]{:S(2)}, u32[]{:S(2)}) collective-permute-start(bf16[128,1024]{1,0:T(8,128)(2,1)S(1)} %collective-permute-done.6._.refs_2_), channel_id=1, source_target_pairs={{0,56},{8,0},{16,8},{24,16},{32,24},{40,32},{48,40},{56,48},{1,57}... | collective-permute-start | bytes 786440 | tf_op jit(solution)/shard_map/ppermute | solution.py:47
  76.7 5.4 %collective-permute-start.12 = (bf16[64,1024]{1,0:T(8,128)(2,1)S(1)}, bf16[64,1024]{1,0:T(8,128)(2,1)S(1)}, u32[]{:S(2)}, u32[]{:S(2)}) collective-permute-start(bf16[64,1024]{1,0:T(8,128)(2,1)S(1)} %slice.8), channel_id=1, source_target_pairs={{0,8},{8,16},{16,24},{24,32},{32,40},{40,48},{48,56},{56,0},{1,9},... | collective-permute-start | bytes 393224 | tf_op jit(solution)/shard_map/ppermute | solution.py:47
  76.8 5.3 %collective-permute-start.13 = (bf16[64,1024]{1,0:T(8,128)(2,1)S(1)}, bf16[64,1024]{1,0:T(8,128)(2,1)S(1)}, u32[]{:S(2)}, u32[]{:S(2)}) collective-permute-start(bf16[64,1024]{1,0:T(8,128)(2,1)S(1)} %slice.9), channel_id=1, source_target_pairs={{0,56},{8,0},{16,8},{24,16},{32,24},{40,32},{48,40},{56,48},{1,57}... | collective-permute-start | bytes 393224 | tf_op jit(solution)/shard_map/ppermute | solution.py:47
  85.6 1.3 copy-start
  86.9 1.0 copy-start.2
  87.9 36.0 %all-to-all-start.2 = ((bf16[16,2,256,128]{3,2,1,0:T(8,128)(2,1)}), bf16[16,2,256,128]{3,2,1,0:T(8,128)(2,1)}, u32[]{:S(2)}, u32[]{:S(2)}) async-start(bf16[16,2,256,128]{3,2,1,0:T(8,128)(2,1)} %bitcast.4), calls=%async_computation.2 | async-start | bytes 4194304 | tf_op jit(solution)/shard_map/all_to_all | solution.py:378
  94.7 1.2 copy-start.3
  97.2 4.7 %collective-permute-start.15 = (bf16[512,1024]{1,0:T(8,128)(2,1)S(1)}, bf16[512,1024]{1,0:T(8,128)(2,1)S(1)}, u32[]{:S(2)}, u32[]{:S(2)}) collective-permute-start(bf16[512,1024]{1,0:T(8,128)(2,1)S(1)} %term.1), channel_id=1, source_target_pairs={{0,128},{128,0},{1,129},{129,1},{2,130},{130,2},{3,131},{131,3},{4... | collective-permute-start | bytes 3145736 | tf_op jit(solution)/shard_map/ppermute | solution.py:47
  103.8 9.6 %collective-permute-start.18 = (bf16[64,1024]{1,0:T(8,128)(2,1)S(1)}, bf16[64,1024]{1,0:T(8,128)(2,1)S(1)}, u32[]{:S(2)}, u32[]{:S(2)}) collective-permute-start(bf16[64,1024]{1,0:T(8,128)(2,1)S(1)} %get-tuple-element.38), channel_id=1, source_target_pairs={{0,24},{8,32},{16,40},{24,48},{32,56},{40,0},{48,8},{56,16},{1,25}... | collective-permute-start | bytes 393224 | tf_op jit(solution)/shard_map/ppermute | solution.py:47
  107.4 16.4 %collective-permute-start.19 = (bf16[64,1024]{1,0:T(8,128)(2,1)S(1)}, bf16[64,1024]{1,0:T(8,128)(2,1)S(1)}, u32[]{:S(2)}, u32[]{:S(2)}) collective-permute-start(bf16[64,1024]{1,0:T(8,128)(2,1)S(1)} %get-tuple-element.39), channel_id=1, source_target_pairs={{0,32},{8,40},{16,48},{24,56},{32,0},{40,8},{48,16},{56,24},{1,33}... | collective-permute-start | bytes 393224 | tf_op jit(solution)/shard_map/ppermute | solution.py:47
  109.8 14.0 %collective-permute-start.20 = (bf16[64,1024]{1,0:T(8,128)(2,1)S(1)}, bf16[64,1024]{1,0:T(8,128)(2,1)S(1)}, u32[]{:S(2)}, u32[]{:S(2)}) collective-permute-start(bf16[64,1024]{1,0:T(8,128)(2,1)S(1)} %get-tuple-element.40), channel_id=1, source_target_pairs={{0,40},{8,48},{16,56},{24,0},{32,8},{40,16},{48,24},{56,32},{1,41}... | collective-permute-start | bytes 393224 | tf_op jit(solution)/shard_map/ppermute | solution.py:47
  111.3 18.2 %collective-permute-start.16 = (bf16[64,1024]{1,0:T(8,128)(2,1)}, bf16[64,1024]{1,0:T(8,128)(2,1)S(1)}, u32[]{:S(2)}, u32[]{:S(2)}) collective-permute-start(bf16[64,1024]{1,0:T(8,128)(2,1)} %get-tuple-element.36), channel_id=1, source_target_pairs={{0,8},{8,16},{16,24},{24,32},{32,40},{40,48},{48,56},{56,0},{1,9},... | collective-permute-start | bytes 393224 | tf_op jit(solution)/shard_map/ppermute | solution.py:47
  111.3 18.2 %collective-permute-start.17 = (bf16[64,1024]{1,0:T(8,128)(2,1)}, bf16[64,1024]{1,0:T(8,128)(2,1)S(1)}, u32[]{:S(2)}, u32[]{:S(2)}) collective-permute-start(bf16[64,1024]{1,0:T(8,128)(2,1)} %get-tuple-element.37), channel_id=1, source_target_pairs={{0,16},{8,24},{16,32},{24,40},{32,48},{40,56},{48,0},{56,8},{1,17}... | collective-permute-start | bytes 393224 | tf_op jit(solution)/shard_map/ppermute | solution.py:47
  113.4 17.6 %collective-permute-start.21 = (bf16[64,1024]{1,0:T(8,128)(2,1)S(1)}, bf16[64,1024]{1,0:T(8,128)(2,1)S(1)}, u32[]{:S(2)}, u32[]{:S(2)}) collective-permute-start(bf16[64,1024]{1,0:T(8,128)(2,1)S(1)} %get-tuple-element.41), channel_id=1, source_target_pairs={{0,48},{8,56},{16,0},{24,8},{32,16},{40,24},{48,32},{56,40},{1,49}... | collective-permute-start | bytes 393224 | tf_op jit(solution)/shard_map/ppermute | solution.py:47
  123.8 9.0 %collective-permute-start.22 = (bf16[64,1024]{1,0:T(8,128)(2,1)S(1)}, bf16[64,1024]{1,0:T(8,128)(2,1)S(1)}, u32[]{:S(2)}, u32[]{:S(2)}) collective-permute-start(bf16[64,1024]{1,0:T(8,128)(2,1)S(1)} %get-tuple-element.42), channel_id=1, source_target_pairs={{0,56},{8,0},{16,8},{24,16},{32,24},{40,32},{48,40},{56,48},{1,57}... | collective-permute-start | bytes 393224 | tf_op jit(solution)/shard_map/ppermute | solution.py:47
  125.7 8.7 %collective-permute-start.23 = (f32[256,128]{1,0:T(8,128)S(1)}, f32[256,128]{1,0:T(8,128)S(1)}, u32[]{:S(2)}, u32[]{:S(2)}) collective-permute-start(f32[256,128]{1,0:T(8,128)S(1)} %get-tuple-element.45), channel_id=1, source_target_pairs={{0,128},{128,0},{1,129},{129,1},{2,130},{130,2},{3,131},{131,3},{4... | collective-permute-start | bytes 393224 | tf_op jit(solution)/shard_map/ppermute | solution.py:47

commit v3 on v2

--- a/solution.py
+++ b/solution.py
@@ -55,7 +55,7 @@
     return [jnp.asarray(t.astype(np.float32)) for t in wide]
 
 
-def attention_kernel(at_ref, q_ref, k_ref, v_ref, g_ref, c_ref, s_ref, qg_ref, own_ref, other_ref, kt, dk, dv):
+def attention_kernel(q_ref, k_ref, v_ref, g_ref, c_ref, s_ref, qg_ref, own_ref, other_ref, kt, dk, dv):
     step = pl.program_id(0)
 
     @pl.when(step == 0)
@@ -95,24 +95,26 @@
         key_grad = (rotated * c_ref[...] + turned * s_ref[...]).astype(BF)
         value_grad = dv[...].astype(BF)
 
-        @pl.when(at_ref[0] == 0)
+        rep = lax.axis_index("rep")
+
+        @pl.when(rep == 0)
         def _():
             own_ref[...] = key_grad
             other_ref[...] = value_grad
 
-        @pl.when(at_ref[0] != 0)
+        @pl.when(rep != 0)
         def _():
             own_ref[...] = value_grad
             other_ref[...] = key_grad
 
 
-def attention_grads(where_at, queries, keys, values, out_grad):
+def attention_grads(queries, keys, values, out_grad):
     whole = pl.BlockSpec((LEN, HD), lambda h: (0, 0))
     head = pl.BlockSpec((LEN, STEP_HEADS * HD), lambda h: (0, h))
     return pl.pallas_call(
         attention_kernel,
         grid=(GROUP // STEP_HEADS,),
-        in_specs=[SMEM, head, whole, whole, head, whole, whole],
+        in_specs=[head, whole, whole, head, whole, whole],
         out_specs=[head, whole, whole],
         out_shape=[struct(LEN, GROUP * HD), struct(LEN, HD), struct(LEN, HD)],
         scratch_shapes=[
@@ -123,7 +125,7 @@
         compiler_params=params(60),
         cost_estimate=cost(12 * 10**9, 4 * 2**20),
         name="attention_grads",
-    )(where_at, queries, keys, values, out_grad, *rope_wide())
+    )(queries, keys, values, out_grad, *rope_wide())
 
 
 def deal_kernel(x_ref, out_ref):
@@ -278,17 +280,17 @@
 
     hidden = pl.pallas_call(
         deal_kernel,
-        grid=(4,),
-        in_specs=[pl.BlockSpec((rows // 4, width), lambda i: (i, 0))],
-        out_specs=pl.BlockSpec((Z, rows // 4, REP * YLO * out_rows), lambda i: (0, i, 0)),
+        grid=(2,),
+        in_specs=[pl.BlockSpec((rows // 2, width), lambda i: (i, 0))],
+        out_specs=pl.BlockSpec((Z, rows // 2, REP * YLO * out_rows), lambda i: (0, i, 0)),
         out_shape=struct(Z, rows, REP * YLO * out_rows),
-        compiler_params=params(16),
+        compiler_params=params(60),
         cost_estimate=cost(0, 2 * 2**20),
         name="deal",
     )(hidden_in)
     hidden = lax.all_to_all(hidden, "z", split_axis=0, concat_axis=0, tiled=True)
 
-    query_grad, own, other = attention_grads(where_at, queries, keys, values, out_grad)
+    query_grad, own, other = attention_grads(queries, keys, values, out_grad)
     other = shift(other, "rep", REP, 1)
     pieces = pl.pallas_call(
         split_kernel,

time: 136 us -> 134 us (0.985)
  starting transfers between devices: 67.4 us -> 63.8 us
  waiting for transfers between devices: 33 us -> 36.3 us
    ppermute x20, starting transfers between devices: 39.4 us -> 35.4 us  [shift(): lax.ppermute(block, axis, [(i, (i + by) % count) for i in range(count)])]
    ppermute x20, waiting for transfers between devices: 26 us -> 28.8 us  [shift(): lax.ppermute(block, axis, [(i, (i + by) % count) for i in range(count)])]
    unnamed x18 -> x14, local copies, waits for them, and re-layouts: 5.64 us -> 4.43 us
  transfers between devices with their start and end apart: 27 -> 27, of which waited for: 12 -> 13; matrix products, arithmetic and copies ran while one was open for 2% -> 1% of each run, Pallas kernels for 17% -> 17%
where the time goes in v3:
time: 134 us
  starting transfers between devices  63.8 us (48%)
  waiting for transfers between devices  36.3 us (27%)
  Pallas kernels  25.8 us (19%)
  local copies, waits for them, and re-layouts  6.22 us (5%)
    ppermute x20, starting transfers between devices, shift(): lax.ppermute(block, axis, [(i, (i + by) % count) for i in range(count)])  35.4 us
    ppermute x20, waiting for transfers between devices, shift(): lax.ppermute(block, axis, [(i, (i + by) % count) for i in range(count)])  28.8 us
    pallas_call x1, Pallas kernels, attention_grads(): pl.pallas_call(attention_kernel, grid=(GROUP // STEP_HEADS,), in_specs=[h...  11.1 us
    all_to_all x1, starting transfers between devices, on_device(): lax.all_to_all(hidden, 'z', split_axis=0, concat_axis=0, tiled=True)  9.01 us
    ppermute x4, waiting for transfers between devices, across(): return lax.ppermute(block, 'tensor', [(i, i ^ mask) for i in range(TEN)])  6.96 us
    ppermute x4, starting transfers between devices, across(): return lax.ppermute(block, 'tensor', [(i, i ^ mask) for i in range(TEN)])  6.95 us
    all_to_all x1, starting transfers between devices, on_device(): lax.all_to_all(partial, PLANE, split_axis=0, concat_axis=0, tiled=True)  6.69 us
    all_to_all x1, starting transfers between devices, on_device(): lax.all_to_all(weight, PLANE, split_axis=0, concat_axis=0, tiled=True)  5.81 us
  transfers between devices with their start and end apart: 27, of which 13 were waited for; matrix products, arithmetic and copies ran while one was open for 1% of the time, Pallas kernels for 17%

profile of v3, /device:TPU:1, one launch (start us, length us, event | category | flops | bytes accessed | tf_op | source)
XLA Modules:
  0.0 133.8 jit_solution(5910607839064757924)
XLA Ops:
  0.6 2.1 %deal.1 = bf16[8,64,1024]{2,1,0:T(8,128)(2,1)} custom-call(bf16[64,8192]{1,0:T(8,128)(2,1)} %x_ref.1), custom_call_target="tpu_custom_call" | custom-call | bytes 2097152 | tf_op jit(solution)/shard_map/deal/pallas_call | solution.py:281
  2.7 9.0 %all-to-all-start = ((bf16[8,64,1024]{2,1,0:T(8,128)(2,1)}), bf16[8,64,1024]{2,1,0:T(8,128)(2,1)S(1)}, u32[]{:S(2)}, u32[]{:S(2)}) async-start(bf16[8,64,1024]{2,1,0:T(8,128)(2,1)} %deal.1), calls=%async_computation | async-start | bytes 2097152 | tf_op jit(solution)/shard_map/all_to_all | solution.py:291
  11.7 11.1 %attention_grads.1 = (bf16[512,1024]{1,0:T(8,128)(2,1)}, bf16[512,128]{1,0:T(8,128)(2,1)}, bf16[512,128]{1,0:T(8,128)(2,1)}) custom-call(bf16[512,1024]{1,0:T(8,128)(2,1)} %q_ref.1, bf16[512,128]{1,0:T(8,128)(2,1)} %k_ref.1, bf16[512,128]{1,0:T(8,128)(2,1)} %v_ref.1, bf16[512,1024]{1,0:T(8,128)(2,1)} %g_ref.1, f32[512,128]{1,0:T(8,128)} %constant.18.clone.c_ref, ...), custom_call_target="tpu_custom_call" | custom-call | flops 12000000000 | bytes 4194304 | tf_op jit(solution)/shard_map/attention_grads/pallas_call | solution.py:114
  22.8 1.0 collective-permute-start
  23.9 1.1 collective-permute-done.other_ref
  25.0 0.9 copy-done.3
  25.9 0.6 split.1
  26.5 1.3 collective-permute-start.1
  27.8 2.5 %collective-permute-start.2 = (bf16[256,128]{1,0:T(8,128)(2,1)S(1)}, bf16[256,128]{1,0:T(8,128)(2,1)S(1)}, u32[]{:S(2)}, u32[]{:S(2)}) collective-permute-start(bf16[256,128]{1,0:T(8,128)(2,1)S(1)} %get-tuple-element.31), channel_id=1, source_target_pairs={{0,4},{1,5},{2,6},{3,7},{4,0},{5,1},{6,2},{7,3},{8,12},{9,13},{10,... | collective-permute-start | bytes 196616 | tf_op jit(solution)/shard_map/ppermute | solution.py:306
  30.4 2.9 %collective-permute-done.2.refs_2_ = bf16[256,128]{1,0:T(8,128)(2,1)S(1)} collective-permute-done((bf16[256,128]{1,0:T(8,128)(2,1)S(1)}, bf16[256,128]{1,0:T(8,128)(2,1)S(1)}, u32[]{:S(2)}, u32[]{:S(2)}) %collective-permute-start.2) | collective-permute-done | bytes 65568 | tf_op jit(solution)/shard_map/ppermute | solution.py:306
  33.3 1.4 %collective-permute-done.3.refs_3_ = bf16[256,128]{1,0:T(8,128)(2,1)S(1)} collective-permute-done((bf16[256,128]{1,0:T(8,128)(2,1)S(1)}, bf16[256,128]{1,0:T(8,128)(2,1)S(1)}, u32[]{:S(2)}, u32[]{:S(2)}) %collective-permute-start.3) | collective-permute-done | bytes 65568 | tf_op jit(solution)/shard_map/ppermute | solution.py:306
  34.7 3.0 %collective-permute-start.4 = (bf16[4,128,128]{2,1,0:T(8,128)(2,1)S(1)}, bf16[4,128,128]{2,1,0:T(8,128)(2,1)S(1)}, u32[]{:S(2)}, u32[]{:S(2)}) collective-permute-start(bf16[4,128,128]{2,1,0:T(8,128)(2,1)S(1)} %middle.1), channel_id=1, source_target_pairs={{0,1},{1,0},{2,3},{3,2},{4,5},{5,4},{6,7},{7,6},{8,9},{9,8},{10,11... | collective-permute-start | bytes 393224 | tf_op jit(solution)/shard_map/ppermute | solution.py:306
  37.7 2.7 %collective-permute-done.4.refs_4_ = bf16[4,128,128]{2,1,0:T(8,128)(2,1)S(1)} collective-permute-done((bf16[4,128,128]{2,1,0:T(8,128)(2,1)S(1)}, bf16[4,128,128]{2,1,0:T(8,128)(2,1)S(1)}, u32[]{:S(2)}, u32[]{:S(2)}) %collective-permute-start.4) | collective-permute-done | bytes 131104 | tf_op jit(solution)/shard_map/ppermute | solution.py:306
  40.9 0.6 place.1.refs_0_._
  41.5 2.5 %collective-permute-start.5 = (bf16[128,1024]{1,0:T(8,128)(2,1)S(1)}, bf16[128,1024]{1,0:T(8,128)(2,1)}, u32[]{:S(2)}, u32[]{:S(2)}) collective-permute-start(bf16[128,1024]{1,0:T(8,128)(2,1)S(1)} %place.1.refs_0_._), channel_id=1, source_target_pairs={{0,56},{8,0},{16,8},{24,16},{32,24},{40,32},{48,40},{56,48},{1,57}... | collective-permute-start | bytes 786440 | tf_op jit(solution)/shard_map/ppermute | solution.py:47
  44.0 0.6 select.1
  44.6 1.8 %broadcast_in_dim.2 = bf16[16,512,128]{2,1,0:T(8,128)(2,1)} broadcast(bf16[512,128]{1,0:T(8,128)(2,1)S(1)} %select.1), dimensions={1,2} | broadcast | bytes 2228224 | tf_op jit(solution)/shard_map/broadcast_in_dim | solution.py:343
  46.3 5.8 %all-to-all-start.1 = ((bf16[16,512,128]{2,1,0:T(8,128)(2,1)}), bf16[16,512,128]{2,1,0:T(8,128)(2,1)S(1)}, u32[]{:S(2)}, u32[]{:S(2)}) async-start(bf16[16,512,128]{2,1,0:T(8,128)(2,1)} %broadcast_in_dim.2), calls=%async_computation.1 | async-start | bytes 4194304 | tf_op jit(solution)/shard_map/all_to_all | solution.py:344
  52.2 2.0 %collective-permute-start.6 = (bf16[128,1024]{1,0:T(8,128)(2,1)}, bf16[128,1024]{1,0:T(8,128)(2,1)S(1)}, u32[]{:S(2)}, u32[]{:S(2)}) collective-permute-start(bf16[128,1024]{1,0:T(8,128)(2,1)} %collective-permute-done.5.refs_1_), channel_id=1, source_target_pairs={{0,56},{8,0},{16,8},{24,16},{32,24},{40,32},{48,40},{56,48},{1,57}... | collective-permute-start | bytes 786440 | tf_op jit(solution)/shard_map/ppermute | solution.py:47
  54.2 4.1 %collective-permute-done.6._.refs_2_ = bf16[128,1024]{1,0:T(8,128)(2,1)S(1)} collective-permute-done((bf16[128,1024]{1,0:T(8,128)(2,1)}, bf16[128,1024]{1,0:T(8,128)(2,1)S(1)}, u32[]{:S(2)}, u32[]{:S(2)}) %collective-permute-start.6) | collective-permute-done | bytes 262176 | tf_op jit(solution)/shard_map/ppermute | solution.py:47
  58.3 2.8 %collective-permute-done.8.__.refs_5_ = bf16[128,1024]{1,0:T(8,128)(2,1)S(1)} collective-permute-done((bf16[128,1024]{1,0:T(8,128)(2,1)}, bf16[128,1024]{1,0:T(8,128)(2,1)S(1)}, u32[]{:S(2)}, u32[]{:S(2)}) %collective-permute-start.8) | collective-permute-done | bytes 262176 | tf_op jit(solution)/shard_map/ppermute | solution.py:47
  61.1 0.9 turn.1.h_own
  62.0 4.2 %collective-permute-start.9 = (bf16[1024,512]{1,0:T(8,128)(2,1)S(1)}, bf16[1024,512]{1,0:T(8,128)(2,1)S(1)}, u32[]{:S(2)}, u32[]{:S(2)}) collective-permute-start(bf16[1024,512]{1,0:T(8,128)(2,1)S(1)} %turn.1.h_own), channel_id=1, source_target_pairs={{0,128},{128,0},{1,129},{129,1},{2,130},{130,2},{3,131},{131,3},{4... | collective-permute-start | bytes 3145736 | tf_op jit(solution)/shard_map/ppermute | solution.py:47
  66.5 2.7 %collective-permute-start.10 = (bf16[128,1024]{1,0:T(8,128)(2,1)S(1)}, bf16[128,1024]{1,0:T(8,128)(2,1)S(1)}, u32[]{:S(2)}, u32[]{:S(2)}) collective-permute-start(bf16[128,1024]{1,0:T(8,128)(2,1)S(1)} %collective-permute-done.6._.refs_2_), channel_id=1, source_target_pairs={{0,56},{8,0},{16,8},{24,16},{32,24},{40,32},{48,40},{56,48},{1,57}... | collective-permute-start | bytes 786440 | tf_op jit(solution)/shard_map/ppermute | solution.py:47
  69.2 6.2 %collective-permute-done.11.refs_4_ = bf16[128,1024]{1,0:T(8,128)(2,1)S(1)} collective-permute-done((bf16[128,1024]{1,0:T(8,128)(2,1)S(1)}, bf16[128,1024]{1,0:T(8,128)(2,1)S(1)}, u32[]{:S(2)}, u32[]{:S(2)}) %collective-permute-start.11) | collective-permute-done | bytes 262176 | tf_op jit(solution)/shard_map/ppermute | solution.py:47
  75.5 2.7 %collective-permute-start.13 = (bf16[64,1024]{1,0:T(8,128)(2,1)S(1)}, bf16[64,1024]{1,0:T(8,128)(2,1)S(1)}, u32[]{:S(2)}, u32[]{:S(2)}) collective-permute-start(bf16[64,1024]{1,0:T(8,128)(2,1)S(1)} %slice.9), channel_id=1, source_target_pairs={{0,56},{8,0},{16,8},{24,16},{32,24},{40,32},{48,40},{56,48},{1,57}... | collective-permute-start | bytes 393224 | tf_op jit(solution)/shard_map/ppermute | solution.py:47
  78.2 2.5 %collective-permute-done.12.refs_7_ = bf16[64,1024]{1,0:T(8,128)(2,1)S(1)} collective-permute-done((bf16[64,1024]{1,0:T(8,128)(2,1)S(1)}, bf16[64,1024]{1,0:T(8,128)(2,1)S(1)}, u32[]{:S(2)}, u32[]{:S(2)}) %collective-permute-start.12) | collective-permute-done | bytes 131104 | tf_op jit(solution)/shard_map/ppermute | solution.py:47
  80.8 3.5 %weight_grad.1 = (bf16[2,8,2,256,128]{4,3,2,1,0:T(8,128)(2,1)S(1)}, bf16[512,1024]{1,0:T(8,128)(2,1)S(1)}, bf16[512,1024]{1,0:T(8,128)(2,1)S(1)}, f32[2,2,256,128]{3,2,1,0:T(8,128)}) custom-call(bf16[1024,512]{1,0:T(8,128)(2,1)S(1)} %turn.1.h_own, bf16[1024,512]{1,0:T(8,128)(2,1)S(1)} %collective-permute-done.9.h_other, ...), custom_call_target="tpu_custom_call" | custom-call | flops 4294967296 | bytes 8388608 | tf_op jit(solution)/shard_map/weight_grad/pallas_call | solution.py:359
  84.3 1.3 copy-done
  85.6 1.0 copy-done.1
  86.6 6.7 %all-to-all-start.2 = ((bf16[16,2,256,128]{3,2,1,0:T(8,128)(2,1)}), bf16[16,2,256,128]{3,2,1,0:T(8,128)(2,1)}, u32[]{:S(2)}, u32[]{:S(2)}) async-start(bf16[16,2,256,128]{3,2,1,0:T(8,128)(2,1)} %bitcast.4), calls=%async_computation.2 | async-start | bytes 4194304 | tf_op jit(solution)/shard_map/all_to_all | solution.py:380
  93.3 1.2 copy-done.2
  94.5 1.3 term.1
  95.8 2.5 %collective-permute-start.15 = (bf16[512,1024]{1,0:T(8,128)(2,1)S(1)}, bf16[512,1024]{1,0:T(8,128)(2,1)S(1)}, u32[]{:S(2)}, u32[]{:S(2)}) collective-permute-start(bf16[512,1024]{1,0:T(8,128)(2,1)S(1)} %term.1), channel_id=1, source_target_pairs={{0,128},{128,0},{1,129},{129,1},{2,130},{130,2},{3,131},{131,3},{4... | collective-permute-start | bytes 3145736 | tf_op jit(solution)/shard_map/ppermute | solution.py:47
  98.3 2.3 %collective-permute-done.15.given_ref = bf16[512,1024]{1,0:T(8,128)(2,1)S(1)} collective-permute-done((bf16[512,1024]{1,0:T(8,128)(2,1)S(1)}, bf16[512,1024]{1,0:T(8,128)(2,1)S(1)}, u32[]{:S(2)}, u32[]{:S(2)}) %collective-permute-start.15) | collective-permute-done | bytes 1048608 | tf_op jit(solution)/shard_map/ppermute | solution.py:47
  100.6 1.9 %add.5 = (bf16[64,1024]{1,0:T(8,128)(2,1)S(1)}, bf16[64,1024]{1,0:T(8,128)(2,1)}, bf16[64,1024]{1,0:T(8,128)(2,1)}, bf16[64,1024]{1,0:T(8,128)(2,1)S(1)}, bf16[6...) custom-call(bf16[512,1024]{1,0:T(8,128)(2,1)S(1)} %get-tuple-element, ...), custom_call_target="tpu_custom_call" | custom-call | flops 1073741824 | bytes 5242880 | tf_op jit(solution)/shard_map/add/pallas_call | solution.py:382
  102.5 3.6 %collective-permute-start.18 = (bf16[64,1024]{1,0:T(8,128)(2,1)S(1)}, bf16[64,1024]{1,0:T(8,128)(2,1)S(1)}, u32[]{:S(2)}, u32[]{:S(2)}) collective-permute-start(bf16[64,1024]{1,0:T(8,128)(2,1)S(1)} %get-tuple-element.38), channel_id=1, source_target_pairs={{0,24},{8,32},{16,40},{24,48},{32,56},{40,0},{48,8},{56,16},{1,25}... | collective-permute-start | bytes 393224 | tf_op jit(solution)/shard_map/ppermute | solution.py:47
  106.1 2.4 %collective-permute-start.19 = (bf16[64,1024]{1,0:T(8,128)(2,1)S(1)}, bf16[64,1024]{1,0:T(8,128)(2,1)S(1)}, u32[]{:S(2)}, u32[]{:S(2)}) collective-permute-start(bf16[64,1024]{1,0:T(8,128)(2,1)S(1)} %get-tuple-element.39), channel_id=1, source_target_pairs={{0,32},{8,40},{16,48},{24,56},{32,0},{40,8},{48,16},{56,24},{1,33}... | collective-permute-start | bytes 393224 | tf_op jit(solution)/shard_map/ppermute | solution.py:47
  108.5 1.4 %collective-permute-start.20 = (bf16[64,1024]{1,0:T(8,128)(2,1)S(1)}, bf16[64,1024]{1,0:T(8,128)(2,1)S(1)}, u32[]{:S(2)}, u32[]{:S(2)}) collective-permute-start(bf16[64,1024]{1,0:T(8,128)(2,1)S(1)} %get-tuple-element.40), channel_id=1, source_target_pairs={{0,40},{8,48},{16,56},{24,0},{32,8},{40,16},{48,24},{56,32},{1,41}... | collective-permute-start | bytes 393224 | tf_op jit(solution)/shard_map/ppermute | solution.py:47
  110.0 2.1 %collective-permute-start.17 = (bf16[64,1024]{1,0:T(8,128)(2,1)}, bf16[64,1024]{1,0:T(8,128)(2,1)S(1)}, u32[]{:S(2)}, u32[]{:S(2)}) collective-permute-start(bf16[64,1024]{1,0:T(8,128)(2,1)} %get-tuple-element.37), channel_id=1, source_target_pairs={{0,16},{8,24},{16,32},{24,40},{32,48},{40,56},{48,0},{56,8},{1,17}... | collective-permute-start | bytes 393224 | tf_op jit(solution)/shard_map/ppermute | solution.py:47
  112.1 4.4 %collective-permute-start.21 = (bf16[64,1024]{1,0:T(8,128)(2,1)S(1)}, bf16[64,1024]{1,0:T(8,128)(2,1)S(1)}, u32[]{:S(2)}, u32[]{:S(2)}) collective-permute-start(bf16[64,1024]{1,0:T(8,128)(2,1)S(1)} %get-tuple-element.41), channel_id=1, source_target_pairs={{0,48},{8,56},{16,0},{24,8},{32,16},{40,24},{48,32},{56,40},{1,49}... | collective-permute-start | bytes 393224 | tf_op jit(solution)/shard_map/ppermute | solution.py:47
  116.4 6.1 %collective-permute-done.19.refs_4_.refs_0_ = bf16[64,1024]{1,0:T(8,128)(2,1)S(1)} collective-permute-done((bf16[64,1024]{1,0:T(8,128)(2,1)S(1)}, bf16[64,1024]{1,0:T(8,128)(2,1)S(1)}, u32[]{:S(2)}, u32[]{:S(2)}) %collective-permute-start.19) | collective-permute-done | bytes 131104 | tf_op jit(solution)/shard_map/ppermute | solution.py:47
  122.6 1.9 %sum.1 = (f32[256,128]{1,0:T(8,128)S(1)}, f32[256,128]{1,0:T(8,128)S(1)}) custom-call(s32[3]{0:T(128)S(1)} %pad_add_fusion.at_ref, bf16[16,2,256,128]{3,2,1,0:T(8,128)(2,1)} %all-to-all-done.2.x_ref, bf16[64,1024]{1,0:T(8,128)(2,1)S(1)} %collective-permute-done.19.refs_4_.refs_0_, bf16[64,1024]{1,0:T(8,128)(2,1)S(1)} %collective-permute-done.18.refs_3_.refs_1_, ...), custom_call_target="tpu_custom_call" | custom-call | bytes 2097152 | tf_op jit(solution)/shard_map/sum/pallas_call | solution.py:405
  124.4 3.4 %collective-permute-start.23 = (f32[256,128]{1,0:T(8,128)S(1)}, f32[256,128]{1,0:T(8,128)S(1)}, u32[]{:S(2)}, u32[]{:S(2)}) collective-permute-start(f32[256,128]{1,0:T(8,128)S(1)} %get-tuple-element.45), channel_id=1, source_target_pairs={{0,128},{128,0},{1,129},{129,1},{2,130},{130,2},{3,131},{131,3},{4... | collective-permute-start | bytes 393224 | tf_op jit(solution)/shard_map/ppermute | solution.py:47
  127.9 1.9 %collective-permute-done.21.refs_6_ = bf16[64,1024]{1,0:T(8,128)(2,1)S(1)} collective-permute-done((bf16[64,1024]{1,0:T(8,128)(2,1)S(1)}, bf16[64,1024]{1,0:T(8,128)(2,1)S(1)}, u32[]{:S(2)}, u32[]{:S(2)}) %collective-permute-start.21) | collective-permute-done | bytes 131104 | tf_op jit(solution)/shard_map/ppermute | solution.py:47
  129.7 1.7 %collective-permute-done.22.refs_7_ = bf16[64,1024]{1,0:T(8,128)(2,1)S(1)} collective-permute-done((bf16[64,1024]{1,0:T(8,128)(2,1)S(1)}, bf16[64,1024]{1,0:T(8,128)(2,1)S(1)}, u32[]{:S(2)}, u32[]{:S(2)}) %collective-permute-start.22) | collective-permute-done | bytes 131104 | tf_op jit(solution)/shard_map/ppermute | solution.py:47
  131.4 1.6 %join.1 = bf16[64,8192]{1,0:T(8,128)(2,1)} custom-call(s32[3]{0:T(128)S(1)} %pad_add_fusion.at_ref, bf16[64,1024]{1,0:T(8,128)(2,1)S(1)} %get-tuple-element.35.refs_0_, bf16[64,1024]{1,0:T(8,128)(2,1)S(1)} %collective-permute-done.16.refs_1_, bf16[64,1024]{1,0:T(8,128)(2,1)S(1)} %collective-permute-done.17.refs_2_, ...), custom_call_target="tpu_custom_call" | custom-call | bytes 2097152 | tf_op jit(solution)/shard_map/join/pallas_call | solution.py:395
  133.0 0.7 broadcast_select_fusion
  (37 shorter events, 1.2 us)
Async XLA Ops:
  2.7 38.2 %all-to-all-start = ((bf16[8,64,1024]{2,1,0:T(8,128)(2,1)}), bf16[8,64,1024]{2,1,0:T(8,128)(2,1)S(1)}, u32[]{:S(2)}, u32[]{:S(2)}) async-start(bf16[8,64,1024]{2,1,0:T(8,128)(2,1)} %deal.1), calls=%async_computation | async-start | bytes 2097152 | tf_op jit(solution)/shard_map/all_to_all | solution.py:291
  11.7 32.3 %copy-start.4 = (bf16[512,128]{1,0:T(8,128)(2,1)S(1)}, bf16[512,128]{1,0:T(8,128)(2,1)}, u32[]{:S(2)}) copy-start(bf16[512,128]{1,0:T(8,128)(2,1)} %key_ref.1) | copy-start | bytes 393220
  11.7 32.3 %copy-start.5 = (bf16[512,128]{1,0:T(8,128)(2,1)S(1)}, bf16[512,128]{1,0:T(8,128)(2,1)}, u32[]{:S(2)}) copy-start(bf16[512,128]{1,0:T(8,128)(2,1)} %value_ref.1) | copy-start | bytes 393220
  22.8 2.2 %collective-permute-start = (bf16[512,128]{1,0:T(8,128)(2,1)}, bf16[512,128]{1,0:T(8,128)(2,1)S(1)}, u32[]{:S(2)}, u32[]{:S(2)}) collective-permute-start(bf16[512,128]{1,0:T(8,128)(2,1)} %get-tuple-element.28), channel_id=1, source_target_pairs={{0,128},{128,0},{1,129},{129,1},{2,130},{130,2},{3,131},{131,3},{4... | collective-permute-start | bytes 393224 | tf_op jit(solution)/shard_map/ppermute | solution.py:47
  25.0 0.9 copy-start.3
  26.5 3.9 %collective-permute-start.1 = (bf16[256,128]{1,0:T(8,128)(2,1)S(1)}, bf16[256,128]{1,0:T(8,128)(2,1)S(1)}, u32[]{:S(2)}, u32[]{:S(2)}) collective-permute-start(bf16[256,128]{1,0:T(8,128)(2,1)S(1)} %get-tuple-element.30), channel_id=1, source_target_pairs={{0,2},{1,3},{2,0},{3,1},{4,6},{5,7},{6,4},{7,5},{8,10},{9,11},{10,... | collective-permute-start | bytes 196616 | tf_op jit(solution)/shard_map/ppermute | solution.py:306
  27.8 5.6 %collective-permute-start.2 = (bf16[256,128]{1,0:T(8,128)(2,1)S(1)}, bf16[256,128]{1,0:T(8,128)(2,1)S(1)}, u32[]{:S(2)}, u32[]{:S(2)}) collective-permute-start(bf16[256,128]{1,0:T(8,128)(2,1)S(1)} %get-tuple-element.31), channel_id=1, source_target_pairs={{0,4},{1,5},{2,6},{3,7},{4,0},{5,1},{6,2},{7,3},{8,12},{9,13},{10,... | collective-permute-start | bytes 196616 | tf_op jit(solution)/shard_map/ppermute | solution.py:306
  30.2 4.5 %collective-permute-start.3 = (bf16[256,128]{1,0:T(8,128)(2,1)S(1)}, bf16[256,128]{1,0:T(8,128)(2,1)S(1)}, u32[]{:S(2)}, u32[]{:S(2)}) collective-permute-start(bf16[256,128]{1,0:T(8,128)(2,1)S(1)} %get-tuple-element.32), channel_id=1, source_target_pairs={{0,6},{1,7},{2,4},{3,5},{4,2},{5,3},{6,0},{7,1},{8,14},{9,15},{10,... | collective-permute-start | bytes 196616 | tf_op jit(solution)/shard_map/ppermute | solution.py:306
  34.7 5.7 %collective-permute-start.4 = (bf16[4,128,128]{2,1,0:T(8,128)(2,1)S(1)}, bf16[4,128,128]{2,1,0:T(8,128)(2,1)S(1)}, u32[]{:S(2)}, u32[]{:S(2)}) collective-permute-start(bf16[4,128,128]{2,1,0:T(8,128)(2,1)S(1)} %middle.1), channel_id=1, source_target_pairs={{0,1},{1,0},{2,3},{3,2},{4,5},{5,4},{6,7},{7,6},{8,9},{9,8},{10,11... | collective-permute-start | bytes 393224 | tf_op jit(solution)/shard_map/ppermute | solution.py:306
  41.5 10.7 %collective-permute-start.5 = (bf16[128,1024]{1,0:T(8,128)(2,1)S(1)}, bf16[128,1024]{1,0:T(8,128)(2,1)}, u32[]{:S(2)}, u32[]{:S(2)}) collective-permute-start(bf16[128,1024]{1,0:T(8,128)(2,1)S(1)} %place.1.refs_0_._), channel_id=1, source_target_pairs={{0,56},{8,0},{16,8},{24,16},{32,24},{40,32},{48,40},{56,48},{1,57}... | collective-permute-start | bytes 786440 | tf_op jit(solution)/shard_map/ppermute | solution.py:47
  44.0 10.2 %collective-permute-start.7 = (bf16[128,1024]{1,0:T(8,128)(2,1)S(1)}, bf16[128,1024]{1,0:T(8,128)(2,1)}, u32[]{:S(2)}, u32[]{:S(2)}) collective-permute-start(bf16[128,1024]{1,0:T(8,128)(2,1)S(1)} %place.1.refs_0_._), channel_id=1, source_target_pairs={{0,8},{8,16},{16,24},{24,32},{32,40},{40,48},{48,56},{56,0},{1,9},... | collective-permute-start | bytes 786440 | tf_op jit(solution)/shard_map/ppermute | solution.py:47
  46.3 40.2 %all-to-all-start.1 = ((bf16[16,512,128]{2,1,0:T(8,128)(2,1)}), bf16[16,512,128]{2,1,0:T(8,128)(2,1)S(1)}, u32[]{:S(2)}, u32[]{:S(2)}) async-start(bf16[16,512,128]{2,1,0:T(8,128)(2,1)} %broadcast_in_dim.2), calls=%async_computation.1 | async-start | bytes 4194304 | tf_op jit(solution)/shard_map/all_to_all | solution.py:344
  52.2 14.0 %copy-start.6 = (f32[2,2,256,128]{3,2,1,0:T(8,128)S(1)}, f32[2,2,256,128]{3,2,1,0:T(8,128)}, u32[]{:S(2)}) copy-start(f32[2,2,256,128]{3,2,1,0:T(8,128)} %param.17) | copy-start | bytes 1572868
  52.2 6.1 %collective-permute-start.6 = (bf16[128,1024]{1,0:T(8,128)(2,1)}, bf16[128,1024]{1,0:T(8,128)(2,1)S(1)}, u32[]{:S(2)}, u32[]{:S(2)}) collective-permute-start(bf16[128,1024]{1,0:T(8,128)(2,1)} %collective-permute-done.5.refs_1_), channel_id=1, source_target_pairs={{0,56},{8,0},{16,8},{24,16},{32,24},{40,32},{48,40},{56,48},{1,57}... | collective-permute-start | bytes 786440 | tf_op jit(solution)/shard_map/ppermute | solution.py:47
  54.2 6.9 %collective-permute-start.8 = (bf16[128,1024]{1,0:T(8,128)(2,1)}, bf16[128,1024]{1,0:T(8,128)(2,1)S(1)}, u32[]{:S(2)}, u32[]{:S(2)}) collective-permute-start(bf16[128,1024]{1,0:T(8,128)(2,1)} %collective-permute-done.7.refs_6_), channel_id=1, source_target_pairs={{0,8},{8,16},{16,24},{24,32},{32,40},{40,48},{48,56},{56,0},{1,9},... | collective-permute-start | bytes 786440 | tf_op jit(solution)/shard_map/ppermute | solution.py:47
  62.0 18.8 %collective-permute-start.9 = (bf16[1024,512]{1,0:T(8,128)(2,1)S(1)}, bf16[1024,512]{1,0:T(8,128)(2,1)S(1)}, u32[]{:S(2)}, u32[]{:S(2)}) collective-permute-start(bf16[1024,512]{1,0:T(8,128)(2,1)S(1)} %turn.1.h_own), channel_id=1, source_target_pairs={{0,128},{128,0},{1,129},{129,1},{2,130},{130,2},{3,131},{131,3},{4... | collective-permute-start | bytes 3145736 | tf_op jit(solution)/shard_map/ppermute | solution.py:47
  66.2 12.1 %collective-permute-start.14 = (f32[2,2,256,128]{3,2,1,0:T(8,128)S(1)}, f32[2,2,256,128]{3,2,1,0:T(8,128)S(1)}, u32[]{:S(2)}, u32[]{:S(2)}) collective-permute-start(f32[2,2,256,128]{3,2,1,0:T(8,128)S(1)} %copy-done.6), channel_id=1, source_target_pairs={{0,128},{128,0},{1,129},{129,1},{2,130},{130,2},{3,131},{131,3},{4... | collective-permute-start | bytes 1572872 | tf_op jit(solution)/shard_map/ppermute | solution.py:47
  66.5 8.9 %collective-permute-start.11 = (bf16[128,1024]{1,0:T(8,128)(2,1)S(1)}, bf16[128,1024]{1,0:T(8,128)(2,1)S(1)}, u32[]{:S(2)}, u32[]{:S(2)}) collective-permute-start(bf16[128,1024]{1,0:T(8,128)(2,1)S(1)} %collective-permute-done.8.__.refs_5_), channel_id=1, source_target_pairs={{0,8},{8,16},{16,24},{24,32},{32,40},{40,48},{48,56},{56,0},{1,9},... | collective-permute-start | bytes 786440 | tf_op jit(solution)/shard_map/ppermute | solution.py:47
  66.5 9.0 %collective-permute-start.10 = (bf16[128,1024]{1,0:T(8,128)(2,1)S(1)}, bf16[128,1024]{1,0:T(8,128)(2,1)S(1)}, u32[]{:S(2)}, u32[]{:S(2)}) collective-permute-start(bf16[128,1024]{1,0:T(8,128)(2,1)S(1)} %collective-permute-done.6._.refs_2_), channel_id=1, source_target_pairs={{0,56},{8,0},{16,8},{24,16},{32,24},{40,32},{48,40},{56,48},{1,57}... | collective-permute-start | bytes 786440 | tf_op jit(solution)/shard_map/ppermute | solution.py:47
  75.4 5.4 %collective-permute-start.12 = (bf16[64,1024]{1,0:T(8,128)(2,1)S(1)}, bf16[64,1024]{1,0:T(8,128)(2,1)S(1)}, u32[]{:S(2)}, u32[]{:S(2)}) collective-permute-start(bf16[64,1024]{1,0:T(8,128)(2,1)S(1)} %slice.8), channel_id=1, source_target_pairs={{0,8},{8,16},{16,24},{24,32},{32,40},{40,48},{48,56},{56,0},{1,9},... | collective-permute-start | bytes 393224 | tf_op jit(solution)/shard_map/ppermute | solution.py:47
  75.5 5.3 %collective-permute-start.13 = (bf16[64,1024]{1,0:T(8,128)(2,1)S(1)}, bf16[64,1024]{1,0:T(8,128)(2,1)S(1)}, u32[]{:S(2)}, u32[]{:S(2)}) collective-permute-start(bf16[64,1024]{1,0:T(8,128)(2,1)S(1)} %slice.9), channel_id=1, source_target_pairs={{0,56},{8,0},{16,8},{24,16},{32,24},{40,32},{48,40},{56,48},{1,57}... | collective-permute-start | bytes 393224 | tf_op jit(solution)/shard_map/ppermute | solution.py:47
  84.3 1.3 copy-start
  85.6 1.0 copy-start.1
  86.6 36.0 %all-to-all-start.2 = ((bf16[16,2,256,128]{3,2,1,0:T(8,128)(2,1)}), bf16[16,2,256,128]{3,2,1,0:T(8,128)(2,1)}, u32[]{:S(2)}, u32[]{:S(2)}) async-start(bf16[16,2,256,128]{3,2,1,0:T(8,128)(2,1)} %bitcast.4), calls=%async_computation.2 | async-start | bytes 4194304 | tf_op jit(solution)/shard_map/all_to_all | solution.py:380
  93.3 1.2 copy-start.2
  95.8 4.8 %collective-permute-start.15 = (bf16[512,1024]{1,0:T(8,128)(2,1)S(1)}, bf16[512,1024]{1,0:T(8,128)(2,1)S(1)}, u32[]{:S(2)}, u32[]{:S(2)}) collective-permute-start(bf16[512,1024]{1,0:T(8,128)(2,1)S(1)} %term.1), channel_id=1, source_target_pairs={{0,128},{128,0},{1,129},{129,1},{2,130},{130,2},{3,131},{131,3},{4... | collective-permute-start | bytes 3145736 | tf_op jit(solution)/shard_map/ppermute | solution.py:47
  102.5 9.6 %collective-permute-start.18 = (bf16[64,1024]{1,0:T(8,128)(2,1)S(1)}, bf16[64,1024]{1,0:T(8,128)(2,1)S(1)}, u32[]{:S(2)}, u32[]{:S(2)}) collective-permute-start(bf16[64,1024]{1,0:T(8,128)(2,1)S(1)} %get-tuple-element.38), channel_id=1, source_target_pairs={{0,24},{8,32},{16,40},{24,48},{32,56},{40,0},{48,8},{56,16},{1,25}... | collective-permute-start | bytes 393224 | tf_op jit(solution)/shard_map/ppermute | solution.py:47
  106.1 16.4 %collective-permute-start.19 = (bf16[64,1024]{1,0:T(8,128)(2,1)S(1)}, bf16[64,1024]{1,0:T(8,128)(2,1)S(1)}, u32[]{:S(2)}, u32[]{:S(2)}) collective-permute-start(bf16[64,1024]{1,0:T(8,128)(2,1)S(1)} %get-tuple-element.39), channel_id=1, source_target_pairs={{0,32},{8,40},{16,48},{24,56},{32,0},{40,8},{48,16},{56,24},{1,33}... | collective-permute-start | bytes 393224 | tf_op jit(solution)/shard_map/ppermute | solution.py:47
  108.5 14.0 %collective-permute-start.20 = (bf16[64,1024]{1,0:T(8,128)(2,1)S(1)}, bf16[64,1024]{1,0:T(8,128)(2,1)S(1)}, u32[]{:S(2)}, u32[]{:S(2)}) collective-permute-start(bf16[64,1024]{1,0:T(8,128)(2,1)S(1)} %get-tuple-element.40), channel_id=1, source_target_pairs={{0,40},{8,48},{16,56},{24,0},{32,8},{40,16},{48,24},{56,32},{1,41}... | collective-permute-start | bytes 393224 | tf_op jit(solution)/shard_map/ppermute | solution.py:47
  110.0 17.9 %collective-permute-start.16 = (bf16[64,1024]{1,0:T(8,128)(2,1)}, bf16[64,1024]{1,0:T(8,128)(2,1)S(1)}, u32[]{:S(2)}, u32[]{:S(2)}) collective-permute-start(bf16[64,1024]{1,0:T(8,128)(2,1)} %get-tuple-element.36), channel_id=1, source_target_pairs={{0,8},{8,16},{16,24},{24,32},{32,40},{40,48},{48,56},{56,0},{1,9},... | collective-permute-start | bytes 393224 | tf_op jit(solution)/shard_map/ppermute | solution.py:47
  110.0 17.9 %collective-permute-start.17 = (bf16[64,1024]{1,0:T(8,128)(2,1)}, bf16[64,1024]{1,0:T(8,128)(2,1)S(1)}, u32[]{:S(2)}, u32[]{:S(2)}) collective-permute-start(bf16[64,1024]{1,0:T(8,128)(2,1)} %get-tuple-element.37), channel_id=1, source_target_pairs={{0,16},{8,24},{16,32},{24,40},{32,48},{40,56},{48,0},{56,8},{1,17}... | collective-permute-start | bytes 393224 | tf_op jit(solution)/shard_map/ppermute | solution.py:47
  112.1 17.7 %collective-permute-start.21 = (bf16[64,1024]{1,0:T(8,128)(2,1)S(1)}, bf16[64,1024]{1,0:T(8,128)(2,1)S(1)}, u32[]{:S(2)}, u32[]{:S(2)}) collective-permute-start(bf16[64,1024]{1,0:T(8,128)(2,1)S(1)} %get-tuple-element.41), channel_id=1, source_target_pairs={{0,48},{8,56},{16,0},{24,8},{32,16},{40,24},{48,32},{56,40},{1,49}... | collective-permute-start | bytes 393224 | tf_op jit(solution)/shard_map/ppermute | solution.py:47
  122.6 8.9 %collective-permute-start.22 = (bf16[64,1024]{1,0:T(8,128)(2,1)S(1)}, bf16[64,1024]{1,0:T(8,128)(2,1)S(1)}, u32[]{:S(2)}, u32[]{:S(2)}) collective-permute-start(bf16[64,1024]{1,0:T(8,128)(2,1)S(1)} %get-tuple-element.42), channel_id=1, source_target_pairs={{0,56},{8,0},{16,8},{24,16},{32,24},{40,32},{48,40},{56,48},{1,57}... | collective-permute-start | bytes 393224 | tf_op jit(solution)/shard_map/ppermute | solution.py:47
  124.4 8.6 %collective-permute-start.23 = (f32[256,128]{1,0:T(8,128)S(1)}, f32[256,128]{1,0:T(8,128)S(1)}, u32[]{:S(2)}, u32[]{:S(2)}) collective-permute-start(f32[256,128]{1,0:T(8,128)S(1)} %get-tuple-element.45), channel_id=1, source_target_pairs={{0,128},{128,0},{1,129},{129,1},{2,130},{130,2},{3,131},{131,3},{4... | collective-permute-start | bytes 393224 | tf_op jit(solution)/shard_map/ppermute | solution.py:47

commit v4 on v3

--- a/solution.py
+++ b/solution.py
@@ -248,14 +248,24 @@
 
 
 def join_kernel(at_ref, *refs):
-    *pieces, out_ref = refs
+    *pieces, out_ref, sems = refs
     z = at_ref[1]
     part = pieces[0].shape[1] // YLO
+    copies = []
     for s, piece in enumerate(pieces):
         source = lax.rem(z - s + Z, Z)
         for y in range(YLO):
             at = pl.multiple_of((y * Z + source) * part, part)
-            out_ref[:, pl.ds(at, part)] = piece[:, y * part : (y + 1) * part]
+            copies.append(
+                pltpu.make_async_copy(
+                    piece.at[:, pl.ds(y * part, part)],
+                    out_ref.at[:, pl.ds(at, part)],
+                    sems.at[s * YLO + y],
+                )
+            )
+            copies[-1].start()
+    for copy in copies:
+        copy.wait()
 
 
 def ring(both):
@@ -394,9 +404,10 @@
     moved = [moved[k] for k in range(Z)]
     input_grad = pl.pallas_call(
         join_kernel,
-        in_specs=[SMEM] + [VMEM] * Z,
-        out_specs=VMEM,
+        in_specs=[SMEM] + [ANY] * Z,
+        out_specs=ANY,
         out_shape=struct(rows, width),
+        scratch_shapes=[pltpu.SemaphoreType.DMA((Z * YLO,))],
         compiler_params=params(16),
         cost_estimate=cost(0, 2 * 2**20),
         name="join",

time: 134 us -> 134 us (level)
  no operation moved by 1% of the time
where the time goes in v4:
time: 134 us
  starting transfers between devices  63.8 us (48%)
  waiting for transfers between devices  36.3 us (27%)
  Pallas kernels  25.9 us (19%)
  local copies, waits for them, and re-layouts  6.22 us (5%)
    ppermute x20, starting transfers between devices, shift(): lax.ppermute(block, axis, [(i, (i + by) % count) for i in range(count)])  35.4 us
    ppermute x20, waiting for transfers between devices, shift(): lax.ppermute(block, axis, [(i, (i + by) % count) for i in range(count)])  28.8 us
    pallas_call x1, Pallas kernels, attention_grads(): pl.pallas_call(attention_kernel, grid=(GROUP // STEP_HEADS,), in_specs=[h...  11.1 us
    all_to_all x1, starting transfers between devices, on_device(): lax.all_to_all(hidden, 'z', split_axis=0, concat_axis=0, tiled=True)  9.01 us
    ppermute x4, waiting for transfers between devices, across(): return lax.ppermute(block, 'tensor', [(i, i ^ mask) for i in range(TEN)])  6.96 us
    ppermute x4, starting transfers between devices, across(): return lax.ppermute(block, 'tensor', [(i, i ^ mask) for i in range(TEN)])  6.95 us
    all_to_all x1, starting transfers between devices, on_device(): lax.all_to_all(partial, PLANE, split_axis=0, concat_axis=0, tiled=True)  6.69 us
    all_to_all x1, starting transfers between devices, on_device(): lax.all_to_all(weight, PLANE, split_axis=0, concat_axis=0, tiled=True)  5.81 us
  transfers between devices with their start and end apart: 27, of which 13 were waited for; matrix products, arithmetic and copies ran while one was open for 1% of the time, Pallas kernels for 17%

profile of v4, /device:TPU:1, one launch (start us, length us, event | category | flops | bytes accessed | tf_op | source)
XLA Modules:
  0.0 133.8 jit_solution(5384134280531094707)
XLA Ops:
  0.6 2.1 %deal.1 = bf16[8,64,1024]{2,1,0:T(8,128)(2,1)} custom-call(bf16[64,8192]{1,0:T(8,128)(2,1)} %x_ref.1), custom_call_target="tpu_custom_call" | custom-call | bytes 2097152 | tf_op jit(solution)/shard_map/deal/pallas_call | solution.py:291
  2.7 9.0 %all-to-all-start = ((bf16[8,64,1024]{2,1,0:T(8,128)(2,1)}), bf16[8,64,1024]{2,1,0:T(8,128)(2,1)S(1)}, u32[]{:S(2)}, u32[]{:S(2)}) async-start(bf16[8,64,1024]{2,1,0:T(8,128)(2,1)} %deal.1), calls=%async_computation | async-start | bytes 2097152 | tf_op jit(solution)/shard_map/all_to_all | solution.py:301
  11.7 11.1 %attention_grads.1 = (bf16[512,1024]{1,0:T(8,128)(2,1)}, bf16[512,128]{1,0:T(8,128)(2,1)}, bf16[512,128]{1,0:T(8,128)(2,1)}) custom-call(bf16[512,1024]{1,0:T(8,128)(2,1)} %q_ref.1, bf16[512,128]{1,0:T(8,128)(2,1)} %k_ref.1, bf16[512,128]{1,0:T(8,128)(2,1)} %v_ref.1, bf16[512,1024]{1,0:T(8,128)(2,1)} %g_ref.1, f32[512,128]{1,0:T(8,128)} %constant.18.clone.c_ref, ...), custom_call_target="tpu_custom_call" | custom-call | flops 12000000000 | bytes 4194304 | tf_op jit(solution)/shard_map/attention_grads/pallas_call | solution.py:114
  22.8 1.0 collective-permute-start
  23.9 1.1 collective-permute-done.other_ref
  25.0 0.9 copy-done.3
  25.9 0.6 split.1
  26.5 1.3 collective-permute-start.1
  27.8 2.5 %collective-permute-start.2 = (bf16[256,128]{1,0:T(8,128)(2,1)S(1)}, bf16[256,128]{1,0:T(8,128)(2,1)S(1)}, u32[]{:S(2)}, u32[]{:S(2)}) collective-permute-start(bf16[256,128]{1,0:T(8,128)(2,1)S(1)} %get-tuple-element.31), channel_id=1, source_target_pairs={{0,4},{1,5},{2,6},{3,7},{4,0},{5,1},{6,2},{7,3},{8,12},{9,13},{10,... | collective-permute-start | bytes 196616 | tf_op jit(solution)/shard_map/ppermute | solution.py:316
  30.4 2.9 %collective-permute-done.2.refs_2_ = bf16[256,128]{1,0:T(8,128)(2,1)S(1)} collective-permute-done((bf16[256,128]{1,0:T(8,128)(2,1)S(1)}, bf16[256,128]{1,0:T(8,128)(2,1)S(1)}, u32[]{:S(2)}, u32[]{:S(2)}) %collective-permute-start.2) | collective-permute-done | bytes 65568 | tf_op jit(solution)/shard_map/ppermute | solution.py:316
  33.3 1.4 %collective-permute-done.3.refs_3_ = bf16[256,128]{1,0:T(8,128)(2,1)S(1)} collective-permute-done((bf16[256,128]{1,0:T(8,128)(2,1)S(1)}, bf16[256,128]{1,0:T(8,128)(2,1)S(1)}, u32[]{:S(2)}, u32[]{:S(2)}) %collective-permute-start.3) | collective-permute-done | bytes 65568 | tf_op jit(solution)/shard_map/ppermute | solution.py:316
  34.7 3.0 %collective-permute-start.4 = (bf16[4,128,128]{2,1,0:T(8,128)(2,1)S(1)}, bf16[4,128,128]{2,1,0:T(8,128)(2,1)S(1)}, u32[]{:S(2)}, u32[]{:S(2)}) collective-permute-start(bf16[4,128,128]{2,1,0:T(8,128)(2,1)S(1)} %middle.1), channel_id=1, source_target_pairs={{0,1},{1,0},{2,3},{3,2},{4,5},{5,4},{6,7},{7,6},{8,9},{9,8},{10,11... | collective-permute-start | bytes 393224 | tf_op jit(solution)/shard_map/ppermute | solution.py:316
  37.7 2.7 %collective-permute-done.4.refs_4_ = bf16[4,128,128]{2,1,0:T(8,128)(2,1)S(1)} collective-permute-done((bf16[4,128,128]{2,1,0:T(8,128)(2,1)S(1)}, bf16[4,128,128]{2,1,0:T(8,128)(2,1)S(1)}, u32[]{:S(2)}, u32[]{:S(2)}) %collective-permute-start.4) | collective-permute-done | bytes 131104 | tf_op jit(solution)/shard_map/ppermute | solution.py:316
  40.9 0.6 place.1.refs_0_._
  41.5 2.5 %collective-permute-start.5 = (bf16[128,1024]{1,0:T(8,128)(2,1)S(1)}, bf16[128,1024]{1,0:T(8,128)(2,1)}, u32[]{:S(2)}, u32[]{:S(2)}) collective-permute-start(bf16[128,1024]{1,0:T(8,128)(2,1)S(1)} %place.1.refs_0_._), channel_id=1, source_target_pairs={{0,56},{8,0},{16,8},{24,16},{32,24},{40,32},{48,40},{56,48},{1,57}... | collective-permute-start | bytes 786440 | tf_op jit(solution)/shard_map/ppermute | solution.py:47
  44.0 0.6 select.1
  44.6 1.8 %broadcast_in_dim.2 = bf16[16,512,128]{2,1,0:T(8,128)(2,1)} broadcast(bf16[512,128]{1,0:T(8,128)(2,1)S(1)} %select.1), dimensions={1,2} | broadcast | bytes 2228224 | tf_op jit(solution)/shard_map/broadcast_in_dim | solution.py:353
  46.3 5.8 %all-to-all-start.1 = ((bf16[16,512,128]{2,1,0:T(8,128)(2,1)}), bf16[16,512,128]{2,1,0:T(8,128)(2,1)S(1)}, u32[]{:S(2)}, u32[]{:S(2)}) async-start(bf16[16,512,128]{2,1,0:T(8,128)(2,1)} %broadcast_in_dim.2), calls=%async_computation.1 | async-start | bytes 4194304 | tf_op jit(solution)/shard_map/all_to_all | solution.py:354
  52.2 2.0 %collective-permute-start.6 = (bf16[128,1024]{1,0:T(8,128)(2,1)}, bf16[128,1024]{1,0:T(8,128)(2,1)S(1)}, u32[]{:S(2)}, u32[]{:S(2)}) collective-permute-start(bf16[128,1024]{1,0:T(8,128)(2,1)} %collective-permute-done.5.refs_1_), channel_id=1, source_target_pairs={{0,56},{8,0},{16,8},{24,16},{32,24},{40,32},{48,40},{56,48},{1,57}... | collective-permute-start | bytes 786440 | tf_op jit(solution)/shard_map/ppermute | solution.py:47
  54.2 4.1 %collective-permute-done.6._.refs_2_ = bf16[128,1024]{1,0:T(8,128)(2,1)S(1)} collective-permute-done((bf16[128,1024]{1,0:T(8,128)(2,1)}, bf16[128,1024]{1,0:T(8,128)(2,1)S(1)}, u32[]{:S(2)}, u32[]{:S(2)}) %collective-permute-start.6) | collective-permute-done | bytes 262176 | tf_op jit(solution)/shard_map/ppermute | solution.py:47
  58.3 2.8 %collective-permute-done.8.__.refs_5_ = bf16[128,1024]{1,0:T(8,128)(2,1)S(1)} collective-permute-done((bf16[128,1024]{1,0:T(8,128)(2,1)}, bf16[128,1024]{1,0:T(8,128)(2,1)S(1)}, u32[]{:S(2)}, u32[]{:S(2)}) %collective-permute-start.8) | collective-permute-done | bytes 262176 | tf_op jit(solution)/shard_map/ppermute | solution.py:47
  61.1 0.9 turn.1.h_own
  62.0 4.2 %collective-permute-start.9 = (bf16[1024,512]{1,0:T(8,128)(2,1)S(1)}, bf16[1024,512]{1,0:T(8,128)(2,1)S(1)}, u32[]{:S(2)}, u32[]{:S(2)}) collective-permute-start(bf16[1024,512]{1,0:T(8,128)(2,1)S(1)} %turn.1.h_own), channel_id=1, source_target_pairs={{0,128},{128,0},{1,129},{129,1},{2,130},{130,2},{3,131},{131,3},{4... | collective-permute-start | bytes 3145736 | tf_op jit(solution)/shard_map/ppermute | solution.py:47
  66.5 2.7 %collective-permute-start.10 = (bf16[128,1024]{1,0:T(8,128)(2,1)S(1)}, bf16[128,1024]{1,0:T(8,128)(2,1)S(1)}, u32[]{:S(2)}, u32[]{:S(2)}) collective-permute-start(bf16[128,1024]{1,0:T(8,128)(2,1)S(1)} %collective-permute-done.6._.refs_2_), channel_id=1, source_target_pairs={{0,56},{8,0},{16,8},{24,16},{32,24},{40,32},{48,40},{56,48},{1,57}... | collective-permute-start | bytes 786440 | tf_op jit(solution)/shard_map/ppermute | solution.py:47
  69.2 6.2 %collective-permute-done.11.refs_4_ = bf16[128,1024]{1,0:T(8,128)(2,1)S(1)} collective-permute-done((bf16[128,1024]{1,0:T(8,128)(2,1)S(1)}, bf16[128,1024]{1,0:T(8,128)(2,1)S(1)}, u32[]{:S(2)}, u32[]{:S(2)}) %collective-permute-start.11) | collective-permute-done | bytes 262176 | tf_op jit(solution)/shard_map/ppermute | solution.py:47
  75.5 2.7 %collective-permute-start.13 = (bf16[64,1024]{1,0:T(8,128)(2,1)S(1)}, bf16[64,1024]{1,0:T(8,128)(2,1)S(1)}, u32[]{:S(2)}, u32[]{:S(2)}) collective-permute-start(bf16[64,1024]{1,0:T(8,128)(2,1)S(1)} %slice.9), channel_id=1, source_target_pairs={{0,56},{8,0},{16,8},{24,16},{32,24},{40,32},{48,40},{56,48},{1,57}... | collective-permute-start | bytes 393224 | tf_op jit(solution)/shard_map/ppermute | solution.py:47
  78.2 2.5 %collective-permute-done.12.refs_7_ = bf16[64,1024]{1,0:T(8,128)(2,1)S(1)} collective-permute-done((bf16[64,1024]{1,0:T(8,128)(2,1)S(1)}, bf16[64,1024]{1,0:T(8,128)(2,1)S(1)}, u32[]{:S(2)}, u32[]{:S(2)}) %collective-permute-start.12) | collective-permute-done | bytes 131104 | tf_op jit(solution)/shard_map/ppermute | solution.py:47
  80.8 3.5 %weight_grad.1 = (bf16[2,8,2,256,128]{4,3,2,1,0:T(8,128)(2,1)S(1)}, bf16[512,1024]{1,0:T(8,128)(2,1)S(1)}, bf16[512,1024]{1,0:T(8,128)(2,1)S(1)}, f32[2,2,256,128]{3,2,1,0:T(8,128)}) custom-call(bf16[1024,512]{1,0:T(8,128)(2,1)S(1)} %turn.1.h_own, bf16[1024,512]{1,0:T(8,128)(2,1)S(1)} %collective-permute-done.9.h_other, ...), custom_call_target="tpu_custom_call" | custom-call | flops 4294967296 | bytes 8388608 | tf_op jit(solution)/shard_map/weight_grad/pallas_call | solution.py:369
  84.3 1.3 copy-done
  85.6 1.0 copy-done.1
  86.6 6.7 %all-to-all-start.2 = ((bf16[16,2,256,128]{3,2,1,0:T(8,128)(2,1)}), bf16[16,2,256,128]{3,2,1,0:T(8,128)(2,1)}, u32[]{:S(2)}, u32[]{:S(2)}) async-start(bf16[16,2,256,128]{3,2,1,0:T(8,128)(2,1)} %bitcast.4), calls=%async_computation.2 | async-start | bytes 4194304 | tf_op jit(solution)/shard_map/all_to_all | solution.py:390
  93.3 1.2 copy-done.2
  94.5 1.3 term.1
  95.8 2.5 %collective-permute-start.15 = (bf16[512,1024]{1,0:T(8,128)(2,1)S(1)}, bf16[512,1024]{1,0:T(8,128)(2,1)S(1)}, u32[]{:S(2)}, u32[]{:S(2)}) collective-permute-start(bf16[512,1024]{1,0:T(8,128)(2,1)S(1)} %term.1), channel_id=1, source_target_pairs={{0,128},{128,0},{1,129},{129,1},{2,130},{130,2},{3,131},{131,3},{4... | collective-permute-start | bytes 3145736 | tf_op jit(solution)/shard_map/ppermute | solution.py:47
  98.3 2.3 %collective-permute-done.15.given_ref = bf16[512,1024]{1,0:T(8,128)(2,1)S(1)} collective-permute-done((bf16[512,1024]{1,0:T(8,128)(2,1)S(1)}, bf16[512,1024]{1,0:T(8,128)(2,1)S(1)}, u32[]{:S(2)}, u32[]{:S(2)}) %collective-permute-start.15) | collective-permute-done | bytes 1048608 | tf_op jit(solution)/shard_map/ppermute | solution.py:47
  100.6 1.9 %add.5 = (bf16[64,1024]{1,0:T(8,128)(2,1)S(1)}, bf16[64,1024]{1,0:T(8,128)(2,1)}, bf16[64,1024]{1,0:T(8,128)(2,1)}, bf16[64,1024]{1,0:T(8,128)(2,1)S(1)}, bf16[6...) custom-call(bf16[512,1024]{1,0:T(8,128)(2,1)S(1)} %get-tuple-element, ...), custom_call_target="tpu_custom_call" | custom-call | flops 1073741824 | bytes 5242880 | tf_op jit(solution)/shard_map/add/pallas_call | solution.py:392
  102.5 3.6 %collective-permute-start.18 = (bf16[64,1024]{1,0:T(8,128)(2,1)S(1)}, bf16[64,1024]{1,0:T(8,128)(2,1)S(1)}, u32[]{:S(2)}, u32[]{:S(2)}) collective-permute-start(bf16[64,1024]{1,0:T(8,128)(2,1)S(1)} %get-tuple-element.38), channel_id=1, source_target_pairs={{0,24},{8,32},{16,40},{24,48},{32,56},{40,0},{48,8},{56,16},{1,25}... | collective-permute-start | bytes 393224 | tf_op jit(solution)/shard_map/ppermute | solution.py:47
  106.1 2.4 %collective-permute-start.19 = (bf16[64,1024]{1,0:T(8,128)(2,1)S(1)}, bf16[64,1024]{1,0:T(8,128)(2,1)S(1)}, u32[]{:S(2)}, u32[]{:S(2)}) collective-permute-start(bf16[64,1024]{1,0:T(8,128)(2,1)S(1)} %get-tuple-element.39), channel_id=1, source_target_pairs={{0,32},{8,40},{16,48},{24,56},{32,0},{40,8},{48,16},{56,24},{1,33}... | collective-permute-start | bytes 393224 | tf_op jit(solution)/shard_map/ppermute | solution.py:47
  108.5 1.4 %collective-permute-start.20 = (bf16[64,1024]{1,0:T(8,128)(2,1)S(1)}, bf16[64,1024]{1,0:T(8,128)(2,1)S(1)}, u32[]{:S(2)}, u32[]{:S(2)}) collective-permute-start(bf16[64,1024]{1,0:T(8,128)(2,1)S(1)} %get-tuple-element.40), channel_id=1, source_target_pairs={{0,40},{8,48},{16,56},{24,0},{32,8},{40,16},{48,24},{56,32},{1,41}... | collective-permute-start | bytes 393224 | tf_op jit(solution)/shard_map/ppermute | solution.py:47
  110.0 2.1 %collective-permute-start.17 = (bf16[64,1024]{1,0:T(8,128)(2,1)}, bf16[64,1024]{1,0:T(8,128)(2,1)S(1)}, u32[]{:S(2)}, u32[]{:S(2)}) collective-permute-start(bf16[64,1024]{1,0:T(8,128)(2,1)} %get-tuple-element.37), channel_id=1, source_target_pairs={{0,16},{8,24},{16,32},{24,40},{32,48},{40,56},{48,0},{56,8},{1,17}... | collective-permute-start | bytes 393224 | tf_op jit(solution)/shard_map/ppermute | solution.py:47
  112.1 4.4 %collective-permute-start.21 = (bf16[64,1024]{1,0:T(8,128)(2,1)S(1)}, bf16[64,1024]{1,0:T(8,128)(2,1)S(1)}, u32[]{:S(2)}, u32[]{:S(2)}) collective-permute-start(bf16[64,1024]{1,0:T(8,128)(2,1)S(1)} %get-tuple-element.41), channel_id=1, source_target_pairs={{0,48},{8,56},{16,0},{24,8},{32,16},{40,24},{48,32},{56,40},{1,49}... | collective-permute-start | bytes 393224 | tf_op jit(solution)/shard_map/ppermute | solution.py:47
  116.4 6.1 %collective-permute-done.19.refs_4_.refs_0_ = bf16[64,1024]{1,0:T(8,128)(2,1)S(1)} collective-permute-done((bf16[64,1024]{1,0:T(8,128)(2,1)S(1)}, bf16[64,1024]{1,0:T(8,128)(2,1)S(1)}, u32[]{:S(2)}, u32[]{:S(2)}) %collective-permute-start.19) | collective-permute-done | bytes 131104 | tf_op jit(solution)/shard_map/ppermute | solution.py:47
  122.6 1.9 %sum.1 = (f32[256,128]{1,0:T(8,128)S(1)}, f32[256,128]{1,0:T(8,128)S(1)}) custom-call(s32[3]{0:T(128)S(1)} %pad_add_fusion.at_ref, bf16[16,2,256,128]{3,2,1,0:T(8,128)(2,1)} %all-to-all-done.2.x_ref, bf16[64,1024]{1,0:T(8,128)(2,1)S(1)} %collective-permute-done.19.refs_4_.refs_0_, bf16[64,1024]{1,0:T(8,128)(2,1)S(1)} %collective-permute-done.18.refs_3_.refs_1_, ...), custom_call_target="tpu_custom_call" | custom-call | bytes 2097152 | tf_op jit(solution)/shard_map/sum/pallas_call | solution.py:416
  124.4 3.4 %collective-permute-start.23 = (f32[256,128]{1,0:T(8,128)S(1)}, f32[256,128]{1,0:T(8,128)S(1)}, u32[]{:S(2)}, u32[]{:S(2)}) collective-permute-start(f32[256,128]{1,0:T(8,128)S(1)} %get-tuple-element.45), channel_id=1, source_target_pairs={{0,128},{128,0},{1,129},{129,1},{2,130},{130,2},{3,131},{131,3},{4... | collective-permute-start | bytes 393224 | tf_op jit(solution)/shard_map/ppermute | solution.py:47
  127.9 1.9 %collective-permute-done.21.refs_6_ = bf16[64,1024]{1,0:T(8,128)(2,1)S(1)} collective-permute-done((bf16[64,1024]{1,0:T(8,128)(2,1)S(1)}, bf16[64,1024]{1,0:T(8,128)(2,1)S(1)}, u32[]{:S(2)}, u32[]{:S(2)}) %collective-permute-start.21) | collective-permute-done | bytes 131104 | tf_op jit(solution)/shard_map/ppermute | solution.py:47
  129.7 1.7 %collective-permute-done.22.refs_7_ = bf16[64,1024]{1,0:T(8,128)(2,1)S(1)} collective-permute-done((bf16[64,1024]{1,0:T(8,128)(2,1)S(1)}, bf16[64,1024]{1,0:T(8,128)(2,1)S(1)}, u32[]{:S(2)}, u32[]{:S(2)}) %collective-permute-start.22) | collective-permute-done | bytes 131104 | tf_op jit(solution)/shard_map/ppermute | solution.py:47
  131.4 1.6 %join.1 = bf16[64,8192]{1,0:T(8,128)(2,1)} custom-call(s32[3]{0:T(128)S(1)} %pad_add_fusion.at_ref, bf16[64,1024]{1,0:T(8,128)(2,1)S(1)} %get-tuple-element.35.refs_0_, bf16[64,1024]{1,0:T(8,128)(2,1)S(1)} %collective-permute-done.16.refs_1_, bf16[64,1024]{1,0:T(8,128)(2,1)S(1)} %collective-permute-done.17.refs_2_, ...), custom_call_target="tpu_custom_call" | custom-call | bytes 2097152 | tf_op jit(solution)/shard_map/join/pallas_call | solution.py:405
  133.1 0.7 broadcast_select_fusion
  (37 shorter events, 1.2 us)
Async XLA Ops:
  2.7 38.2 %all-to-all-start = ((bf16[8,64,1024]{2,1,0:T(8,128)(2,1)}), bf16[8,64,1024]{2,1,0:T(8,128)(2,1)S(1)}, u32[]{:S(2)}, u32[]{:S(2)}) async-start(bf16[8,64,1024]{2,1,0:T(8,128)(2,1)} %deal.1), calls=%async_computation | async-start | bytes 2097152 | tf_op jit(solution)/shard_map/all_to_all | solution.py:301
  11.7 32.3 %copy-start.4 = (bf16[512,128]{1,0:T(8,128)(2,1)S(1)}, bf16[512,128]{1,0:T(8,128)(2,1)}, u32[]{:S(2)}) copy-start(bf16[512,128]{1,0:T(8,128)(2,1)} %key_ref.1) | copy-start | bytes 393220
  11.7 32.3 %copy-start.5 = (bf16[512,128]{1,0:T(8,128)(2,1)S(1)}, bf16[512,128]{1,0:T(8,128)(2,1)}, u32[]{:S(2)}) copy-start(bf16[512,128]{1,0:T(8,128)(2,1)} %value_ref.1) | copy-start | bytes 393220
  22.8 2.2 %collective-permute-start = (bf16[512,128]{1,0:T(8,128)(2,1)}, bf16[512,128]{1,0:T(8,128)(2,1)S(1)}, u32[]{:S(2)}, u32[]{:S(2)}) collective-permute-start(bf16[512,128]{1,0:T(8,128)(2,1)} %get-tuple-element.28), channel_id=1, source_target_pairs={{0,128},{128,0},{1,129},{129,1},{2,130},{130,2},{3,131},{131,3},{4... | collective-permute-start | bytes 393224 | tf_op jit(solution)/shard_map/ppermute | solution.py:47
  25.0 0.9 copy-start.3
  26.5 3.9 %collective-permute-start.1 = (bf16[256,128]{1,0:T(8,128)(2,1)S(1)}, bf16[256,128]{1,0:T(8,128)(2,1)S(1)}, u32[]{:S(2)}, u32[]{:S(2)}) collective-permute-start(bf16[256,128]{1,0:T(8,128)(2,1)S(1)} %get-tuple-element.30), channel_id=1, source_target_pairs={{0,2},{1,3},{2,0},{3,1},{4,6},{5,7},{6,4},{7,5},{8,10},{9,11},{10,... | collective-permute-start | bytes 196616 | tf_op jit(solution)/shard_map/ppermute | solution.py:316
  27.8 5.6 %collective-permute-start.2 = (bf16[256,128]{1,0:T(8,128)(2,1)S(1)}, bf16[256,128]{1,0:T(8,128)(2,1)S(1)}, u32[]{:S(2)}, u32[]{:S(2)}) collective-permute-start(bf16[256,128]{1,0:T(8,128)(2,1)S(1)} %get-tuple-element.31), channel_id=1, source_target_pairs={{0,4},{1,5},{2,6},{3,7},{4,0},{5,1},{6,2},{7,3},{8,12},{9,13},{10,... | collective-permute-start | bytes 196616 | tf_op jit(solution)/shard_map/ppermute | solution.py:316
  30.2 4.5 %collective-permute-start.3 = (bf16[256,128]{1,0:T(8,128)(2,1)S(1)}, bf16[256,128]{1,0:T(8,128)(2,1)S(1)}, u32[]{:S(2)}, u32[]{:S(2)}) collective-permute-start(bf16[256,128]{1,0:T(8,128)(2,1)S(1)} %get-tuple-element.32), channel_id=1, source_target_pairs={{0,6},{1,7},{2,4},{3,5},{4,2},{5,3},{6,0},{7,1},{8,14},{9,15},{10,... | collective-permute-start | bytes 196616 | tf_op jit(solution)/shard_map/ppermute | solution.py:316
  34.7 5.7 %collective-permute-start.4 = (bf16[4,128,128]{2,1,0:T(8,128)(2,1)S(1)}, bf16[4,128,128]{2,1,0:T(8,128)(2,1)S(1)}, u32[]{:S(2)}, u32[]{:S(2)}) collective-permute-start(bf16[4,128,128]{2,1,0:T(8,128)(2,1)S(1)} %middle.1), channel_id=1, source_target_pairs={{0,1},{1,0},{2,3},{3,2},{4,5},{5,4},{6,7},{7,6},{8,9},{9,8},{10,11... | collective-permute-start | bytes 393224 | tf_op jit(solution)/shard_map/ppermute | solution.py:316
  41.5 10.7 %collective-permute-start.5 = (bf16[128,1024]{1,0:T(8,128)(2,1)S(1)}, bf16[128,1024]{1,0:T(8,128)(2,1)}, u32[]{:S(2)}, u32[]{:S(2)}) collective-permute-start(bf16[128,1024]{1,0:T(8,128)(2,1)S(1)} %place.1.refs_0_._), channel_id=1, source_target_pairs={{0,56},{8,0},{16,8},{24,16},{32,24},{40,32},{48,40},{56,48},{1,57}... | collective-permute-start | bytes 786440 | tf_op jit(solution)/shard_map/ppermute | solution.py:47
  44.0 10.2 %collective-permute-start.7 = (bf16[128,1024]{1,0:T(8,128)(2,1)S(1)}, bf16[128,1024]{1,0:T(8,128)(2,1)}, u32[]{:S(2)}, u32[]{:S(2)}) collective-permute-start(bf16[128,1024]{1,0:T(8,128)(2,1)S(1)} %place.1.refs_0_._), channel_id=1, source_target_pairs={{0,8},{8,16},{16,24},{24,32},{32,40},{40,48},{48,56},{56,0},{1,9},... | collective-permute-start | bytes 786440 | tf_op jit(solution)/shard_map/ppermute | solution.py:47
  46.3 40.2 %all-to-all-start.1 = ((bf16[16,512,128]{2,1,0:T(8,128)(2,1)}), bf16[16,512,128]{2,1,0:T(8,128)(2,1)S(1)}, u32[]{:S(2)}, u32[]{:S(2)}) async-start(bf16[16,512,128]{2,1,0:T(8,128)(2,1)} %broadcast_in_dim.2), calls=%async_computation.1 | async-start | bytes 4194304 | tf_op jit(solution)/shard_map/all_to_all | solution.py:354
  52.2 14.0 %copy-start.6 = (f32[2,2,256,128]{3,2,1,0:T(8,128)S(1)}, f32[2,2,256,128]{3,2,1,0:T(8,128)}, u32[]{:S(2)}) copy-start(f32[2,2,256,128]{3,2,1,0:T(8,128)} %param.17) | copy-start | bytes 1572868
  52.2 6.1 %collective-permute-start.6 = (bf16[128,1024]{1,0:T(8,128)(2,1)}, bf16[128,1024]{1,0:T(8,128)(2,1)S(1)}, u32[]{:S(2)}, u32[]{:S(2)}) collective-permute-start(bf16[128,1024]{1,0:T(8,128)(2,1)} %collective-permute-done.5.refs_1_), channel_id=1, source_target_pairs={{0,56},{8,0},{16,8},{24,16},{32,24},{40,32},{48,40},{56,48},{1,57}... | collective-permute-start | bytes 786440 | tf_op jit(solution)/shard_map/ppermute | solution.py:47
  54.2 6.9 %collective-permute-start.8 = (bf16[128,1024]{1,0:T(8,128)(2,1)}, bf16[128,1024]{1,0:T(8,128)(2,1)S(1)}, u32[]{:S(2)}, u32[]{:S(2)}) collective-permute-start(bf16[128,1024]{1,0:T(8,128)(2,1)} %collective-permute-done.7.refs_6_), channel_id=1, source_target_pairs={{0,8},{8,16},{16,24},{24,32},{32,40},{40,48},{48,56},{56,0},{1,9},... | collective-permute-start | bytes 786440 | tf_op jit(solution)/shard_map/ppermute | solution.py:47
  62.0 18.8 %collective-permute-start.9 = (bf16[1024,512]{1,0:T(8,128)(2,1)S(1)}, bf16[1024,512]{1,0:T(8,128)(2,1)S(1)}, u32[]{:S(2)}, u32[]{:S(2)}) collective-permute-start(bf16[1024,512]{1,0:T(8,128)(2,1)S(1)} %turn.1.h_own), channel_id=1, source_target_pairs={{0,128},{128,0},{1,129},{129,1},{2,130},{130,2},{3,131},{131,3},{4... | collective-permute-start | bytes 3145736 | tf_op jit(solution)/shard_map/ppermute | solution.py:47
  66.2 12.1 %collective-permute-start.14 = (f32[2,2,256,128]{3,2,1,0:T(8,128)S(1)}, f32[2,2,256,128]{3,2,1,0:T(8,128)S(1)}, u32[]{:S(2)}, u32[]{:S(2)}) collective-permute-start(f32[2,2,256,128]{3,2,1,0:T(8,128)S(1)} %copy-done.6), channel_id=1, source_target_pairs={{0,128},{128,0},{1,129},{129,1},{2,130},{130,2},{3,131},{131,3},{4... | collective-permute-start | bytes 1572872 | tf_op jit(solution)/shard_map/ppermute | solution.py:47
  66.5 8.9 %collective-permute-start.11 = (bf16[128,1024]{1,0:T(8,128)(2,1)S(1)}, bf16[128,1024]{1,0:T(8,128)(2,1)S(1)}, u32[]{:S(2)}, u32[]{:S(2)}) collective-permute-start(bf16[128,1024]{1,0:T(8,128)(2,1)S(1)} %collective-permute-done.8.__.refs_5_), channel_id=1, source_target_pairs={{0,8},{8,16},{16,24},{24,32},{32,40},{40,48},{48,56},{56,0},{1,9},... | collective-permute-start | bytes 786440 | tf_op jit(solution)/shard_map/ppermute | solution.py:47
  66.5 9.0 %collective-permute-start.10 = (bf16[128,1024]{1,0:T(8,128)(2,1)S(1)}, bf16[128,1024]{1,0:T(8,128)(2,1)S(1)}, u32[]{:S(2)}, u32[]{:S(2)}) collective-permute-start(bf16[128,1024]{1,0:T(8,128)(2,1)S(1)} %collective-permute-done.6._.refs_2_), channel_id=1, source_target_pairs={{0,56},{8,0},{16,8},{24,16},{32,24},{40,32},{48,40},{56,48},{1,57}... | collective-permute-start | bytes 786440 | tf_op jit(solution)/shard_map/ppermute | solution.py:47
  75.4 5.4 %collective-permute-start.12 = (bf16[64,1024]{1,0:T(8,128)(2,1)S(1)}, bf16[64,1024]{1,0:T(8,128)(2,1)S(1)}, u32[]{:S(2)}, u32[]{:S(2)}) collective-permute-start(bf16[64,1024]{1,0:T(8,128)(2,1)S(1)} %slice.8), channel_id=1, source_target_pairs={{0,8},{8,16},{16,24},{24,32},{32,40},{40,48},{48,56},{56,0},{1,9},... | collective-permute-start | bytes 393224 | tf_op jit(solution)/shard_map/ppermute | solution.py:47
  75.5 5.3 %collective-permute-start.13 = (bf16[64,1024]{1,0:T(8,128)(2,1)S(1)}, bf16[64,1024]{1,0:T(8,128)(2,1)S(1)}, u32[]{:S(2)}, u32[]{:S(2)}) collective-permute-start(bf16[64,1024]{1,0:T(8,128)(2,1)S(1)} %slice.9), channel_id=1, source_target_pairs={{0,56},{8,0},{16,8},{24,16},{32,24},{40,32},{48,40},{56,48},{1,57}... | collective-permute-start | bytes 393224 | tf_op jit(solution)/shard_map/ppermute | solution.py:47
  84.3 1.3 copy-start
  85.6 1.0 copy-start.1
  86.6 36.0 %all-to-all-start.2 = ((bf16[16,2,256,128]{3,2,1,0:T(8,128)(2,1)}), bf16[16,2,256,128]{3,2,1,0:T(8,128)(2,1)}, u32[]{:S(2)}, u32[]{:S(2)}) async-start(bf16[16,2,256,128]{3,2,1,0:T(8,128)(2,1)} %bitcast.4), calls=%async_computation.2 | async-start | bytes 4194304 | tf_op jit(solution)/shard_map/all_to_all | solution.py:390
  93.3 1.2 copy-start.2
  95.8 4.8 %collective-permute-start.15 = (bf16[512,1024]{1,0:T(8,128)(2,1)S(1)}, bf16[512,1024]{1,0:T(8,128)(2,1)S(1)}, u32[]{:S(2)}, u32[]{:S(2)}) collective-permute-start(bf16[512,1024]{1,0:T(8,128)(2,1)S(1)} %term.1), channel_id=1, source_target_pairs={{0,128},{128,0},{1,129},{129,1},{2,130},{130,2},{3,131},{131,3},{4... | collective-permute-start | bytes 3145736 | tf_op jit(solution)/shard_map/ppermute | solution.py:47
  102.5 9.6 %collective-permute-start.18 = (bf16[64,1024]{1,0:T(8,128)(2,1)S(1)}, bf16[64,1024]{1,0:T(8,128)(2,1)S(1)}, u32[]{:S(2)}, u32[]{:S(2)}) collective-permute-start(bf16[64,1024]{1,0:T(8,128)(2,1)S(1)} %get-tuple-element.38), channel_id=1, source_target_pairs={{0,24},{8,32},{16,40},{24,48},{32,56},{40,0},{48,8},{56,16},{1,25}... | collective-permute-start | bytes 393224 | tf_op jit(solution)/shard_map/ppermute | solution.py:47
  106.1 16.4 %collective-permute-start.19 = (bf16[64,1024]{1,0:T(8,128)(2,1)S(1)}, bf16[64,1024]{1,0:T(8,128)(2,1)S(1)}, u32[]{:S(2)}, u32[]{:S(2)}) collective-permute-start(bf16[64,1024]{1,0:T(8,128)(2,1)S(1)} %get-tuple-element.39), channel_id=1, source_target_pairs={{0,32},{8,40},{16,48},{24,56},{32,0},{40,8},{48,16},{56,24},{1,33}... | collective-permute-start | bytes 393224 | tf_op jit(solution)/shard_map/ppermute | solution.py:47
  108.5 14.0 %collective-permute-start.20 = (bf16[64,1024]{1,0:T(8,128)(2,1)S(1)}, bf16[64,1024]{1,0:T(8,128)(2,1)S(1)}, u32[]{:S(2)}, u32[]{:S(2)}) collective-permute-start(bf16[64,1024]{1,0:T(8,128)(2,1)S(1)} %get-tuple-element.40), channel_id=1, source_target_pairs={{0,40},{8,48},{16,56},{24,0},{32,8},{40,16},{48,24},{56,32},{1,41}... | collective-permute-start | bytes 393224 | tf_op jit(solution)/shard_map/ppermute | solution.py:47
  110.0 17.9 %collective-permute-start.16 = (bf16[64,1024]{1,0:T(8,128)(2,1)}, bf16[64,1024]{1,0:T(8,128)(2,1)S(1)}, u32[]{:S(2)}, u32[]{:S(2)}) collective-permute-start(bf16[64,1024]{1,0:T(8,128)(2,1)} %get-tuple-element.36), channel_id=1, source_target_pairs={{0,8},{8,16},{16,24},{24,32},{32,40},{40,48},{48,56},{56,0},{1,9},... | collective-permute-start | bytes 393224 | tf_op jit(solution)/shard_map/ppermute | solution.py:47
  110.0 17.9 %collective-permute-start.17 = (bf16[64,1024]{1,0:T(8,128)(2,1)}, bf16[64,1024]{1,0:T(8,128)(2,1)S(1)}, u32[]{:S(2)}, u32[]{:S(2)}) collective-permute-start(bf16[64,1024]{1,0:T(8,128)(2,1)} %get-tuple-element.37), channel_id=1, source_target_pairs={{0,16},{8,24},{16,32},{24,40},{32,48},{40,56},{48,0},{56,8},{1,17}... | collective-permute-start | bytes 393224 | tf_op jit(solution)/shard_map/ppermute | solution.py:47
  112.1 17.7 %collective-permute-start.21 = (bf16[64,1024]{1,0:T(8,128)(2,1)S(1)}, bf16[64,1024]{1,0:T(8,128)(2,1)S(1)}, u32[]{:S(2)}, u32[]{:S(2)}) collective-permute-start(bf16[64,1024]{1,0:T(8,128)(2,1)S(1)} %get-tuple-element.41), channel_id=1, source_target_pairs={{0,48},{8,56},{16,0},{24,8},{32,16},{40,24},{48,32},{56,40},{1,49}... | collective-permute-start | bytes 393224 | tf_op jit(solution)/shard_map/ppermute | solution.py:47
  122.6 8.9 %collective-permute-start.22 = (bf16[64,1024]{1,0:T(8,128)(2,1)S(1)}, bf16[64,1024]{1,0:T(8,128)(2,1)S(1)}, u32[]{:S(2)}, u32[]{:S(2)}) collective-permute-start(bf16[64,1024]{1,0:T(8,128)(2,1)S(1)} %get-tuple-element.42), channel_id=1, source_target_pairs={{0,56},{8,0},{16,8},{24,16},{32,24},{40,32},{48,40},{56,48},{1,57}... | collective-permute-start | bytes 393224 | tf_op jit(solution)/shard_map/ppermute | solution.py:47
  124.4 8.7 %collective-permute-start.23 = (f32[256,128]{1,0:T(8,128)S(1)}, f32[256,128]{1,0:T(8,128)S(1)}, u32[]{:S(2)}, u32[]{:S(2)}) collective-permute-start(f32[256,128]{1,0:T(8,128)S(1)} %get-tuple-element.45), channel_id=1, source_target_pairs={{0,128},{128,0},{1,129},{129,1},{2,130},{130,2},{3,131},{131,3},{4... | collective-permute-start | bytes 393224 | tf_op jit(solution)/shard_map/ppermute | solution.py:47
